TPU v7x, 128 devices: a whole 4x4x4 slice. The times are simulated.
128 devices in a mesh: fsdp: 16 (over x_lo, z, core), tp: 8 (over x_hi, y).
Axes of the slice: x: 4 (x_hi: 2, x_lo: 2; x = x_hi * 2 + x_lo), y: 4, z: 4, core: 2. Of those that a mesh axis runs over, the one named last changes fastest.
Arguments:
- weight_master: float32 [4096, 18560], P(('fsdp', 'tp')), may hold values from -0.09375 to 0.09375
- weight_grad: bfloat16 [4096, 18560], P(('fsdp', 'tp')), may hold values from -6 to 6
- weight_first: float32 [4096, 18560], P(('fsdp', 'tp')), may hold values from -2 to 2
- weight_second: float32 [4096, 18560], P(('fsdp', 'tp')), may hold values from 0.05 to 0.5
- conv_master: float32 [5, 10240], P(None, ('fsdp', 'tp')), may hold values from -3 to 3
- conv_grad: bfloat16 [5, 10240], P(None, ('fsdp', 'tp')), may hold values from -6 to 6
- conv_first: float32 [5, 10240], P(None, ('fsdp', 'tp')), may hold values from -2 to 2
- conv_second: float32 [5, 10240], P(None, ('fsdp', 'tp')), may hold values from 0.05 to 0.5
- learn_rate: float32 [1], replicated, may hold values from 0.005 to 0.02
- segment_offsets: int32 [5], replicated, may hold values from 0 to 18432, as said below
- head_order: int32 [128], replicated, may hold values from 0 to 127, each once
- group_order: int32 [8], replicated, may hold values from 0 to 7, each once
- hidden_input: bfloat16 [3, 768, 4096], P(None, 'fsdp'), may hold values from -6 to 6
- scan_state: bfloat16 [768, 128, 64, 128], P('fsdp', 'tp'), may hold values from -6 to 6
- conv_heads: bfloat16 [768, 3, 8192], P('fsdp', None, 'tp'), may hold values from -6 to 6
- conv_groups: bfloat16 [768, 3, 2, 8, 128], P('fsdp', None, None, 'tp'), may hold values from -6 to 6
- decay_log: float32 [128], replicated, may hold values from 0 to 2.5
- delta_bias: float32 [128], replicated, may hold values from -3 to 0
- skip_gain: float32 [128], replicated, may hold values from 0.5 to 1.5
- norm_gain: float32 [8192], replicated, may hold values from 0.5 to 1.5
Outputs:
- mixer_out: bfloat16 [3, 768, 8192], P(None, 'fsdp', 'tp')
Inputs may be any that keep to these rules, and one draw needn't show every extreme that they name: `segment_offsets`: the five segments z, x, B, C, dt have lengths 8192, 8192, 1024, 1024, 128 and together cover columns 0 to 18559 without gaps; dt is the last segment, the order of the other four varies. `head_order`: each head once; owner i of tp holds head slots i * 128 / 8 onward. `group_order`: each group once; owner i of tp holds group slots i * 8 / 8 onward.
All inputs are finite; a program needn't handle non-finite values.
Results may differ from a plain program's by a relative error of at most 0.002.
The roundings to bfloat16 on the way count: a program that leaves them out, or rounds other values in their place, can miss the bound.
Values may be sent and summed in bfloat16 or wider, within the bound.
No kernel may reach another device: no remote copies, remote signals or barrier semaphores. Data moves between devices by JAX's collectives and lax.ppermute only.
A program may use at most 256 MiB of HBM per device.

v0:
```python
import jax
import jax.numpy as jnp
from jax import lax
from jax.sharding import PartitionSpec as P

TAPS = 4
ADAM_STEP = 100


beta_one = 0.9
beta_two = 0.95
adam_eps = 1e-08
weight_decay = 0.1
norm_eps = 1e-05


def adamw(master, gradient, first, second, rate):
    slope = gradient.astype(jnp.float32)
    moment_one = beta_one * first + (1.0 - beta_one) * slope
    moment_two = beta_two * second + (1.0 - beta_two) * slope * slope
    fixed_one = moment_one / (1.0 - beta_one**ADAM_STEP)
    fixed_two = moment_two / (1.0 - beta_two**ADAM_STEP)
    update = fixed_one / (jnp.sqrt(fixed_two) + adam_eps) + weight_decay * master
    return (master - rate * update).astype(jnp.bfloat16)


def conv_silu(values, stored, taps):
    window = jnp.concatenate(
        [stored.astype(jnp.float32), jnp.swapaxes(values, 0, 1).astype(jnp.float32)], axis=1
    )
    weights = taps.astype(jnp.float32)
    outputs = []
    for moment in range(values.shape[0]):
        total = weights[TAPS]
        for lag in range(TAPS):
            total = total + weights[lag] * window[:, moment + lag]
        outputs.append(jax.nn.silu(total))
    return jnp.stack(outputs).astype(jnp.bfloat16)


def per_device(
    weight_master,
    weight_grad,
    weight_first,
    weight_second,
    conv_master,
    conv_grad,
    conv_first,
    conv_second,
    learn_rate,
    segment_offsets,
    head_order,
    group_order,
    hidden_input,
    scan_state,
    conv_heads,
    conv_groups,
    decay_log,
    delta_bias,
    skip_gain,
    norm_gain,
):
    owners = lax.axis_size("tp")
    owner = lax.axis_index("tp")
    heads = head_order.shape[0]
    groups = group_order.shape[0]
    head_dim = scan_state.shape[2]
    state_dim = scan_state.shape[3]
    own_heads = heads // owners
    own_groups = groups // owners
    inner = heads * head_dim
    width_groups = groups * state_dim
    steps, requests, model_width = hidden_input.shape
    rate = learn_rate[0]
    new_weight = adamw(weight_master, weight_grad, weight_first, weight_second, rate)
    new_conv = adamw(conv_master, conv_grad, conv_first, conv_second, rate)
    conv_all = lax.all_gather(new_conv, ("fsdp", "tp"), axis=1, tiled=True)
    lanes = jnp.arange(head_dim, dtype=jnp.int32)
    state_lanes = jnp.arange(state_dim, dtype=jnp.int32)
    head_table = head_order.reshape(owners, own_heads)
    head_cols = (head_table[:, :, None] * head_dim + lanes).reshape(owners, own_heads * head_dim)
    group_table = group_order.reshape(owners, own_groups)
    group_cols = (group_table[:, :, None] * state_dim + state_lanes).reshape(
        owners, own_groups * state_dim
    )
    table = jnp.concatenate(
        [
            segment_offsets[0] + head_cols,
            segment_offsets[1] + head_cols,
            segment_offsets[2] + group_cols,
            segment_offsets[3] + group_cols,
            segment_offsets[4] + head_table,
        ],
        axis=1,
    )
    picked = jnp.take(new_weight, table, axis=1)
    arrived = lax.all_to_all(picked, "tp", split_axis=1, concat_axis=0, tiled=True)
    block = arrived.reshape(arrived.shape[0], arrived.shape[2])
    columns = block.shape[1]
    flat = hidden_input.reshape(steps * requests, model_width)
    summed = jnp.dot(
        flat, lax.all_gather(block, "fsdp", axis=0, tiled=True), preferred_element_type=jnp.float32
    )
    projected = summed.astype(jnp.bfloat16).reshape(steps, requests, columns)
    span = own_heads * head_dim
    gate_in = projected[:, :, :span]
    x_in = projected[:, :, span : 2 * span]
    my_heads = lax.dynamic_slice_in_dim(head_order, owner * own_heads, own_heads)
    my_cols = (my_heads[:, None] * head_dim + lanes).reshape(-1)
    x_conv = conv_silu(x_in, conv_heads, jnp.take(conv_all, my_cols, axis=1))
    groups_width = 2 * own_groups * state_dim
    groups_in = projected[:, :, 2 * span : 2 * span + groups_width]
    delta_raw = projected[:, :, 2 * span + groups_width :]
    my_groups = lax.dynamic_slice_in_dim(group_order, owner * own_groups, own_groups)
    my_group_cols = (my_groups[:, None] * state_dim + state_lanes).reshape(-1)
    group_taps = jnp.take(
        conv_all,
        jnp.concatenate([inner + my_group_cols, inner + width_groups + my_group_cols]),
        axis=1,
    )
    local_conv = conv_silu(
        groups_in, conv_groups.reshape(requests, TAPS - 1, groups_width), group_taps
    )
    local_conv = local_conv.reshape(steps, requests, 2, own_groups, state_dim)
    group_conv = lax.all_gather(local_conv, "tp", axis=3, tiled=True)
    group_conv = group_conv.astype(jnp.float32)
    per_group = heads // groups
    head_group = my_heads // per_group
    pick = (group_order[None, :] == head_group[:, None]).astype(jnp.float32)
    b_heads = jnp.einsum(
        "srqn,hq->srhn", group_conv[:, :, 0], pick, precision=lax.Precision.HIGHEST
    )
    c_heads = jnp.einsum(
        "srqn,hq->srhn", group_conv[:, :, 1], pick, precision=lax.Precision.HIGHEST
    )
    x_heads = x_conv.astype(jnp.float32).reshape(steps, requests, own_heads, head_dim)
    decay_rate = -jnp.exp(decay_log[my_heads])
    bias = delta_bias[my_heads]
    skip = skip_gain[my_heads]
    state = scan_state.astype(jnp.float32)
    outputs = []
    for moment in range(steps):
        delta = jax.nn.softplus(delta_raw[moment].astype(jnp.float32) + bias)
        keep = jnp.exp(delta * decay_rate)
        values = x_heads[moment]
        state = (
            state * keep[:, :, None, None]
            + (delta[:, :, None] * values)[:, :, :, None] * b_heads[moment][:, :, None, :]
        )
        read = jnp.einsum("rhpn,rhn->rhp", state, c_heads[moment], precision=lax.Precision.HIGHEST)
        outputs.append(read + skip[None, :, None] * values)
    scanned = jnp.stack(outputs)
    gated = scanned * jax.nn.silu(
        gate_in.astype(jnp.float32).reshape(steps, requests, own_heads, head_dim)
    )
    member = (head_group[:, None] == jnp.arange(groups, dtype=jnp.int32)[None, :]).astype(
        jnp.float32
    )
    partial_squares = jnp.einsum(
        "srh,hg->srg", jnp.sum(gated * gated, axis=3), member, precision=lax.Precision.HIGHEST
    )
    squares = lax.psum(partial_squares, "tp")
    scale = lax.rsqrt(squares / (per_group * head_dim) + norm_eps)
    scale_heads = jnp.einsum("srg,hg->srh", scale, member, precision=lax.Precision.HIGHEST)
    gain_slots = jnp.take(norm_gain, my_cols).reshape(own_heads, head_dim)
    mixer_out = gated * scale_heads[:, :, :, None] * gain_slots[None, None]
    return mixer_out.astype(jnp.bfloat16).reshape(steps, requests, span)


def solution(mesh):
    return jax.shard_map(
        per_device,
        mesh=mesh,
        in_specs=(
            P(("fsdp", "tp"), None),
            P(("fsdp", "tp"), None),
            P(("fsdp", "tp"), None),
            P(("fsdp", "tp"), None),
            P(None, ("fsdp", "tp")),
            P(None, ("fsdp", "tp")),
            P(None, ("fsdp", "tp")),
            P(None, ("fsdp", "tp")),
            P(),
            P(),
            P(),
            P(),
            P(None, "fsdp", None),
            P("fsdp", "tp", None, None),
            P("fsdp", None, "tp"),
            P("fsdp", None, None, "tp", None),
            P(),
            P(),
            P(),
            P(),
        ),
        out_specs=P(None, "fsdp", "tp"),
        check_vma=False,
    )
```

profile of v0, /device:TPU:0, one launch (start us, length us, event | category | flops | bytes accessed | tf_op | source)
XLA Modules:
  0.0 701.7 jit_solution(7727351056849122417)
XLA Ops:
  6.5 1.5 fusion.113
  8.0 1.3 broadcast_add_fusion
  12.4 0.8 constant_dynamic-update-slice_fusion.5
  13.1 0.7 constant_dynamic-update-slice_fusion.4
  14.6 5.3 fusion.34
  19.9 3.5 copy.107
  23.4 37.9 %gather_fusion = bf16[18560,32]{1,0:T(8,128)(2,1)} fusion(bf16[32,18560]{0,1:T(8,128)(2,1)} %copy.107, s32[19456]{0:T(1024)S(1)} %pad_clamp_fusion), kind=kCustom, calls=%fused_computation | custom fusion | bytes 2449920 | tf_op jit(solution)/shard_map/jit(_take)/gather | solution.py:96
  61.3 3.9 copy.108
  65.8 0.8 constant_dynamic-update-slice_fusion.2
  66.5 0.7 constant_dynamic-update-slice_fusion.1
  67.5 26.4 %all_to_all.15 = bf16[32,8,2320]{2,0,1:T(8,128)(2,1)} all-to-all(bf16[32,8,2320]{2,0,1:T(8,128)(2,1)S(1)} %select_bitcast_fusion), channel_id=1, replica_groups=mesh['fsdp'=16,'tp'=8] {'tp'}, dimensions={1} | all-to-all | bytes 2375680 | tf_op jit(solution)/shard_map/all_to_all | solution.py:97
  94.4 314.5 %all-gather = bf16[128,80,5]{1,2,0:T(8,128)(2,1)S(1)} all-gather(bf16[1,80,5]{1,2,0:T(8,128)(2,1)S(1)} %fusion.101), channel_id=1, replica_groups=mesh['fsdp'=16,'tp'=8] {'fsdp','tp'}, dimensions={0}, use_global_device_ids=true | all-gather | bytes 103200 | tf_op jit(solution)/shard_map/all_gather | solution.py:77
  408.9 2.2 copy.109
  413.1 4.9 gather_fusion.3
  418.8 2.8 gather_fusion.4
  422.8 6.1 gather_fusion.6
  429.7 1.3 slice_reduce_fusion.4
  431.1 8.5 %convolution_convert_fusion = bf16[2320,144]{0,1:T(8,128)(2,1)S(1)} fusion(bf16[144,4096]{1,0:T(8,128)(2,1)S(1)} %bitcast.212, bf16[4096,2320]{1,0:T(8,128)(2,1)} %all-gather.3.cloned.1.call-done), kind=kOutput, calls=%fused_computation.33 | convolution fusion | flops 2737117440 | bytes 20853248 | tf_op jit(solution)/shard_map/dot_general | solution.py:101
  439.6 1.0 slice_convert_fusion
  441.8 35.3 %all_gather.11 = bf16[3,48,2,8,128]{4,1,2,0,3:T(8,128)(2,1)S(1)} all-gather(bf16[3,48,2,1,128]{4,1,2,0,3:T(8,128)(2,1)S(1)} %maximum_bitcast_fusion), channel_id=1, replica_groups=mesh['fsdp'=16,'tp'=8] {'tp'}, dimensions={3}, use_global_device_ids=true | all-gather | bytes 663552 | tf_op jit(solution)/shard_map/all_gather | solution.py:125
  477.6 1.0 slice_bitcast_fusion.2
  479.0 1.1 fusion.108
  480.1 1.4 reshape.1909
  482.4 44.5 %fusion.4 = f32[48,16,1,64]{3,2,1,0:T(1,128)S(1)} fusion(f32[48,16,128,1]{2,3,1,0:T(1,128)S(1)} %bitcast.226, bf16[48,16,64,128]{3,2,1,0:T(8,128)(2,1)} %param.33, f32[48,16,128]{2,1,0:T(8,128)S(1)} %get-tuple-element.21, f32[48,16,64]{2,1,0:T(8,128)S(1)} %broadcast_multiply_fusion.2, f32[48,16]{1,0:T(8,128)S(1)} %get-tuple-element.24), kind=kOutput, calls=%fused_computation.13 | convolution fusion | flops 100663296 | bytes 13765632 | tf_op jit(solution)/shard_map/rhpn,rhn->rhp/dot_general | solution.py:150
  527.1 56.8 %fusion.5 = f32[48,16,1,64]{3,2,1,0:T(1,128)S(1)} fusion(f32[48,16,128,1]{2,3,1,0:T(1,128)S(1)} %bitcast.225, bf16[48,16,64,128]{3,2,1,0:T(8,128)(2,1)S(1)} %bitcast.242, f32[48,16,128]{2,1,0:T(8,128)S(1)} %copy-done.13, f32[48,16,64]{2,1,0:T(8,128)S(1)} %get-tuple-element.66, f32[48,16]{1,0:T(8,128)S(1)} %get-tuple-element.25, ...), kind=kOutput, calls=%fused_computation.14 | convolution fusion | flops 119537664 | bytes 14358528 | tf_op jit(solution)/shard_map/rhpn,rhn->rhp/dot_general | solution.py:150
  583.9 67.0 %fusion = f32[48,16,1,64]{3,2,1,0:T(1,128)S(1)} fusion(f32[48,16,128,1]{2,3,1,0:T(1,128)S(1)} %bitcast.224, bf16[48,16,64,128]{3,2,1,0:T(8,128)(2,1)S(1)} %bitcast.242, f32[48,16,128]{2,1,0:T(8,128)S(1)} %copy-done.12, f32[48,16,64]{2,1,0:T(8,128)S(1)} %get-tuple-element.65, f32[48,16]{1,0:T(8,128)S(1)} %get-tuple-element.26, ...), kind=kOutput, calls=%fused_computation.7 | convolution fusion | flops 138412032 | bytes 14951424 | tf_op jit(solution)/shard_map/rhpn,rhn->rhp/dot_general | solution.py:150
  651.1 0.8 stack.44
  652.0 0.8 stack.45
  652.8 0.8 stack.46
  654.3 36.7 %psum.7 = f32[3,48,8]{1,2,0:T(8,128)S(1)} all-reduce(f32[3,48,8]{1,2,0:T(8,128)S(1)} %fusion.88), channel_id=1, replica_groups=mesh['fsdp'=16,'tp'=8] {'tp'}, use_global_device_ids=true, to_apply=%region_1.2 | all-reduce | flops 1152 | bytes 9216 | tf_op jit(solution)/shard_map/psum | solution.py:162
  691.6 1.2 mul.897
  692.8 2.0 fusion.39
  (140 shorter events, 12.8 us)
Async XLA Ops:
  6.5 424.6 %copy-start = (bf16[3,48,4096]{2,1,0:T(8,128)(2,1)S(1)}, bf16[3,48,4096]{2,1,0:T(8,128)(2,1)}, u32[]{:S(2)}) copy-start(bf16[3,48,4096]{2,1,0:T(8,128)(2,1)} %param.32) | copy-start | bytes 3538948
  6.5 424.5 %all-gather.3.cloned.1.call-start = ((), (), s32[]{:S(2)}) async-start(), calls=%async_computation.1 | async-start | bytes 21168128 | tf_op jit(solution)/shard_map/all_gather | solution.py:102
  67.5 26.5 %copy-start.24 = (s32[128]{0:T(128)S(1)}, s32[128]{0:T(128)}, u32[]{:S(2)}) copy-start(s32[128]{0:T(128)} %param.30) | copy-start | bytes 1540
  67.5 26.8 %copy-start.19 = (f32[5,80]{1,0:T(8,128)S(1)}, f32[5,80]{1,0:T(8,128)}, u32[]{:S(2)}) copy-start(f32[5,80]{1,0:T(8,128)} %param.24) | copy-start | bytes 4804
  67.5 26.8 %copy-start.20 = (f32[5,80]{1,0:T(8,128)S(1)}, f32[5,80]{1,0:T(8,128)}, u32[]{:S(2)}) copy-start(f32[5,80]{1,0:T(8,128)} %param.27) | copy-start | bytes 4804
  67.5 26.8 %copy-start.21 = (f32[5,80]{1,0:T(8,128)S(1)}, f32[5,80]{1,0:T(8,128)}, u32[]{:S(2)}) copy-start(f32[5,80]{1,0:T(8,128)} %param.26) | copy-start | bytes 4804
  67.5 26.8 %copy-start.23 = (bf16[5,80]{1,0:T(8,128)(2,1)S(1)}, bf16[5,80]{1,0:T(8,128)(2,1)}, u32[]{:S(2)}) copy-start(bf16[5,80]{1,0:T(8,128)(2,1)} %param.25) | copy-start | bytes 2404
  93.9 317.2 %copy-start.17 = (bf16[48,3,1024]{2,0,1:T(8,128)(2,1)S(1)}, bf16[48,3,1024]{2,0,1:T(8,128)(2,1)}, u32[]{:S(2)}) copy-start(bf16[48,3,1024]{2,0,1:T(8,128)(2,1)} %param.34) | copy-start | bytes 884740
  93.9 317.3 %copy-start.3 = (f32[128]{0:T(128)S(1)}, f32[128]{0:T(128)}, u32[]{:S(2)}) copy-start(f32[128]{0:T(128)} %param.36) | copy-start | bytes 1540
  93.9 318.0 %copy-start.4 = (f32[128]{0:T(128)S(1)}, f32[128]{0:T(128)}, u32[]{:S(2)}) copy-start(f32[128]{0:T(128)} %param.37) | copy-start | bytes 1540
  408.9 3.7 copy-start.22
  408.9 12.7 %copy-start.18 = (bf16[48,3,2,1,128]{4,2,3,1,0:T(2,128)(2,1)S(1)}, bf16[48,3,2,1,128]{4,2,3,1,0:T(2,128)(2,1)}, u32[]{:S(2)}) copy-start(bf16[48,3,2,1,128]{4,2,3,1,0:T(2,128)(2,1)} %param.35) | copy-start | bytes 221188
  408.9 13.0 %copy-start.5 = (f32[128]{0:T(128)S(1)}, f32[128]{0:T(128)}, u32[]{:S(2)}) copy-start(f32[128]{0:T(128)} %param.38) | copy-start | bytes 1540
  411.1 11.7 %copy-start.2 = (f32[8192]{0:T(1024)S(1)}, f32[8192]{0:T(1024)}, u32[]{:S(2)}) copy-start(f32[8192]{0:T(1024)} %param.39) | copy-start | bytes 98308
  441.1 40.6 %copy-start.6 = (f32[48,16,64]{2,1,0:T(8,128)}, f32[48,16,64]{2,1,0:T(8,128)S(1)}, u32[]{:S(2)}) copy-start(f32[48,16,64]{2,1,0:T(8,128)S(1)} %squeeze.115) | copy-start | bytes 589828
  441.2 40.5 %copy-start.8 = (f32[48,16,64]{2,1,0:T(8,128)}, f32[48,16,64]{2,1,0:T(8,128)S(1)}, u32[]{:S(2)}) copy-start(f32[48,16,64]{2,1,0:T(8,128)S(1)} %squeeze.117) | copy-start | bytes 589828
  481.4 1.0 copy-start.16
  481.7 45.3 %slice-start = ((s8[12582912]{0:T(1024)(128)(4,1)}), s8[4194304]{0:T(1024)(128)(4,1)S(1)}, s32[]{:S(2)}) async-start(s8[12582912]{0:T(1024)(128)(4,1)} %bitcast.241), calls=%async_computation.2 | async-start | bytes 8388608
  482.4 44.6 %copy-start.13 = (f32[48,16,128]{2,1,0:T(8,128)S(1)}, f32[48,16,128]{2,1,0:T(8,128)}, u32[]{:S(2)}) copy-start(f32[48,16,128]{2,1,0:T(8,128)} %get-tuple-element.23) | copy-start | bytes 1179652
  482.4 44.6 %copy-start.15 = (f32[1,48,16,128]{3,2,1,0:T(8,128)S(1)}, f32[1,48,16,128]{3,2,1,0:T(8,128)}, u32[]{:S(2)}) copy-start(f32[1,48,16,128]{3,2,1,0:T(8,128)} %get-tuple-element.20) | copy-start | bytes 1179652
  482.4 44.6 %slice-start.1 = ((s8[12582912]{0:T(1024)(128)(4,1)}), s8[4194304]{0:T(1024)(128)(4,1)S(1)}, s32[]{:S(2)}) async-start(s8[12582912]{0:T(1024)(128)(4,1)} %bitcast.241), calls=%async_computation.3 | async-start | bytes 8388608
  482.4 44.6 %slice-start.2 = ((s8[12582912]{0:T(1024)(128)(4,1)}), s8[4194304]{0:T(1024)(128)(4,1)S(1)}, s32[]{:S(2)}) async-start(s8[12582912]{0:T(1024)(128)(4,1)} %bitcast.241), calls=%async_computation.4 | async-start | bytes 8388608
  527.0 56.8 %copy-start.12 = (f32[48,16,128]{2,1,0:T(8,128)S(1)}, f32[48,16,128]{2,1,0:T(8,128)}, u32[]{:S(2)}) copy-start(f32[48,16,128]{2,1,0:T(8,128)} %get-tuple-element.22) | copy-start | bytes 1179652
  527.1 56.8 %copy-start.14 = (f32[1,48,16,128]{3,2,1,0:T(8,128)S(1)}, f32[1,48,16,128]{3,2,1,0:T(8,128)}, u32[]{:S(2)}) copy-start(f32[1,48,16,128]{3,2,1,0:T(8,128)} %get-tuple-element.19) | copy-start | bytes 1179652
  583.9 67.0 %copy-start.7 = (f32[48,16,64]{2,1,0:T(8,128)S(1)}, f32[48,16,64]{2,1,0:T(8,128)}, u32[]{:S(2)}) copy-start(f32[48,16,64]{2,1,0:T(8,128)} %copy-done.6) | copy-start | bytes 589828
  583.9 67.0 %copy-start.9 = (f32[48,16,64]{2,1,0:T(8,128)S(1)}, f32[48,16,64]{2,1,0:T(8,128)}, u32[]{:S(2)}) copy-start(f32[48,16,64]{2,1,0:T(8,128)} %copy-done.8) | copy-start | bytes 589828
  654.1 38.7 %copy-start.10 = (f32[1,48,1024]{2,1,0:T(8,128)S(1)}, f32[1,48,1024]{2,1,0:T(8,128)}, u32[]{:S(2)}) copy-start(f32[1,48,1024]{2,1,0:T(8,128)} %stack.44) | copy-start | bytes 589828
  654.1 38.7 %copy-start.11 = (f32[1,48,1024]{2,1,0:T(8,128)S(1)}, f32[1,48,1024]{2,1,0:T(8,128)}, u32[]{:S(2)}) copy-start(f32[1,48,1024]{2,1,0:T(8,128)} %stack.45) | copy-start | bytes 589828
  691.0 3.8 copy-start.1
Sparse Core Ops, SparseCore 0:
  94.0 104.8 all-gather.2
where the time goes:
time: 702 us
  blocking collectives  413 us (59%)
  matrix products  178 us (25%)
  local copies, waits for them, and re-layouts  77 us (11%)
  other arithmetic  18.3 us (3%)
  between operations  15.4 us (2%)
    all_gather x1, blocking collectives, per_device(): conv_all = lax.all_gather(new_conv, ('fsdp', 'tp'), axis=1, tiled=True)  315 us
    dot_general x3, matrix products, per_device(): jnp.einsum('rhpn,rhn->rhp', state, c_heads[moment], precision=lax.Precisi...  168 us
    gather x2, local copies, waits for them, and re-layouts, per_device(): picked = jnp.take(new_weight, table, axis=1)  41.8 us
    psum x1, blocking collectives, per_device(): squares = lax.psum(partial_squares, 'tp')  36.7 us
    all_gather x1, blocking collectives, per_device(): group_conv = lax.all_gather(local_conv, 'tp', axis=3, tiled=True)  35.3 us
    all_to_all x1, blocking collectives, per_device(): lax.all_to_all(picked, 'tp', split_axis=1, concat_axis=0, tiled=True)  26.4 us
  transfers between devices with their start and end apart: 1, of which 0 were waited for; matrix products, arithmetic and copies ran while one was open for 3% of the time, Pallas kernels for 0%

commit v1 on v0

v1 whole, which is shorter than its diff:
```python
import functools

import jax
import jax.numpy as jnp
from jax import lax
from jax.experimental import pallas as pl
from jax.experimental.pallas import tpu as pltpu
from jax.sharding import PartitionSpec as P

TAPS = 4
ADAM_STEP = 100
STEPS = 3
ROWS = 48
FLAT = STEPS * ROWS
HEADS = 128
GROUPS = 8
HEAD_DIM = 64
STATE = 128
OWN_HEADS = 16
SPAN = OWN_HEADS * HEAD_DIM
JOINED = 18560
PIECE = 3712
SHARD = 80
INNER = HEADS * HEAD_DIM
FIRST = 3 * 128 + SPAN

beta_one = 0.9
beta_two = 0.95
adam_eps = 1e-08
weight_decay = 0.1
norm_eps = 1e-05
HIGH = lax.Precision.HIGHEST


def adamw(master, gradient, first, second, rate):
    slope = gradient.astype(jnp.float32)
    moment_one = beta_one * first + (1.0 - beta_one) * slope
    moment_two = beta_two * second + (1.0 - beta_two) * slope * slope
    fixed_one = moment_one / (1.0 - beta_one**ADAM_STEP)
    fixed_two = moment_two / (1.0 - beta_two**ADAM_STEP)
    update = fixed_one / (jnp.sqrt(fixed_two) + adam_eps) + weight_decay * master
    return (master - rate * update).astype(jnp.bfloat16)


def refit_kernel(rate, offsets, heads, groups, order, master, grad, first, second, conv, front, gate, work):
    step = pl.program_id(0)
    for j in range(PIECE // 128):
        cols = slice(j * 128, (j + 1) * 128)
        new = adamw(master[:, cols], grad[:, cols], first[:, cols], second[:, cols], rate[0])
        work[:, pl.ds(pl.multiple_of(step * PIECE + j * 128, 128), 128)] = new.astype(jnp.float32)

    @pl.when(step == JOINED // PIECE - 1)
    def _():
        lane = lax.broadcasted_iota(jnp.int32, (32, 128), 1)
        dt = work[:, pl.ds(pl.multiple_of(offsets[4], 128), 128)]
        onehot = (lax.broadcasted_iota(jnp.int32, (HEADS, HEADS), 0) == order[...]).astype(jnp.bfloat16)
        dt = jnp.dot(dt.astype(jnp.bfloat16), onehot, preferred_element_type=jnp.float32)

        def block(start):
            return work[:, pl.ds(pl.multiple_of(start, 128), 128)]

        def half(start, head, low):
            wide = block(start + (head // 2) * 128)
            turn = (head % 2) != (0 if low else 1)
            return jnp.where(turn, pltpu.roll(wide, 64, 1), wide)

        for owner in range(8):
            for k in range(8):
                low = heads[owner * OWN_HEADS + 2 * k]
                high = heads[owner * OWN_HEADS + 2 * k + 1]
                for segment, out, at in ((1, front, 384), (0, gate, 0)):
                    start = offsets[segment]
                    both = jnp.where(lane < 64, half(start, low, True), half(start, high, False))
                    out[owner, :, at + k * 128 : at + (k + 1) * 128] = both.astype(jnp.bfloat16)
            group = groups[owner]
            front[owner, :, 0:128] = block(offsets[2] + group * 128).astype(jnp.bfloat16)
            front[owner, :, 128:256] = block(offsets[3] + group * 128).astype(jnp.bfloat16)
            mine = dt if owner == 0 else pltpu.roll(dt, 128 - 16 * owner, 1)
            front[owner, :, 256:384] = jnp.where(lane < 16, mine, conv[...]).astype(jnp.bfloat16)


def refit(rate, offsets, heads, groups, master, grad, first, second, conv):
    smem = pl.BlockSpec(memory_space=pltpu.SMEM)
    piece = pl.BlockSpec((32, PIECE), lambda i: (0, i))
    whole = lambda shape: pl.BlockSpec(shape, lambda i: (0,) * len(shape))
    return pl.pallas_call(
        refit_kernel,
        grid=(JOINED // PIECE,),
        in_specs=[smem, smem, smem, smem, whole((1, HEADS)), piece, piece, piece, piece, whole((32, 128))],
        out_specs=[whole((8, 32, FIRST)), whole((8, 32, SPAN))],
        out_shape=[
            jax.ShapeDtypeStruct((8, 32, FIRST), jnp.bfloat16),
            jax.ShapeDtypeStruct((8, 32, SPAN), jnp.bfloat16),
        ],
        scratch_shapes=[pltpu.VMEM((32, JOINED), jnp.float32)],
        compiler_params=pltpu.CompilerParams(vmem_limit_bytes=40 * 2**20),
        name="refit",
    )(rate, offsets, heads, groups, heads.reshape(1, HEADS), master, grad, first, second, conv)


def silu(value):
    return value * jax.nn.sigmoid(value)


def convolve(inputs, stored, taps):
    window = [stored[j].astype(jnp.float32) for j in range(TAPS - 1)] + inputs
    outputs = []
    for moment in range(STEPS):
        total = taps[TAPS : TAPS + 1]
        for lag in range(TAPS):
            total = total + taps[lag : lag + 1] * window[moment + lag]
        outputs.append(silu(total).astype(jnp.bfloat16))
    return outputs


def rounded(ours, theirs, moment, cols=slice(None)):
    rows = slice(moment * ROWS, (moment + 1) * ROWS)
    return (ours[rows, cols] + theirs[rows, cols]).astype(jnp.bfloat16).astype(jnp.float32)


def groups_kernel(ours, theirs, stored, taps, out, dt):
    inputs = [rounded(ours, theirs, t, slice(0, 256)) for t in range(STEPS)]
    for t, value in enumerate(convolve(inputs, stored, taps[...])):
        out[t] = value
        dt[t] = rounded(ours, theirs, t, slice(256, 384)).astype(jnp.bfloat16)


def state_kernel(state, b_all, c_all, mask, out, pair):
    chosen = mask[...]
    for r in range(8):
        c = c_all[r]
        b = b_all[r]
        read = lax.dot_general(
            c.astype(jnp.bfloat16),
            state[r].reshape(SPAN, STATE),
            (((1,), (1,)), ((), ())),
            preferred_element_type=jnp.float32,
        )
        n = 0
        for t in range(STEPS):
            rows = slice(8 * t, 8 * t + 8)
            out[t, r : r + 1, :] = jnp.sum(read[rows] * chosen, axis=0, keepdims=True)
            for s in range(t + 1):
                both = jnp.sum(c[rows] * b[8 * s : 8 * s + 8], axis=1, keepdims=True)
                pair[n, r : r + 1, :] = jnp.sum(both * chosen, axis=0, keepdims=True)
                n += 1


def scan_kernel(ours, theirs, stored, taps, read, pair, dt, spread, params, out):
    inputs = [rounded(ours, theirs, t) for t in range(STEPS)]
    values = [v.astype(jnp.float32) for v in convolve(inputs, stored, taps[...])]
    rate = -jnp.exp(params[0:1])
    bias = params[1:2]
    skip = params[2:3]
    keeps, driven = [], []
    for t in range(STEPS):
        raw = jnp.dot(dt[t], spread[...], preferred_element_type=jnp.float32)
        delta = jax.nn.softplus(raw + bias)
        keeps.append(jnp.exp(delta * rate))
        driven.append(delta * values[t])
    n = 0
    for t in range(STEPS):
        total = skip * values[t]
        offset = n + t
        after = None
        for s in range(t, -1, -1):
            term = pair[offset] * driven[s]
            total = total + (term if after is None else after * term)
            after = keeps[s] if after is None else after * keeps[s]
            offset -= 1
        out[t] = total + after * read[t]
        n += t + 1


def gate_kernel(ours, theirs, scanned, member, gated, squares):
    for t in range(STEPS):
        value = scanned[t] * silu(rounded(ours, theirs, t))
        gated[t] = value
        squares[t] = lax.dot_general(
            member[...], value * value, (((1,), (1,)), ((), ())), precision=HIGH, preferred_element_type=jnp.float32
        )


def norm_kernel(gated, squares, member, gain, out):
    for t in range(STEPS):
        scale = lax.rsqrt(squares[t] / SPAN + norm_eps)
        lanes = lax.dot_general(
            scale, member[...], (((0,), (0,)), ((), ())), precision=HIGH, preferred_element_type=jnp.float32
        )
        out[t] = (gated[t] * lanes * gain[...]).astype(jnp.bfloat16)


def call(kernel, shapes, *args):
    vmem = pl.BlockSpec(memory_space=pltpu.VMEM)
    return pl.pallas_call(
        kernel,
        in_specs=[vmem] * len(args),
        out_specs=[vmem] * len(shapes),
        out_shape=[jax.ShapeDtypeStruct(s, d) for s, d in shapes],
        compiler_params=pltpu.CompilerParams(vmem_limit_bytes=40 * 2**20),
        name=kernel.__name__,
    )(*args)


def read_state(state, b_all, c_all, mask):
    return pl.pallas_call(
        state_kernel,
        grid=(ROWS // 8,),
        in_specs=[
            pl.BlockSpec((8, OWN_HEADS, HEAD_DIM, STATE), lambda i: (i, 0, 0, 0)),
            pl.BlockSpec((8, 24, STATE), lambda i: (i, 0, 0)),
            pl.BlockSpec((8, 24, STATE), lambda i: (i, 0, 0)),
            pl.BlockSpec((8, SPAN), lambda i: (0, 0)),
        ],
        out_specs=[
            pl.BlockSpec((3, 8, SPAN), lambda i: (0, i, 0)),
            pl.BlockSpec((6, 8, SPAN), lambda i: (0, i, 0)),
        ],
        out_shape=[
            jax.ShapeDtypeStruct((3, ROWS, SPAN), jnp.float32),
            jax.ShapeDtypeStruct((6, ROWS, SPAN), jnp.float32),
        ],
        compiler_params=pltpu.CompilerParams(vmem_limit_bytes=40 * 2**20),
        name="read_state",
    )(state, b_all, c_all, mask)


def per_device(
    weight_master,
    weight_grad,
    weight_first,
    weight_second,
    conv_master,
    conv_grad,
    conv_first,
    conv_second,
    learn_rate,
    segment_offsets,
    head_order,
    group_order,
    hidden_input,
    scan_state,
    conv_heads,
    conv_groups,
    decay_log,
    delta_bias,
    skip_gain,
    norm_gain,
):
    owner = lax.axis_index("tp")
    side = lax.axis_index("fsdp") // 8
    across = [(i, (i + 8) % 16) for i in range(16)]
    planes = [[8 * s + i for i in range(8)] for s in range(2)]
    swap = lambda value: lax.ppermute(value, "fsdp", across)

    flat = hidden_input.reshape(FLAT, -1)
    depth = flat.shape[1] // 2
    near = lax.dynamic_slice_in_dim(flat, side * depth, depth, 1)
    far = swap(lax.dynamic_slice_in_dim(flat, (1 - side) * depth, depth, 1))
    rows = jnp.concatenate([near, far], axis=0)

    new_conv = adamw(conv_master, conv_grad, conv_first, conv_second, learn_rate[0])
    conv_lanes = jnp.pad(new_conv.astype(jnp.float32), ((0, 27), (16, 32)))
    front, gate = refit(
        learn_rate, segment_offsets, head_order, group_order,
        weight_master, weight_grad, weight_first, weight_second, conv_lanes,
    )

    def owned(value):
        value = lax.all_to_all(value, "tp", split_axis=0, concat_axis=0, tiled=True)
        return value.reshape(256, value.shape[2])

    def gathered(value):
        return lax.all_gather(value, "fsdp", axis_index_groups=planes, axis=0, tiled=True)

    front = gathered(owned(front))
    gate = gathered(owned(gate))

    my_heads = lax.dynamic_slice_in_dim(head_order, owner * OWN_HEADS, OWN_HEADS)
    pick_heads = my_heads[:, None] == jnp.arange(HEADS, dtype=jnp.int32)[None, :]
    lane_group = jnp.repeat(my_heads // OWN_HEADS, HEAD_DIM)
    member = (jnp.arange(GROUPS, dtype=jnp.int32)[:, None] == lane_group[None, :]).astype(jnp.float32)
    partner = owner ^ jnp.arange(GROUPS, dtype=jnp.int32)
    mask = (jnp.take(group_order, partner)[:, None] == lane_group[None, :]).astype(jnp.float32)
    spread = (jnp.arange(128, dtype=jnp.int32)[:, None] == (jnp.arange(SPAN, dtype=jnp.int32) // HEAD_DIM)[None, :])
    spread = spread.astype(jnp.bfloat16)
    params = jnp.stack([decay_log[my_heads], delta_bias[my_heads], skip_gain[my_heads]])
    params = jnp.repeat(params, HEAD_DIM, axis=1)
    gain = jnp.dot(
        pick_heads.astype(jnp.float32), norm_gain.reshape(HEADS, HEAD_DIM), precision=HIGH
    ).reshape(1, SPAN)
    stored_heads = jnp.swapaxes(conv_heads, 0, 1)
    stored_groups = jnp.swapaxes(conv_groups.reshape(ROWS, TAPS - 1, 2 * STATE), 0, 1)

    here = front.reshape(64, 32, FIRST)[:, :16, 256:384]
    there = swap(here)
    low = jnp.where(side == 0, here, there)
    high = jnp.where(side == 0, there, here)
    conv_all = jnp.concatenate([low, high], axis=0)[:, :5, 16 : 16 + SHARD]
    conv_all = jnp.swapaxes(conv_all, 0, 1).reshape(5, 128 * SHARD)
    head_taps = jnp.einsum(
        "hk,jkp->jhp",
        pick_heads.astype(jnp.bfloat16),
        conv_all[:, :INNER].reshape(5, HEADS, HEAD_DIM),
        preferred_element_type=jnp.float32,
    ).reshape(5, SPAN)
    my_group = lax.dynamic_slice_in_dim(group_order, owner, 1)
    pick_group = (my_group == jnp.arange(GROUPS, dtype=jnp.int32)).astype(jnp.bfloat16)
    group_taps = jnp.einsum(
        "g,jagn->jan",
        pick_group,
        conv_all[:, INNER:].reshape(5, 2, GROUPS, STATE),
        preferred_element_type=jnp.float32,
    ).reshape(5, 2 * STATE)

    product = lambda weights: jnp.dot(rows, weights, preferred_element_type=jnp.float32)
    first = product(front[:, :384])
    b_and_c, dt = call(
        groups_kernel,
        [((STEPS, ROWS, 2 * STATE), jnp.bfloat16), ((STEPS, ROWS, 128), jnp.bfloat16)],
        first[:FLAT], swap(first[FLAT:]), stored_groups, group_taps,
    )
    every = [b_and_c] + [
        lax.ppermute(b_and_c, "tp", [(i, i ^ k) for i in range(8)]) for k in range(1, 8)
    ]
    every = jnp.stack(every, axis=1).astype(jnp.float32)
    every = every.transpose(2, 0, 1, 3).reshape(ROWS, STEPS * GROUPS, 2 * STATE)
    read, pair = read_state(scan_state, every[:, :, :STATE], every[:, :, STATE:], mask)

    second = product(front[:, 384:])
    (scanned,) = call(
        scan_kernel,
        [((STEPS, ROWS, SPAN), jnp.float32)],
        second[:FLAT], swap(second[FLAT:]), stored_heads, head_taps, read, pair, dt, spread, params,
    )
    third = product(gate)
    gated, squares = call(
        gate_kernel,
        [((STEPS, ROWS, SPAN), jnp.float32), ((STEPS, GROUPS, ROWS), jnp.float32)],
        third[:FLAT], swap(third[FLAT:]), scanned, member,
    )
    for k in (1, 2, 4):
        squares = squares + lax.ppermute(squares, "tp", [(i, i ^ k) for i in range(8)])
    (mixer_out,) = call(
        norm_kernel, [((STEPS, ROWS, SPAN), jnp.bfloat16)], gated, squares, member, gain
    )
    return mixer_out


def solution(mesh):
    return jax.shard_map(
        per_device,
        mesh=mesh,
        in_specs=(
            P(("fsdp", "tp"), None),
            P(("fsdp", "tp"), None),
            P(("fsdp", "tp"), None),
            P(("fsdp", "tp"), None),
            P(None, ("fsdp", "tp")),
            P(None, ("fsdp", "tp")),
            P(None, ("fsdp", "tp")),
            P(None, ("fsdp", "tp")),
            P(),
            P(),
            P(),
            P(),
            P(None, "fsdp", None),
            P("fsdp", "tp", None, None),
            P("fsdp", None, "tp"),
            P("fsdp", None, None, "tp", None),
            P(),
            P(),
            P(),
            P(),
        ),
        out_specs=P(None, "fsdp", "tp"),
        check_vma=False,
    )
```

time: 702 us -> 199 us (0.28)
  blocking collectives: 413 us -> 33.8 us
  matrix products: 178 us -> 10.3 us
  waiting for transfers between devices: 0.04 us -> 70.2 us
  local copies, waits for them, and re-layouts: 77 us -> 22.1 us
  starting transfers between devices: 0.01 us -> 27.9 us
  Pallas kernels: 0 us -> 17.8 us
  other arithmetic: 18.3 us -> 1.39 us
    all_gather x2 -> x0, blocking collectives: 350 us -> none  [the longest x1 315 us: per_device(): conv_all = lax.all_gather(new_conv, ('fsdp', 'tp'), axis=1, tiled=True)]
    dot_general x8 -> x6, matrix products: 178 us -> 10.3 us  [the longest x3 8.56 us: per_device(): jnp.dot(rows, weights, preferred_element_type=jnp.float32)]
    gather x8 -> x4, local copies, waits for them, and re-layouts: 57.7 us -> 2.63 us  [the longest x1 0.66 us: per_device(): decay_log[my_heads]]
    all_gather x1 -> x2, waiting for transfers between devices: 0.02 us -> 37.7 us  [gathered(): lax.all_gather(value, 'fsdp', axis_index_groups=planes, axis=0, tiled=True)]
    psum x1 -> x0, blocking collectives: 36.7 us -> none  [per_device(): squares = lax.psum(partial_squares, 'tp')]
    ppermute x0 -> x15, waiting for transfers between devices: none -> 32.5 us  [the longest x7 16.4 us: per_device(): lax.ppermute(b_and_c, 'tp', [(i, i ^ k) for i in range(8)])]
    ppermute x0 -> x15, starting transfers between devices: none -> 27.9 us  [the longest x7 17 us: per_device(): lax.ppermute(b_and_c, 'tp', [(i, i ^ k) for i in range(8)])]
    pallas_call x0 -> x6, Pallas kernels: none -> 17.8 us  [the longest x1 10 us: read_state(): pl.pallas_call(state_kernel, grid=(ROWS // 8,), in_specs=[pl.BlockSpec((8...]
  transfers between devices with their start and end apart: 1 -> 17, of which waited for: 0 -> 12; matrix products, arithmetic and copies ran while one was open for 3% -> 12% of each run, Pallas kernels for 0% -> 6%
where the time goes in v1:
time: 199 us; the launch traced here: 198 us
  waiting for transfers between devices  70.2 us (35%)
  blocking collectives  33.8 us (17%)
  starting transfers between devices  27.9 us (14%)
  local copies, waits for them, and re-layouts  22.1 us (11%)
  Pallas kernels  17.8 us (9%)
  between operations  14.4 us (7%)
  matrix products  10.3 us (5%)
    all_gather x2, waiting for transfers between devices, gathered(): lax.all_gather(value, 'fsdp', axis_index_groups=planes, axis=0, tiled=True)  37.7 us
    all_to_all x2, blocking collectives, owned(): value = lax.all_to_all(value, 'tp', split_axis=0, concat_axis=0, tiled=True)  33.8 us
    ppermute x7, starting transfers between devices, per_device(): lax.ppermute(b_and_c, 'tp', [(i, i ^ k) for i in range(8)])  17 us
    ppermute x7, waiting for transfers between devices, per_device(): lax.ppermute(b_and_c, 'tp', [(i, i ^ k) for i in range(8)])  16.4 us
    unnamed x51, local copies, waits for them, and re-layouts  10.2 us
    pallas_call x1, Pallas kernels, read_state(): pl.pallas_call(state_kernel, grid=(ROWS // 8,), in_specs=[pl.BlockSpec((8...  10 us
    ppermute x3, waiting for transfers between devices, per_device(): lax.ppermute(squares, 'tp', [(i, i ^ k) for i in range(8)])  8.59 us
    dot_general x3, matrix products, per_device(): jnp.dot(rows, weights, preferred_element_type=jnp.float32)  8.56 us
  transfers between devices with their start and end apart: 17, of which 12 were waited for; matrix products, arithmetic and copies ran while one was open for 12% of the time, Pallas kernels for 6%

profile of v1, /device:TPU:0, one launch (start us, length us, event | category | flops | bytes accessed | tf_op | source)
XLA Modules:
  0.0 197.9 jit_solution(10650839867151788152)
XLA Ops:
  8.7 1.7 copy-done.3
  10.4 1.7 copy-done.4
  12.0 1.7 copy-done.5
  16.3 4.6 %refit.1 = (bf16[8,32,1408]{2,1,0:T(8,128)(2,1)S(1)}, bf16[8,32,1024]{2,1,0:T(8,128)(2,1)S(1)}) custom-call(f32[1]{0:T(128)} %copy.48.rate, s32[5]{0:T(128)S(1)} %copy-done.10, s32[128]{0:T(128)S(1)} %copy-done.8, s32[8]{0:T(128)S(1)} %copy-done.1, s32[1,128]{1,0:T(1,128)S(1)} %bitcast.68, f32[32,18560]{1,0:T(8,128)S(1)} %copy-done.3, ...), custom_call_target="tpu_custom_call" | custom-call | tf_op jit(solution)/shard_map/refit/pallas_call | solution.py:86
  20.9 18.4 %all_to_all.10 = bf16[8,32,1024]{2,1,0:T(8,128)(2,1)} all-to-all(bf16[8,32,1024]{2,1,0:T(8,128)(2,1)S(1)} %get-tuple-element.13), channel_id=1, replica_groups=mesh['fsdp'=16,'tp'=8] {'tp'}, dimensions={0} | all-to-all | bytes 1048576 | tf_op jit(solution)/shard_map/all_to_all | solution.py:270
  39.4 15.4 %all_to_all.11 = bf16[8,32,1408]{2,1,0:T(8,128)(2,1)} all-to-all(bf16[8,32,1408]{2,1,0:T(8,128)(2,1)S(1)} %get-tuple-element.14), channel_id=1, replica_groups=mesh['fsdp'=16,'tp'=8] {'tp'}, dimensions={0} | all-to-all | bytes 1441792 | tf_op jit(solution)/shard_map/all_to_all | solution.py:270
  59.6 7.2 %collective-permute-done = bf16[144,2048]{1,0:T(8,128)(2,1)S(1)} collective-permute-done((bf16[144,2048]{1,0:T(8,128)(2,1)S(1)}, bf16[144,2048]{1,0:T(8,128)(2,1)S(1)}, u32[]{:S(2)}, u32[]{:S(2)}) %collective-permute-start) | collective-permute-done | bytes 589856 | tf_op jit(solution)/shard_map/ppermute | solution.py:254
  66.8 3.2 %all-gather.3.cloned.1.call-done = bf16[2048,1024]{1,0:T(8,128)(2,1)} async-done(((bf16[256,1024]{1,0:T(8,128)(2,1)}), bf16[2048,1024]{1,0:T(8,128)(2,1)}) %all-gather.3.cloned.1.call-update) | async-done | bytes 4194320 | tf_op jit(solution)/shard_map/all_gather | solution.py:274
  70.1 3.6 %fusion.5 = f32[288,1024]{1,0:T(8,128)S(1)} fusion(bf16[2048,1024]{1,0:T(8,128)(2,1)} %all-gather.3.cloned.1.call-done, bf16[144,2048]{1,0:T(8,128)(2,1)S(1)} %collective-permute-done, bf16[144,2048]{1,0:T(8,128)(2,1)S(1)} %get-tuple-element.31), kind=kOutput, calls=%fused_computation.14 | convolution fusion | flops 1210318848 | bytes 6553600 | tf_op jit(solution)/shard_map/dot_general | solution.py:316
  74.6 1.5 collective-permute-start.1
  76.1 34.5 %all-gather.5.cloned.1.call-done = bf16[2048,1408]{1,0:T(8,128)(2,1)} async-done(((bf16[256,1408]{1,0:T(8,128)(2,1)}), bf16[2048,1408]{1,0:T(8,128)(2,1)}) %all-gather.5.cloned.1.call-update) | async-done | bytes 5767184 | tf_op jit(solution)/shard_map/all_gather | solution.py:274
  111.5 1.5 collective-permute-start.3
  113.1 2.3 %fusion.2 = f32[288,384]{1,0:T(8,128)S(1)} fusion(bf16[2048,1408]{1,0:T(8,128)(2,1)} %all-gather.5.cloned.1.call-done, bf16[144,2048]{1,0:T(8,128)(2,1)S(1)} %collective-permute-done, bf16[144,2048]{1,0:T(8,128)(2,1)S(1)} %get-tuple-element.31), kind=kOutput, calls=%fused_computation.6 | convolution fusion | flops 455344128 | bytes 3194880 | tf_op jit(solution)/shard_map/dot_general | solution.py:316
  116.8 2.7 %fusion = f32[288,1024]{1,0:T(8,128)S(1)} fusion(bf16[2048,1408]{1,0:T(8,128)(2,1)S(1)} %copy-done.16, bf16[144,2048]{1,0:T(8,128)(2,1)} %copy-done.20, bf16[144,2048]{1,0:T(8,128)(2,1)} %copy-done.14), kind=kOutput, calls=%fused_computation.4 | convolution fusion | flops 1210318848 | bytes 6553600 | tf_op jit(solution)/shard_map/dot_general | solution.py:316
  120.4 1.3 collective-permute-start.2
  125.6 5.2 %collective-permute-start.11 = (bf16[3,48,256]{2,1,0:T(8,128)(2,1)S(1)}, bf16[3,48,256]{2,1,0:T(8,128)(2,1)S(1)}, u32[]{:S(2)}, u32[]{:S(2)}) collective-permute-start(bf16[3,48,256]{2,1,0:T(8,128)(2,1)S(1)} %get-tuple-element.15), channel_id=1, source_target_pairs={{0,7},{1,6},{2,5},{3,4},{4,3},{5,2},{6,1},{7,0},{8,15},{9,14},{10,... | collective-permute-start | bytes 221192 | tf_op jit(solution)/shard_map/ppermute | solution.py:324
  134.2 1.9 collective-permute-done.5
  136.1 2.7 %collective-permute-start.6 = (bf16[3,48,256]{2,1,0:T(8,128)(2,1)S(1)}, bf16[3,48,256]{2,1,0:T(8,128)(2,1)S(1)}, u32[]{:S(2)}, u32[]{:S(2)}) collective-permute-start(bf16[3,48,256]{2,1,0:T(8,128)(2,1)S(1)} %get-tuple-element.15), channel_id=1, source_target_pairs={{0,2},{1,3},{2,0},{3,1},{4,6},{5,7},{6,4},{7,5},{8,10},{9,11},{10,... | collective-permute-start | bytes 221192 | tf_op jit(solution)/shard_map/ppermute | solution.py:324
  139.7 2.9 %collective-permute-done.6 = bf16[3,48,256]{2,1,0:T(8,128)(2,1)S(1)} collective-permute-done((bf16[3,48,256]{2,1,0:T(8,128)(2,1)S(1)}, bf16[3,48,256]{2,1,0:T(8,128)(2,1)S(1)}, u32[]{:S(2)}, u32[]{:S(2)}) %collective-permute-start.6) | collective-permute-done | bytes 73760 | tf_op jit(solution)/shard_map/ppermute | solution.py:324
  142.6 1.8 collective-permute-start.7
  144.4 3.8 %collective-permute-done.7 = bf16[3,48,256]{2,1,0:T(8,128)(2,1)S(1)} collective-permute-done((bf16[3,48,256]{2,1,0:T(8,128)(2,1)S(1)}, bf16[3,48,256]{2,1,0:T(8,128)(2,1)S(1)}, u32[]{:S(2)}, u32[]{:S(2)}) %collective-permute-start.7) | collective-permute-done | bytes 73760 | tf_op jit(solution)/shard_map/ppermute | solution.py:324
  148.2 4.2 %collective-permute-start.8 = (bf16[3,48,256]{2,1,0:T(8,128)(2,1)S(1)}, bf16[3,48,256]{2,1,0:T(8,128)(2,1)S(1)}, u32[]{:S(2)}, u32[]{:S(2)}) collective-permute-start(bf16[3,48,256]{2,1,0:T(8,128)(2,1)S(1)} %get-tuple-element.15), channel_id=1, source_target_pairs={{0,4},{1,5},{2,6},{3,7},{4,0},{5,1},{6,2},{7,3},{8,12},{9,13},{10,... | collective-permute-start | bytes 221192 | tf_op jit(solution)/shard_map/ppermute | solution.py:324
  152.4 2.8 %collective-permute-done.8 = bf16[3,48,256]{2,1,0:T(8,128)(2,1)S(1)} collective-permute-done((bf16[3,48,256]{2,1,0:T(8,128)(2,1)S(1)}, bf16[3,48,256]{2,1,0:T(8,128)(2,1)S(1)}, u32[]{:S(2)}, u32[]{:S(2)}) %collective-permute-start.8) | collective-permute-done | bytes 73760 | tf_op jit(solution)/shard_map/ppermute | solution.py:324
  155.2 1.7 collective-permute-start.9
  156.8 5.1 %collective-permute-done.9 = bf16[3,48,256]{2,1,0:T(8,128)(2,1)S(1)} collective-permute-done((bf16[3,48,256]{2,1,0:T(8,128)(2,1)S(1)}, bf16[3,48,256]{2,1,0:T(8,128)(2,1)S(1)}, u32[]{:S(2)}, u32[]{:S(2)}) %collective-permute-start.9) | collective-permute-done | bytes 73760 | tf_op jit(solution)/shard_map/ppermute | solution.py:324
  163.8 10.0 %read_state.1 = (f32[3,48,1024]{2,1,0:T(8,128)S(1)}, f32[6,48,1024]{2,1,0:T(8,128)S(1)}) custom-call(bf16[48,16,64,128]{3,2,1,0:T(8,128)(2,1)} %state.1, f32[48,24,128]{2,1,0:T(8,128)S(1)} %get-tuple-element.26.b_all, f32[48,24,128]{2,1,0:T(8,128)S(1)} %get-tuple-element.25.c_all, f32[8,1024]{1,0:T(8,128)S(1)} %get-tuple-element.36.mask), custom_call_target="tpu_custom_call" | custom-call | tf_op jit(solution)/shard_map/read_state/pallas_call | solution.py:206
  175.7 3.6 %collective-permute-done.12 = f32[3,8,48]{2,1,0:T(8,128)S(1)} collective-permute-done((f32[3,8,48]{2,1,0:T(8,128)S(1)}, f32[3,8,48]{2,1,0:T(8,128)S(1)}, u32[]{:S(2)}, u32[]{:S(2)}) %collective-permute-start.12) | collective-permute-done | bytes 4640 | tf_op jit(solution)/shard_map/ppermute | solution.py:343
  179.3 2.0 %collective-permute-start.13 = (f32[3,8,48]{2,1,0:T(8,128)S(1)}, f32[3,8,48]{2,1,0:T(8,128)S(1)}, u32[]{:S(2)}, u32[]{:S(2)}) collective-permute-start(f32[3,8,48]{2,1,0:T(8,128)S(1)} %add.80), channel_id=1, source_target_pairs={{0,2},{1,3},{2,0},{3,1},{4,6},{5,7},{6,4},{7,5},{8,10},{9,11},{10,... | collective-permute-start | bytes 13832 | tf_op jit(solution)/shard_map/ppermute | solution.py:343
  181.4 3.1 %collective-permute-done.13 = f32[3,8,48]{2,1,0:T(8,128)S(1)} collective-permute-done((f32[3,8,48]{2,1,0:T(8,128)S(1)}, f32[3,8,48]{2,1,0:T(8,128)S(1)}, u32[]{:S(2)}, u32[]{:S(2)}) %collective-permute-start.13) | collective-permute-done | bytes 4640 | tf_op jit(solution)/shard_map/ppermute | solution.py:343
  184.5 3.1 %collective-permute-start.14 = (f32[3,8,48]{2,1,0:T(8,128)S(1)}, f32[3,8,48]{2,1,0:T(8,128)S(1)}, u32[]{:S(2)}, u32[]{:S(2)}) collective-permute-start(f32[3,8,48]{2,1,0:T(8,128)S(1)} %add.81), channel_id=1, source_target_pairs={{0,4},{1,5},{2,6},{3,7},{4,0},{5,1},{6,2},{7,3},{8,12},{9,13},{10,... | collective-permute-start | bytes 13832 | tf_op jit(solution)/shard_map/ppermute | solution.py:343
  187.8 1.9 collective-permute-done.14
  189.7 1.4 norm_kernel.1
  (112 shorter events, 25.2 us)
Async XLA Ops:
  6.5 49.9 %copy-start = (f32[128]{0:T(128)S(1)}, f32[128]{0:T(128)}, u32[]{:S(2)}) copy-start(f32[128]{0:T(128)} %param.38) | copy-start | bytes 1540
  6.5 63.5 %all-gather.3.cloned.1.call-start = ((), (), s32[]{:S(2)}) async-start(), calls=%async_computation.2 | async-start | bytes 4718592 | tf_op jit(solution)/shard_map/all_gather | solution.py:274
  8.7 1.7 copy-start.3
  10.4 1.7 copy-start.4
  12.0 1.7 copy-start.5
  39.3 15.5 %copy-start.13 = (bf16[3,48,4096]{2,1,0:T(8,128)(2,1)S(1)}, bf16[3,48,4096]{2,1,0:T(8,128)(2,1)}, u32[]{:S(2)}) copy-start(bf16[3,48,4096]{2,1,0:T(8,128)(2,1)} %param.32) | copy-start | bytes 3538948
  39.3 71.2 %all-gather.5.cloned.1.call-start = ((), (), s32[]{:S(2)}) async-start(), calls=%async_computation.3 | async-start | bytes 6488064 | tf_op jit(solution)/shard_map/all_gather | solution.py:274
  54.8 2.2 %copy-start.11 = (f32[128]{0:T(128)S(1)}, f32[128]{0:T(128)}, u32[]{:S(2)}) copy-start(f32[128]{0:T(128)} %param.37) | copy-start | bytes 1540
  54.8 2.9 %copy-start.12 = (f32[128]{0:T(128)S(1)}, f32[128]{0:T(128)}, u32[]{:S(2)}) copy-start(f32[128]{0:T(128)} %param.36) | copy-start | bytes 1540
  54.9 58.1 %copy-start.14 = (bf16[144,2048]{1,0:T(8,128)(2,1)}, bf16[144,2048]{1,0:T(8,128)(2,1)S(1)}, u32[]{:S(2)}) copy-start(bf16[144,2048]{1,0:T(8,128)(2,1)S(1)} %get-tuple-element.31) | copy-start | bytes 1769476
  55.0 4.4 %copy-start.15 = (bf16[48,3,2,1,128]{4,2,3,1,0:T(2,128)(2,1)S(1)}, bf16[48,3,2,1,128]{4,2,3,1,0:T(2,128)(2,1)}, u32[]{:S(2)}) copy-start(bf16[48,3,2,1,128]{4,2,3,1,0:T(2,128)(2,1)} %param.35) | copy-start | bytes 221188
  55.0 11.9 %collective-permute-start = (bf16[144,2048]{1,0:T(8,128)(2,1)S(1)}, bf16[144,2048]{1,0:T(8,128)(2,1)S(1)}, u32[]{:S(2)}, u32[]{:S(2)}) collective-permute-start(bf16[144,2048]{1,0:T(8,128)(2,1)S(1)} %get-tuple-element.32), channel_id=1, source_target_pairs={{0,64},{8,72},{16,80},{24,88},{32,96},{40,104},{48,112},{56,120},{... | collective-permute-start | bytes 1769480 | tf_op jit(solution)/shard_map/ppermute | solution.py:254
  55.7 18.0 %copy-start.18 = (s32[16]{0:T(128)}, s32[16]{0:T(128)S(1)}, u32[]{:S(2)}) copy-start(s32[16]{0:T(128)S(1)} %get-tuple-element.22) | copy-start | bytes 196
  66.8 46.2 %copy-start.20 = (bf16[144,2048]{1,0:T(8,128)(2,1)}, bf16[144,2048]{1,0:T(8,128)(2,1)S(1)}, u32[]{:S(2)}) copy-start(bf16[144,2048]{1,0:T(8,128)(2,1)S(1)} %collective-permute-done) | copy-start | bytes 1769476
  74.6 100.3 %collective-permute-start.1 = (f32[144,1024]{1,0:T(8,128)}, f32[144,1024]{1,0:T(8,128)S(1)}, u32[]{:S(2)}, u32[]{:S(2)}) collective-permute-start(f32[144,1024]{1,0:T(8,128)} %get-tuple-element.29), channel_id=1, source_target_pairs={{0,64},{8,72},{16,80},{24,88},{32,96},{40,104},{48,112},{56,120},{... | collective-permute-start | bytes 1769480 | tf_op jit(solution)/shard_map/ppermute | solution.py:254
  111.5 5.3 %copy-start.16 = (bf16[2048,1408]{1,0:T(8,128)(2,1)S(1)}, bf16[2048,1408]{1,0:T(8,128)(2,1)}, u32[]{:S(2)}) copy-start(bf16[2048,1408]{1,0:T(8,128)(2,1)} %all-gather.5.cloned.1.call-done) | copy-start | bytes 17301508
  111.5 10.2 %collective-permute-start.3 = (bf16[64,16,128]{2,1,0:T(8,128)(2,1)S(1)}, bf16[64,16,128]{2,1,0:T(8,128)(2,1)S(1)}, u32[]{:S(2)}, u32[]{:S(2)}) collective-permute-start(bf16[64,16,128]{2,1,0:T(8,128)(2,1)S(1)} %slice.69), channel_id=1, source_target_pairs={{0,64},{8,72},{16,80},{24,88},{32,96},{40,104},{48,112},{56,120},{... | collective-permute-start | bytes 786440 | tf_op jit(solution)/shard_map/ppermute | solution.py:254
  116.1 9.4 %collective-permute-start.4 = (f32[144,384]{1,0:T(8,128)}, f32[144,384]{1,0:T(8,128)S(1)}, u32[]{:S(2)}, u32[]{:S(2)}) collective-permute-start(f32[144,384]{1,0:T(8,128)} %get-tuple-element.33), channel_id=1, source_target_pairs={{0,64},{8,72},{16,80},{24,88},{32,96},{40,104},{48,112},{56,120},{... | collective-permute-start | bytes 663560 | tf_op jit(solution)/shard_map/ppermute | solution.py:254
  120.4 53.4 %collective-permute-start.2 = (f32[144,1024]{1,0:T(8,128)}, f32[144,1024]{1,0:T(8,128)S(1)}, u32[]{:S(2)}, u32[]{:S(2)}) collective-permute-start(f32[144,1024]{1,0:T(8,128)} %get-tuple-element.27), channel_id=1, source_target_pairs={{0,64},{8,72},{16,80},{24,88},{32,96},{40,104},{48,112},{56,120},{... | collective-permute-start | bytes 1769480 | tf_op jit(solution)/shard_map/ppermute | solution.py:254
  125.6 37.2 %collective-permute-start.11 = (bf16[3,48,256]{2,1,0:T(8,128)(2,1)S(1)}, bf16[3,48,256]{2,1,0:T(8,128)(2,1)S(1)}, u32[]{:S(2)}, u32[]{:S(2)}) collective-permute-start(bf16[3,48,256]{2,1,0:T(8,128)(2,1)S(1)} %get-tuple-element.15), channel_id=1, source_target_pairs={{0,7},{1,6},{2,5},{3,4},{4,3},{5,2},{6,1},{7,0},{8,15},{9,14},{10,... | collective-permute-start | bytes 221192 | tf_op jit(solution)/shard_map/ppermute | solution.py:324
  130.8 31.1 %collective-permute-start.10 = (bf16[3,48,256]{2,1,0:T(8,128)(2,1)S(1)}, bf16[3,48,256]{2,1,0:T(8,128)(2,1)}, u32[]{:S(2)}, u32[]{:S(2)}) collective-permute-start(bf16[3,48,256]{2,1,0:T(8,128)(2,1)S(1)} %get-tuple-element.15), channel_id=1, source_target_pairs={{0,6},{1,7},{2,4},{3,5},{4,2},{5,3},{6,0},{7,1},{8,14},{9,15},{10,... | collective-permute-start | bytes 221192 | tf_op jit(solution)/shard_map/ppermute | solution.py:324
  131.6 4.5 %collective-permute-start.5 = (bf16[3,48,256]{2,1,0:T(8,128)(2,1)S(1)}, bf16[3,48,256]{2,1,0:T(8,128)(2,1)}, u32[]{:S(2)}, u32[]{:S(2)}) collective-permute-start(bf16[3,48,256]{2,1,0:T(8,128)(2,1)S(1)} %get-tuple-element.15), channel_id=1, source_target_pairs={{0,1},{1,0},{2,3},{3,2},{4,5},{5,4},{6,7},{7,6},{8,9},{9,8},{10,11... | collective-permute-start | bytes 221192 | tf_op jit(solution)/shard_map/ppermute | solution.py:324
  136.1 6.5 %collective-permute-start.6 = (bf16[3,48,256]{2,1,0:T(8,128)(2,1)S(1)}, bf16[3,48,256]{2,1,0:T(8,128)(2,1)S(1)}, u32[]{:S(2)}, u32[]{:S(2)}) collective-permute-start(bf16[3,48,256]{2,1,0:T(8,128)(2,1)S(1)} %get-tuple-element.15), channel_id=1, source_target_pairs={{0,2},{1,3},{2,0},{3,1},{4,6},{5,7},{6,4},{7,5},{8,10},{9,11},{10,... | collective-permute-start | bytes 221192 | tf_op jit(solution)/shard_map/ppermute | solution.py:324
  142.6 5.6 %collective-permute-start.7 = (bf16[3,48,256]{2,1,0:T(8,128)(2,1)S(1)}, bf16[3,48,256]{2,1,0:T(8,128)(2,1)S(1)}, u32[]{:S(2)}, u32[]{:S(2)}) collective-permute-start(bf16[3,48,256]{2,1,0:T(8,128)(2,1)S(1)} %get-tuple-element.15), channel_id=1, source_target_pairs={{0,3},{1,2},{2,1},{3,0},{4,7},{5,6},{6,5},{7,4},{8,11},{9,10},{10,... | collective-permute-start | bytes 221192 | tf_op jit(solution)/shard_map/ppermute | solution.py:324
  148.2 7.0 %collective-permute-start.8 = (bf16[3,48,256]{2,1,0:T(8,128)(2,1)S(1)}, bf16[3,48,256]{2,1,0:T(8,128)(2,1)S(1)}, u32[]{:S(2)}, u32[]{:S(2)}) collective-permute-start(bf16[3,48,256]{2,1,0:T(8,128)(2,1)S(1)} %get-tuple-element.15), channel_id=1, source_target_pairs={{0,4},{1,5},{2,6},{3,7},{4,0},{5,1},{6,2},{7,3},{8,12},{9,13},{10,... | collective-permute-start | bytes 221192 | tf_op jit(solution)/shard_map/ppermute | solution.py:324
  155.2 6.8 %collective-permute-start.9 = (bf16[3,48,256]{2,1,0:T(8,128)(2,1)S(1)}, bf16[3,48,256]{2,1,0:T(8,128)(2,1)S(1)}, u32[]{:S(2)}, u32[]{:S(2)}) collective-permute-start(bf16[3,48,256]{2,1,0:T(8,128)(2,1)S(1)} %get-tuple-element.15), channel_id=1, source_target_pairs={{0,5},{1,4},{2,7},{3,6},{4,1},{5,0},{6,3},{7,2},{8,13},{9,12},{10,... | collective-permute-start | bytes 221192 | tf_op jit(solution)/shard_map/ppermute | solution.py:324
  163.7 10.0 %copy-start.7 = (bf16[48,3,1024]{2,0,1:T(8,128)(2,1)S(1)}, bf16[48,3,1024]{2,0,1:T(8,128)(2,1)}, u32[]{:S(2)}) copy-start(bf16[48,3,1024]{2,0,1:T(8,128)(2,1)} %param.34) | copy-start | bytes 884740
  174.9 6.4 %copy-start.17 = (f32[8192]{0:T(1024)S(1)}, f32[8192]{0:T(1024)}, u32[]{:S(2)}) copy-start(f32[8192]{0:T(1024)} %param.39) | copy-start | bytes 98308
  174.9 12.6 %copy-start.19 = (s32[16]{0:T(128)S(1)}, s32[16]{0:T(128)}, u32[]{:S(2)}) copy-start(s32[16]{0:T(128)} %copy-done.18) | copy-start | bytes 196
  175.6 3.7 %collective-permute-start.12 = (f32[3,8,48]{2,1,0:T(8,128)S(1)}, f32[3,8,48]{2,1,0:T(8,128)S(1)}, u32[]{:S(2)}, u32[]{:S(2)}) collective-permute-start(f32[3,8,48]{2,1,0:T(8,128)S(1)} %get-tuple-element.20), channel_id=1, source_target_pairs={{0,1},{1,0},{2,3},{3,2},{4,5},{5,4},{6,7},{7,6},{8,9},{9,8},{10,11... | collective-permute-start | bytes 13832 | tf_op jit(solution)/shard_map/ppermute | solution.py:343
  179.3 5.2 %collective-permute-start.13 = (f32[3,8,48]{2,1,0:T(8,128)S(1)}, f32[3,8,48]{2,1,0:T(8,128)S(1)}, u32[]{:S(2)}, u32[]{:S(2)}) collective-permute-start(f32[3,8,48]{2,1,0:T(8,128)S(1)} %add.80), channel_id=1, source_target_pairs={{0,2},{1,3},{2,0},{3,1},{4,6},{5,7},{6,4},{7,5},{8,10},{9,11},{10,... | collective-permute-start | bytes 13832 | tf_op jit(solution)/shard_map/ppermute | solution.py:343
  184.5 5.2 %collective-permute-start.14 = (f32[3,8,48]{2,1,0:T(8,128)S(1)}, f32[3,8,48]{2,1,0:T(8,128)S(1)}, u32[]{:S(2)}, u32[]{:S(2)}) collective-permute-start(f32[3,8,48]{2,1,0:T(8,128)S(1)} %add.81), channel_id=1, source_target_pairs={{0,4},{1,5},{2,6},{3,7},{4,0},{5,1},{6,2},{7,3},{8,12},{9,13},{10,... | collective-permute-start | bytes 13832 | tf_op jit(solution)/shard_map/ppermute | solution.py:343
  (6 other events, 5.1 us)
Sparse Core Ops, SparseCore 0:
  39.5 30.5 all-gather.2
  71.8 38.7 all-gather.4

commit v2 on v1

v2 whole, which is shorter than its diff:
```python
import functools

import jax
import jax.numpy as jnp
from jax import lax
from jax.experimental import pallas as pl
from jax.experimental.pallas import tpu as pltpu
from jax.sharding import Mesh
from jax.sharding import PartitionSpec as P

TAPS = 4
ADAM_STEP = 100
STEPS = 3
ROWS = 48
FLAT = STEPS * ROWS
HEADS = 128
GROUPS = 8
HEAD_DIM = 64
STATE = 128
OWN_HEADS = 16
SPAN = OWN_HEADS * HEAD_DIM
JOINED = 18560
PIECE = 3712
PIECES = JOINED // PIECE
SHARD = 80
INNER = HEADS * HEAD_DIM

beta_one = 0.9
beta_two = 0.95
adam_eps = 1e-08
weight_decay = 0.1
norm_eps = 1e-05
HIGH = lax.Precision.HIGHEST


def adamw(master, gradient, first, second, rate):
    slope = gradient.astype(jnp.float32)
    moment_one = beta_one * first + (1.0 - beta_one) * slope
    moment_two = beta_two * second + (1.0 - beta_two) * slope * slope
    fixed_one = moment_one / (1.0 - beta_one**ADAM_STEP)
    fixed_two = moment_two / (1.0 - beta_two**ADAM_STEP)
    update = fixed_one / (jnp.sqrt(fixed_two) + adam_eps) + weight_decay * master
    return (master - rate * update).astype(jnp.bfloat16)


def refit_kernel(
    ints, order, rate, conv_m, conv_g, conv_f, conv_s, master, grad, first, second,
    out, work, m, g, f, s, sems,
):
    copies = []
    for p in range(PIECES):
        cols = pl.ds(p * PIECE, PIECE)
        copies.append(
            [
                pltpu.make_async_copy(hbm.at[:, cols], vmem.at[:, cols], sems.at[p, i])
                for i, (hbm, vmem) in enumerate(((master, m), (grad, g), (first, f), (second, s)))
            ]
        )
    for piece in copies:
        for copy in piece:
            copy.start()
    for p, piece in enumerate(copies):
        for copy in piece:
            copy.wait()
        for j in range(p * PIECE, (p + 1) * PIECE, 128):
            cols = slice(j, j + 128)
            work[:, cols] = adamw(m[:, cols], g[:, cols], f[:, cols], s[:, cols], rate[...]).astype(jnp.float32)

    lane = lax.broadcasted_iota(jnp.int32, (32, 128), 1)
    conv = adamw(conv_m[...], conv_g[...], conv_f[...], conv_s[...], rate[...])
    shift = lax.broadcasted_iota(jnp.int32, (SHARD, 128), 1) - lax.broadcasted_iota(jnp.int32, (SHARD, 128), 0) == 16
    conv = jnp.dot(conv, shift.astype(jnp.bfloat16), preferred_element_type=jnp.float32)
    conv = jnp.concatenate([conv, jnp.zeros((27, 128), jnp.float32)], axis=0)
    offsets = [ints[HEADS + GROUPS + i] for i in range(5)]
    dt = work[:, pl.ds(pl.multiple_of(offsets[4], 128), 128)]
    onehot = (lax.broadcasted_iota(jnp.int32, (HEADS, HEADS), 0) == order[...]).astype(jnp.bfloat16)
    dt = jnp.dot(dt.astype(jnp.bfloat16), onehot, preferred_element_type=jnp.float32)

    def block(start):
        return work[:, pl.ds(pl.multiple_of(start, 128), 128)]

    def half(start, head, low):
        wide = block(start + (head // 2) * 128)
        turn = (head % 2) != (0 if low else 1)
        return jnp.where(turn, pltpu.roll(wide, 64, 1), wide)

    for owner in range(8):
        group = ints[HEADS + owner]
        mine = dt if owner == 0 else pltpu.roll(dt, 128 - 16 * owner, 1)
        leading = (block(offsets[2] + group * 128), block(offsets[3] + group * 128), jnp.where(lane < 16, mine, 0.0), conv)
        for quarter in range(4):
            to = quarter * 8 + owner
            out[to, :, 0:128] = leading[quarter].astype(jnp.bfloat16)
            for k in range(2):
                low = ints[owner * OWN_HEADS + 4 * quarter + 2 * k]
                high = ints[owner * OWN_HEADS + 4 * quarter + 2 * k + 1]
                for segment, at in ((1, 128), (0, 384)):
                    start = offsets[segment]
                    both = jnp.where(lane < 64, half(start, low, True), half(start, high, False))
                    out[to, :, at + k * 128 : at + (k + 1) * 128] = both.astype(jnp.bfloat16)


def refit(rate, ints, order, conv, weight):
    vmem = pl.BlockSpec(memory_space=pltpu.VMEM)
    hbm = pl.BlockSpec(memory_space=pltpu.HBM)
    return pl.pallas_call(
        refit_kernel,
        in_specs=[pl.BlockSpec(memory_space=pltpu.SMEM)] + [vmem] * 6 + [hbm] * 4,
        out_specs=vmem,
        out_shape=jax.ShapeDtypeStruct((32, 32, 640), jnp.bfloat16),
        scratch_shapes=[
            pltpu.VMEM((32, JOINED), jnp.float32),
            pltpu.VMEM((32, JOINED), jnp.float32),
            pltpu.VMEM((32, JOINED), jnp.bfloat16),
            pltpu.VMEM((32, JOINED), jnp.float32),
            pltpu.VMEM((32, JOINED), jnp.float32),
            pltpu.SemaphoreType.DMA((PIECES, 4)),
        ],
        compiler_params=pltpu.CompilerParams(vmem_limit_bytes=58 * 2**20),
        name="refit",
    )(ints, order, rate.reshape(1, 1), *conv, *weight)


def tables_kernel(place, ints, decay, bias, skip, gain, lanes, member, mask, spread):
    owner = place[0]
    lane = lax.broadcasted_iota(jnp.int32, (1, 128), 1)
    heads = []
    for k in range(8):
        low = ints[owner * OWN_HEADS + 2 * k]
        high = ints[owner * OWN_HEADS + 2 * k + 1]
        heads.append(jnp.where(lane < 64, low, high))
        halves = []
        for head, odd in ((low, 0), (high, 1)):
            wide = gain[:, pl.ds(pl.multiple_of(head // 2 * 128, 128), 128)]
            halves.append(jnp.where(head % 2 != odd, pltpu.roll(wide, 64, 1), wide))
        lanes[3:4, k * 128 : (k + 1) * 128] = jnp.where(lane < 64, halves[0], halves[1])
    heads = jnp.concatenate(heads, axis=1)
    onehot = (lax.broadcasted_iota(jnp.int32, (HEADS, SPAN), 0) == heads).astype(jnp.float32)
    rows = jnp.concatenate([-jnp.exp(decay[...]), bias[...], skip[...], jnp.zeros((5, HEADS), jnp.float32)], axis=0)
    lanes[0:3, :] = jnp.dot(rows, onehot, precision=HIGH, preferred_element_type=jnp.float32)[0:3]
    group = heads // OWN_HEADS
    member[...] = (lax.broadcasted_iota(jnp.int32, (GROUPS, SPAN), 0) == group).astype(jnp.float32)
    for k in range(GROUPS):
        partner = lax.rem(owner // 4 * 4 + k // 4 * 4, 8) + lax.rem(owner + k, 4)
        mask[k : k + 1, :] = (group == ints[HEADS + partner]).astype(jnp.float32)
    slot = lax.broadcasted_iota(jnp.int32, (128, SPAN), 1) // HEAD_DIM
    spread[...] = (lax.broadcasted_iota(jnp.int32, (128, SPAN), 0) == slot).astype(jnp.bfloat16)


def multiply(place, rows, weights, outs):
    total = None
    for n, turn in enumerate((0, 3, 1, 2)):
        at = lax.rem(place[2] + turn, 4)
        cols = [pl.ds(pl.multiple_of((x * 4 + at) * 512, 512), 512) for x in range(2)]
        left = jnp.concatenate([jnp.concatenate([ref[:, c] for c in cols], axis=1) for ref in rows], axis=0)
        right = jnp.concatenate([part[...] for part in weights[n]], axis=0)
        term = jnp.dot(left, right, preferred_element_type=jnp.float32)
        total = term if total is None else total + term
    for i, out in enumerate(outs):
        out[0:FLAT, :] = total[i * FLAT : (i + 1) * FLAT].astype(jnp.bfloat16)


def wide_product_kernel(place, *refs):
    top, bottom, left_top, right_bottom, from_left, from_right = refs[6:12]
    halves = lambda ref: (ref.at[0:512, :], ref.at[512:1024, :])
    left_bottom, far_top = halves(from_left)
    right_top, far_bottom = halves(from_right)
    weights = ((top, bottom), (left_top, left_bottom), (right_top, right_bottom), (far_top, far_bottom))
    multiply(place, refs[:6], weights, refs[12:16])


def first_product_kernel(place, ints, *refs):
    buffers, outs, shards = refs[6:10], refs[10:14], refs[14]
    multiply(place, refs[:6], [(ref,) for ref in buffers], outs)
    owner, z = place[0], place[2]
    row = 0
    for piece in buffers:
        for t in range(piece.shape[0] // 32):
            shards[row : row + 8, :] = piece[t * 32 : t * 32 + 16, :].astype(jnp.float32)[:8]
            row += 8
    lane = lax.broadcasted_iota(jnp.int32, (8, 128), 1)

    def shard(device, shift):
        device = jnp.minimum(device, 127)
        turn = lax.rem(device // 16 % 4 + 4 - z, 4)
        at = jnp.where(turn == 0, 0, jnp.where(turn == 3, 1, turn + 1)) * 32
        at = (at + device // 64 * 16 + device % 16) * 8
        return pltpu.roll(shards[pl.ds(pl.multiple_of(at, 8), 8), :], lax.rem(shift, 128), 1)

    def unit(u, at):
        device = 4 * u // 5
        offset = 64 * u - 80 * device
        low = shard(device, at + 240 - offset)
        high = shard(device + 1, at + 192 - offset)
        return jnp.where(lane - at < 80 - offset, low, high)

    blocks = []
    for block in range(10):
        if block < 8:
            units = [ints[owner * OWN_HEADS + 2 * block + i] for i in range(2)]
        else:
            units = [HEADS + 16 * (block - 8) + 2 * ints[HEADS + owner] + i for i in range(2)]
        blocks.append(jnp.where(lane < 64, unit(units[0], 0), unit(units[1], 64)))
    taps = jnp.concatenate(blocks, axis=0).astype(jnp.bfloat16)
    for out in outs:
        out[FLAT : FLAT + 80, :] = taps


def silu(value):
    return value * jax.nn.sigmoid(value)


def convolve(inputs, stored, taps):
    window = [stored[j].astype(jnp.float32) for j in range(TAPS - 1)] + inputs
    outputs = []
    for moment in range(STEPS):
        total = taps[TAPS : TAPS + 1]
        for lag in range(TAPS):
            total = total + taps[lag : lag + 1] * window[moment + lag]
        outputs.append(silu(total).astype(jnp.bfloat16))
    return outputs


def gathered(place, pieces, buffer):
    quarter = 2 * place[1] + place[3]
    width = min(pieces[0].shape[1], 256)
    for i, piece in enumerate(pieces):
        for part in range(piece.shape[1] // width):
            at = pl.multiple_of(lax.bitwise_xor(quarter, i) * width + part * SPAN, 128)
            buffer[:, pl.ds(at, width)] = piece[:, part * width : (part + 1) * width]
    return [buffer[t * ROWS : (t + 1) * ROWS, :].astype(jnp.float32) for t in range(STEPS)]


def groups_kernel(place, *refs):
    pieces, (stored, out, dt, head_taps, buffer) = refs[:4], refs[4:]
    values = gathered(place, pieces, buffer)
    taps = buffer[FLAT : FLAT + 80, 384:512].astype(jnp.float32)
    for block in range(8):
        head_taps[:, block * 128 : (block + 1) * 128] = taps[block * 8 : block * 8 + 8]
    taps = jnp.concatenate([taps[64:72], taps[72:80]], axis=1)
    for t, value in enumerate(convolve([value[:, :256] for value in values], stored, taps)):
        out[t] = value
        dt[t] = values[t][:, 256:384].astype(jnp.bfloat16)


def state_kernel(state, every, c_all, mask, out, pair):
    chosen = mask[...]
    for r in range(8):
        read = lax.dot_general(
            c_all[r].astype(jnp.bfloat16),
            state[r].reshape(SPAN, STATE),
            (((1,), (1,)), ((), ())),
            preferred_element_type=jnp.float32,
        )
        for t in range(STEPS):
            rows = slice(8 * t, 8 * t + 8)
            out[t, r : r + 1, :] = jnp.sum(read[rows] * chosen, axis=0, keepdims=True)
    n = 0
    for t in range(STEPS):
        for s in range(t + 1):
            total = None
            for k in range(GROUPS):
                both = every[k, t, :, STATE:] * every[k, s, :, :STATE]
                term = jnp.sum(both, axis=1, keepdims=True) * mask[k : k + 1, :]
                total = term if total is None else total + term
            pair[n] = total
            n += 1


def scan_kernel(place, *refs):
    pieces, (stored, taps, read, pair, dt, spread, params, member, gated, squares, buffer) = refs[:4], refs[4:]
    both = gathered(place, pieces, buffer)
    inputs = [value[:, :SPAN] for value in both]
    values = [v.astype(jnp.float32) for v in convolve(inputs, stored, taps[...])]
    rate = params[0:1]
    bias = params[1:2]
    skip = params[2:3]
    keeps, driven = [], []
    for t in range(STEPS):
        raw = jnp.dot(dt[t], spread[...], preferred_element_type=jnp.float32)
        delta = jax.nn.softplus(raw + bias)
        keeps.append(jnp.exp(delta * rate))
        driven.append(delta * values[t])
    n = 0
    for t in range(STEPS):
        total = skip * values[t]
        offset = n + t
        after = None
        for s in range(t, -1, -1):
            term = pair[offset] * driven[s]
            total = total + (term if after is None else after * term)
            after = keeps[s] if after is None else after * keeps[s]
            offset -= 1
        value = (total + after * read[t]) * silu(both[t][:, SPAN:])
        gated[t] = value
        squares[t] = lax.dot_general(
            member[...], value * value, (((1,), (1,)), ((), ())), precision=HIGH, preferred_element_type=jnp.float32
        )
        n += t + 1


def norm_kernel(gated, squares, member, params, out):
    for t in range(STEPS):
        scale = lax.rsqrt(squares[t] / SPAN + norm_eps)
        lanes = lax.dot_general(
            scale, member[...], (((0,), (0,)), ((), ())), precision=HIGH, preferred_element_type=jnp.float32
        )
        out[t] = (gated[t] * lanes * params[3:4]).astype(jnp.bfloat16)


def call(kernel, shapes, *args, scalars=0, scratch=()):
    vmem = pl.BlockSpec(memory_space=pltpu.VMEM)
    smem = pl.BlockSpec(memory_space=pltpu.SMEM)
    return pl.pallas_call(
        kernel,
        in_specs=[smem] * scalars + [vmem] * (len(args) - scalars),
        out_specs=[vmem] * len(shapes),
        out_shape=[jax.ShapeDtypeStruct(s, d) for s, d in shapes],
        scratch_shapes=scratch,
        compiler_params=pltpu.CompilerParams(vmem_limit_bytes=32 * 2**20),
        name=kernel.__name__,
    )(*args)


def read_state(state, every, c_all, mask):
    return pl.pallas_call(
        state_kernel,
        grid=(ROWS // 8,),
        in_specs=[
            pl.BlockSpec((8, OWN_HEADS, HEAD_DIM, STATE), lambda i: (i, 0, 0, 0)),
            pl.BlockSpec((GROUPS, STEPS, 8, 2 * STATE), lambda i: (0, 0, i, 0)),
            pl.BlockSpec((8, 24, STATE), lambda i: (i, 0, 0)),
            pl.BlockSpec((8, SPAN), lambda i: (0, 0)),
        ],
        out_specs=[
            pl.BlockSpec((3, 8, SPAN), lambda i: (0, i, 0)),
            pl.BlockSpec((6, 8, SPAN), lambda i: (0, i, 0)),
        ],
        out_shape=[
            jax.ShapeDtypeStruct((3, ROWS, SPAN), jnp.float32),
            jax.ShapeDtypeStruct((6, ROWS, SPAN), jnp.float32),
        ],
        compiler_params=pltpu.CompilerParams(vmem_limit_bytes=20 * 2**20),
        name="read_state",
    )(state, every, c_all, mask)


def per_device(
    weight_master,
    weight_grad,
    weight_first,
    weight_second,
    conv_master,
    conv_grad,
    conv_first,
    conv_second,
    learn_rate,
    segment_offsets,
    head_order,
    group_order,
    hidden_input,
    scan_state,
    conv_heads,
    conv_groups,
    decay_log,
    delta_bias,
    skip_gain,
    norm_gain,
):
    owner = lax.axis_index("tp")
    side, z, core = lax.axis_index("x"), lax.axis_index("z"), lax.axis_index("c")
    up = lambda value: lax.ppermute(value, "z", [(i, (i + 1) % 4) for i in range(4)])
    down = lambda value: lax.ppermute(value, "z", [(i, (i + 3) % 4) for i in range(4)])

    def swap(value, turn):
        return lax.ppermute(value, ("x", "c"), [(i, i ^ turn) for i in range(4)])

    position = jnp.stack([owner, side, z, core]).astype(jnp.int32)
    ints = jnp.concatenate([head_order, group_order, segment_offsets])
    def after(value, *others):
        return lax.optimization_barrier((value, *others))[0]

    far = [swap(hidden_input[0], 2)]
    near = swap(hidden_input.reshape(FLAT, -1), 1)

    sent = refit(
        learn_rate, ints, head_order.reshape(1, HEADS),
        (conv_master, conv_grad, conv_first, conv_second),
        (weight_master, weight_grad, weight_first, weight_second),
    )
    owned = lax.all_to_all(after(sent, *far, near), ("x", "c", "tp"), split_axis=0, concat_axis=0, tiled=True)
    owned = owned.reshape(1024, 640)
    far.append(swap(after(hidden_input[1:].reshape(2 * ROWS, -1), owned), 2))

    def exchanged(outs):
        return [outs[0]] + [swap(outs[i], i) for i in range(1, 4)]

    row = lambda value: value.reshape(1, -1)
    params, member, mask, spread = call(
        tables_kernel,
        [
            ((8, SPAN), jnp.float32),
            ((GROUPS, SPAN), jnp.float32),
            ((GROUPS, SPAN), jnp.float32),
            ((128, SPAN), jnp.bfloat16),
        ],
        position, after(ints, sent), row(decay_log), row(delta_bias), row(skip_gain), row(norm_gain), scalars=2,
    )
    stored_heads = jnp.swapaxes(conv_heads, 0, 1)
    stored_groups = jnp.swapaxes(conv_groups.reshape(ROWS, TAPS - 1, 2 * STATE), 0, 1)

    own = owned[:, :128]
    pieces = [own, up(own), down(own), lax.ppermute(own, "z", [(i, (i + 2) % 4) for i in range(4)])]
    far_pair = after(far, *pieces[1:])
    rows = [hidden_input.reshape(FLAT, -1), near, *far, *[swap(value, 1) for value in far_pair]]
    top, bottom = [after(owned[512 * i : 512 * i + 512, 128:], *pieces[1:]) for i in range(2)]
    left_top, right_bottom = up(top), down(bottom)

    first = call(
        first_product_kernel, [((FLAT + 80, 128), jnp.bfloat16)] * 4, position, ints, *rows, *pieces,
        scalars=2, scratch=[pltpu.VMEM((1024, 128), jnp.float32)],
    )
    arrived = after((left_top, right_bottom), first)
    from_left = up(jnp.concatenate([bottom, arrived[0]]))
    from_right = down(jnp.concatenate([top, arrived[1]]))
    b_and_c, dt, head_taps = call(
        groups_kernel,
        [((STEPS, ROWS, 2 * STATE), jnp.bfloat16), ((STEPS, ROWS, 128), jnp.bfloat16), ((8, SPAN), jnp.float32)],
        position, *exchanged(first), stored_groups, scalars=1, scratch=[pltpu.VMEM((FLAT + 80, 512), jnp.bfloat16)],
    )
    ahead = lambda k: [(i, i // 4 * 4 + (i + 4 - k) % 4) for i in range(8)]
    every = jnp.stack([b_and_c] + [lax.ppermute(b_and_c, "tp", ahead(k)) for k in range(1, 4)])
    every = jnp.concatenate([every, lax.ppermute(every, "tp", [(i, i ^ 4) for i in range(8)])])
    every = every.astype(jnp.float32)
    c_all = every[..., STATE:].transpose(2, 1, 0, 3).reshape(ROWS, STEPS * GROUPS, STATE)
    read, pair = read_state(scan_state, every, c_all, mask)

    second = exchanged(
        call(
            wide_product_kernel, [((FLAT, 512), jnp.bfloat16)] * 4, position, *rows,
            after(top, read), bottom, left_top, right_bottom, from_left, from_right,
            scalars=1,
        )
    )
    gated, squares = call(
        scan_kernel,
        [((STEPS, ROWS, SPAN), jnp.float32), ((STEPS, GROUPS, ROWS), jnp.float32)],
        position, *second, stored_heads, head_taps, read, pair, dt, spread, params, member,
        scalars=1, scratch=[pltpu.VMEM((FLAT, 2 * SPAN), jnp.bfloat16)],
    )
    for k in (1, 2, 4):
        squares = squares + lax.ppermute(squares, "tp", [(i, i ^ k) for i in range(8)])
    (mixer_out,) = call(
        norm_kernel, [((STEPS, ROWS, SPAN), jnp.bfloat16)], gated, squares, member, params
    )
    return mixer_out


def solution(mesh):
    mesh = Mesh(mesh.devices.reshape(2, 4, 2, 8), ("x", "z", "c", "tp"))
    fsdp = ("x", "z", "c")
    every = fsdp + ("tp",)
    return jax.shard_map(
        per_device,
        mesh=mesh,
        in_specs=(P(every, None),) * 4
        + (P(None, every),) * 4
        + (P(),) * 4
        + (P(None, fsdp, None), P(fsdp, "tp", None, None), P(fsdp, None, "tp"), P(fsdp, None, None, "tp", None))
        + (P(),) * 4,
        out_specs=P(None, fsdp, "tp"),
        check_vma=False,
    )
```

time: 199 us -> 143 us (0.72)
  blocking collectives: 33.8 us -> 0 us
  waiting for transfers between devices: 70.2 us -> 55.2 us
  between operations: 14.4 us -> 0.93 us
  starting transfers between devices: 27.9 us -> 38.8 us
  matrix products: 10.3 us -> 0 us
  Pallas kernels: 17.8 us -> 26.2 us
  local copies, waits for them, and re-layouts: 22.1 us -> 17.3 us
  other arithmetic: 1.39 us -> 3.82 us
    all_gather x2 -> x0, waiting for transfers between devices: 37.7 us -> none  [gathered(): lax.all_gather(value, 'fsdp', axis_index_groups=planes, axis=0, tiled=True)]
    all_to_all x2 -> x0, blocking collectives: 33.8 us -> none  [owned(): value = lax.all_to_all(value, 'tp', split_axis=0, concat_axis=0, tiled=True)]
    all_to_all x0 -> x1, waiting for transfers between devices: none -> 18.5 us  [per_device(): lax.all_to_all(after(sent, *far, near), ('x', 'c', 'tp'), split_axis=0, c...]
    pallas_call x5 -> x7, Pallas kernels: 7.78 us -> 20.5 us  [the longest x6 13.5 us: call(): pl.pallas_call(kernel, in_specs=[smem] * scalars + [vmem] * (len(args) -...]
    dot_general x6 -> x0, matrix products: 10.3 us -> none  [the longest x3 8.56 us: per_device(): jnp.dot(rows, weights, preferred_element_type=jnp.float32)]
    all_to_all x0 -> x1, starting transfers between devices: none -> 7.52 us  [per_device(): lax.all_to_all(after(sent, *far, near), ('x', 'c', 'tp'), split_axis=0, c...]
    pallas_call x1, Pallas kernels: 10 us -> 5.71 us  [read_state(): pl.pallas_call(state_kernel, grid=(ROWS // 8,), in_specs=[pl.BlockSpec((8...]
    ppermute x12 -> x22, starting transfers between devices: 22.7 us -> 26.5 us  [the longest x11 6.31 us: swap(): return lax.ppermute(value, ('x', 'c'), [(i, i ^ turn) for i in range(4)])]
  transfers between devices with their start and end apart: 17 -> 26, of which waited for: 12 -> 14; matrix products, arithmetic and copies ran while one was open for 12% -> 7% of each run, Pallas kernels for 6% -> 13%
where the time goes in v2:
time: 143 us; the launch traced here: 142 us
  waiting for transfers between devices  55.2 us (39%)
  starting transfers between devices  38.8 us (27%)
  Pallas kernels  26.2 us (18%)
  local copies, waits for them, and re-layouts  17.3 us (12%)
  other arithmetic  3.82 us (3%)
    all_to_all x1, waiting for transfers between devices, per_device(): lax.all_to_all(after(sent, *far, near), ('x', 'c', 'tp'), split_axis=0, c...  18.5 us
    pallas_call x6, Pallas kernels, call(): pl.pallas_call(kernel, in_specs=[smem] * scalars + [vmem] * (len(args) -...  13.5 us
    unnamed x39, local copies, waits for them, and re-layouts  11.9 us
    ppermute x3, waiting for transfers between devices, per_device(): lax.ppermute(squares, 'tp', [(i, i ^ k) for i in range(8)])  9.33 us
    ppermute x11, waiting for transfers between devices, swap(): return lax.ppermute(value, ('x', 'c'), [(i, i ^ turn) for i in range(4)])  8.27 us
    all_to_all x1, starting transfers between devices, per_device(): lax.all_to_all(after(sent, *far, near), ('x', 'c', 'tp'), split_axis=0, c...  7.52 us
    ppermute x1, waiting for transfers between devices, per_device(): lax.ppermute(every, 'tp', [(i, i ^ 4) for i in range(8)])  7.27 us
    pallas_call x1, Pallas kernels, refit(): pl.pallas_call(refit_kernel, in_specs=[pl.BlockSpec(memory_space=pltpu.SM...  7.09 us
  transfers between devices with their start and end apart: 26, of which 14 were waited for; matrix products, arithmetic and copies ran while one was open for 7% of the time, Pallas kernels for 13%

profile of v2, /device:TPU:0, one launch (start us, length us, event | category | flops | bytes accessed | tf_op | source)
XLA Modules:
  0.0 142.3 jit_solution(2753993608843302807)
XLA Ops:
  1.0 1.7 %collective-permute-start.1 = (bf16[48,4096]{1,0:T(8,128)(2,1)S(1)}, bf16[48,4096]{1,0:T(8,128)(2,1)}, u32[]{:S(2)}, u32[]{:S(2)}) collective-permute-start(bf16[48,4096]{1,0:T(8,128)(2,1)S(1)} %slice_bitcast_fusion.1), channel_id=1, source_target_pairs={{0,64},{8,72},{64,0},{72,8},{1,65},{9,73},{65,1},{73,9},{2,66},{10... | collective-permute-start | bytes 1179656 | tf_op jit(solution)/shard_map/ppermute | solution.py:376
  3.3 1.3 pad_add_fusion.ints
  4.7 7.1 %refit.1 = bf16[32,32,640]{2,1,0:T(8,128)(2,1)} custom-call(s32[141]{0:T(256)} %pad_add_fusion.ints, s32[1,128]{1,0:T(1,128)} %bitcast.47, f32[1,1]{1,0:T(1,128)} %bitcast.32.rate, f32[5,80]{1,0:T(8,128)} %conv_m.1, bf16[5,80]{1,0:T(8,128)(2,1)} %conv_g.1, f32[5,80]{1,0:T(8,128)} %conv_f.1, f32[5,80]{1,0:T(8,128)} %conv_s.1, f32[32,18560]{1,0:T(8,128)} %master.1, ...), custom_call_target="tpu_custom_call" | custom-call | tf_op jit(solution)/shard_map/refit/pallas_call | solution.py:106
  12.7 7.5 %all-to-all-start = ((bf16[32,32,640]{2,1,0:T(8,128)(2,1)}), bf16[32,32,640]{2,1,0:T(8,128)(2,1)}, u32[]{:S(2)}, u32[]{:S(2)}) async-start(bf16[32,32,640]{2,1,0:T(8,128)(2,1)} %refit.1), calls=%async_computation | async-start | bytes 2621440 | tf_op jit(solution)/shard_map/all_to_all | solution.py:391
  21.3 18.5 %all-to-all-done = bf16[32,32,640]{2,1,0:T(8,128)(2,1)} async-done(((bf16[32,32,640]{2,1,0:T(8,128)(2,1)}), bf16[32,32,640]{2,1,0:T(8,128)(2,1)}, u32[]{:S(2)}, u32[]{:S(2)}) %all-to-all-start) | async-done | bytes 1310752 | tf_op jit(solution)/shard_map/all_to_all | solution.py:391
  41.4 4.0 %collective-permute-start.5 = (bf16[1024,128]{1,0:T(8,128)(2,1)S(1)}, bf16[1024,128]{1,0:T(8,128)(2,1)S(1)}, u32[]{:S(2)}, u32[]{:S(2)}) collective-permute-start(bf16[1024,128]{1,0:T(8,128)(2,1)S(1)} %slice.24.refs_6_), channel_id=1, source_target_pairs={{0,32},{16,48},{32,0},{48,16},{1,33},{17,49},{33,1},{49,17},{2,34}... | collective-permute-start | bytes 786440 | tf_op jit(solution)/shard_map/ppermute | solution.py:413
  46.0 1.3 collective-permute-start.3
  48.1 4.5 %collective-permute-done.5.refs_9_ = bf16[1024,128]{1,0:T(8,128)(2,1)S(1)} collective-permute-done((bf16[1024,128]{1,0:T(8,128)(2,1)S(1)}, bf16[1024,128]{1,0:T(8,128)(2,1)S(1)}, u32[]{:S(2)}, u32[]{:S(2)}) %collective-permute-start.5) | collective-permute-done | bytes 262176 | tf_op jit(solution)/shard_map/ppermute | solution.py:413
  53.3 4.2 %collective-permute-done.4.refs_8_ = bf16[1024,128]{1,0:T(8,128)(2,1)S(1)} collective-permute-done((bf16[1024,128]{1,0:T(8,128)(2,1)S(1)}, bf16[1024,128]{1,0:T(8,128)(2,1)S(1)}, u32[]{:S(2)}, u32[]{:S(2)}) %collective-permute-start.4) | collective-permute-done | bytes 262176 | tf_op jit(solution)/shard_map/ppermute | solution.py:373
  60.4 2.0 %collective-permute-start.15 = (bf16[512,512]{1,0:T(8,128)(2,1)S(1)}, bf16[512,512]{1,0:T(8,128)(2,1)}, u32[]{:S(2)}, u32[]{:S(2)}) collective-permute-start(bf16[512,512]{1,0:T(8,128)(2,1)S(1)} %get-tuple-element.47.refs_6_), channel_id=1, source_target_pairs={{0,16},{16,32},{32,48},{48,0},{1,17},{17,33},{33,49},{49,1},{2,18}... | collective-permute-start | bytes 1572872 | tf_op jit(solution)/shard_map/ppermute | solution.py:372
  62.3 2.2 %collective-permute-start.16 = (bf16[512,512]{1,0:T(8,128)(2,1)S(1)}, bf16[512,512]{1,0:T(8,128)(2,1)}, u32[]{:S(2)}, u32[]{:S(2)}) collective-permute-start(bf16[512,512]{1,0:T(8,128)(2,1)S(1)} %get-tuple-element.48.refs_7_), channel_id=1, source_target_pairs={{0,48},{16,0},{32,16},{48,32},{1,49},{17,1},{33,17},{49,33},{2,50}... | collective-permute-start | bytes 1572872 | tf_op jit(solution)/shard_map/ppermute | solution.py:373
  71.3 3.6 %first_product_kernel.1 = (bf16[224,128]{1,0:T(8,128)(2,1)S(1)}, bf16[224,128]{1,0:T(8,128)(2,1)S(1)}, bf16[224,128]{1,0:T(8,128)(2,1)S(1)}, bf16[224,128]{1,0:T(8,128)(2,1)S(1)}) custom-call(s32[4]{0:T(128)S(1)} %pad_add_fusion.1.place, s32[141]{0:T(256)S(1)} %copy-done.12, bf16[144,4096]{1,0:T(8,128)(2,1)S(1)} %bitcast.34, ...), custom_call_target="tpu_custom_call" | custom-call | tf_op jit(solution)/shard_map/first_product_kernel/pallas_call | solution.py:314
  79.4 3.1 %collective-permute-start.18 = (bf16[1024,512]{1,0:T(8,128)(2,1)S(1)}, bf16[1024,512]{1,0:T(8,128)(2,1)S(1)}, u32[]{:S(2)}, u32[]{:S(2)}) collective-permute-start(bf16[1024,512]{1,0:T(8,128)(2,1)S(1)} %pad_maximum_fusion.1), channel_id=1, source_target_pairs={{0,48},{16,0},{32,16},{48,32},{1,49},{17,1},{33,17},{49,33},{2,50}... | collective-permute-start | bytes 3145736 | tf_op jit(solution)/shard_map/ppermute | solution.py:373
  83.2 2.2 %collective-permute-start.13 = (bf16[3,48,256]{2,1,0:T(8,128)(2,1)S(1)}, bf16[3,48,256]{2,1,0:T(8,128)(2,1)S(1)}, u32[]{:S(2)}, u32[]{:S(2)}) collective-permute-start(bf16[3,48,256]{2,1,0:T(8,128)(2,1)S(1)} %get-tuple-element.43), channel_id=1, source_target_pairs={{0,1},{1,2},{2,3},{3,0},{4,5},{5,6},{6,7},{7,4},{8,9},{9,10},{10,1... | collective-permute-start | bytes 221192 | tf_op jit(solution)/shard_map/ppermute | solution.py:432
  85.4 1.5 %collective-permute-start.12 = (bf16[3,48,256]{2,1,0:T(8,128)(2,1)S(1)}, bf16[3,48,256]{2,1,0:T(8,128)(2,1)S(1)}, u32[]{:S(2)}, u32[]{:S(2)}) collective-permute-start(bf16[3,48,256]{2,1,0:T(8,128)(2,1)S(1)} %get-tuple-element.43), channel_id=1, source_target_pairs={{0,2},{1,3},{2,0},{3,1},{4,6},{5,7},{6,4},{7,5},{8,10},{9,11},{10,... | collective-permute-start | bytes 221192 | tf_op jit(solution)/shard_map/ppermute | solution.py:432
  86.8 1.6 %collective-permute-start.11 = (bf16[3,48,256]{2,1,0:T(8,128)(2,1)S(1)}, bf16[3,48,256]{2,1,0:T(8,128)(2,1)S(1)}, u32[]{:S(2)}, u32[]{:S(2)}) collective-permute-start(bf16[3,48,256]{2,1,0:T(8,128)(2,1)S(1)} %get-tuple-element.43), channel_id=1, source_target_pairs={{0,3},{1,0},{2,1},{3,2},{4,7},{5,4},{6,5},{7,6},{8,11},{9,8},{10,9... | collective-permute-start | bytes 221192 | tf_op jit(solution)/shard_map/ppermute | solution.py:432
  89.4 1.9 %collective-permute-done.12 = bf16[3,48,256]{2,1,0:T(8,128)(2,1)S(1)} collective-permute-done((bf16[3,48,256]{2,1,0:T(8,128)(2,1)S(1)}, bf16[3,48,256]{2,1,0:T(8,128)(2,1)S(1)}, u32[]{:S(2)}, u32[]{:S(2)}) %collective-permute-start.12) | collective-permute-done | bytes 73760 | tf_op jit(solution)/shard_map/ppermute | solution.py:432
  91.3 1.7 %collective-permute-start.14 = (bf16[4,3,48,256]{3,2,1,0:T(8,128)(2,1)S(1)}, bf16[4,3,48,256]{3,2,1,0:T(8,128)(2,1)S(1)}, u32[]{:S(2)}, u32[]{:S(2)}) collective-permute-start(bf16[4,3,48,256]{3,2,1,0:T(8,128)(2,1)S(1)} %pad_maximum_fusion.2), channel_id=1, source_target_pairs={{0,4},{1,5},{2,6},{3,7},{4,0},{5,1},{6,2},{7,3},{8,12},{9,13},{10,... | collective-permute-start | bytes 884744 | tf_op jit(solution)/shard_map/ppermute | solution.py:433
  93.0 7.3 %collective-permute-done.14 = bf16[4,3,48,256]{3,2,1,0:T(8,128)(2,1)S(1)} collective-permute-done((bf16[4,3,48,256]{3,2,1,0:T(8,128)(2,1)S(1)}, bf16[4,3,48,256]{3,2,1,0:T(8,128)(2,1)S(1)}, u32[]{:S(2)}, u32[]{:S(2)}) %collective-permute-start.14) | collective-permute-done | bytes 294944 | tf_op jit(solution)/shard_map/ppermute | solution.py:433
  100.7 4.6 %copy-done = bf16[48,16,64,128]{3,2,1,0:T(8,128)(2,1)S(1)} copy-done((bf16[48,16,64,128]{3,2,1,0:T(8,128)(2,1)S(1)}, bf16[48,16,64,128]{3,2,1,0:T(8,128)(2,1)}, u32[]{:S(2)}) %copy-start) | copy-done | bytes 12582936
  105.3 5.7 %read_state.1 = (f32[3,48,1024]{2,1,0:T(8,128)S(1)}, f32[6,48,1024]{2,1,0:T(8,128)S(1)}) custom-call(bf16[48,16,64,128]{3,2,1,0:T(8,128)(2,1)S(1)} %copy-done, f32[8,3,48,256]{3,2,1,0:T(8,128)S(1)} %convert_element_type.3.every, f32[48,24,128]{2,1,0:T(8,128)S(1)} %bitcast.36, f32[8,1024]{1,0:T(8,128)S(1)} %get-tuple-element.45.mask), custom_call_target="tpu_custom_call" | custom-call | tf_op jit(solution)/shard_map/read_state/pallas_call | solution.py:326
  111.0 4.6 %wide_product_kernel.1 = (bf16[144,512]{1,0:T(8,128)(2,1)S(1)}, bf16[144,512]{1,0:T(8,128)(2,1)S(1)}, bf16[144,512]{1,0:T(8,128)(2,1)S(1)}, bf16[144,512]{1,0:T(8,128)(2,1)S(1)}) custom-call(s32[4]{0:T(128)S(1)} %pad_add_fusion.1.place, bf16[144,4096]{1,0:T(8,128)(2,1)S(1)} %bitcast.35, bf16[144,4096]{1,0:T(8,128)(2,1)S(1)} %collective-permute-done.refs_1_, ...), custom_call_target="tpu_custom_call" | custom-call | tf_op jit(solution)/shard_map/wide_product_kernel/pallas_call | solution.py:314
  116.2 1.3 collective-permute-start.21
  117.6 4.9 %collective-permute-done.20.refs_2_ = bf16[144,512]{1,0:T(8,128)(2,1)S(1)} collective-permute-done((bf16[144,512]{1,0:T(8,128)(2,1)S(1)}, bf16[144,512]{1,0:T(8,128)(2,1)S(1)}, u32[]{:S(2)}, u32[]{:S(2)}) %collective-permute-start.20) | collective-permute-done | bytes 147488 | tf_op jit(solution)/shard_map/ppermute | solution.py:376
  122.4 2.2 %collective-permute-done.21.refs_3_ = bf16[144,512]{1,0:T(8,128)(2,1)S(1)} collective-permute-done((bf16[144,512]{1,0:T(8,128)(2,1)S(1)}, bf16[144,512]{1,0:T(8,128)(2,1)S(1)}, u32[]{:S(2)}, u32[]{:S(2)}) %collective-permute-start.21) | collective-permute-done | bytes 147488 | tf_op jit(solution)/shard_map/ppermute | solution.py:376
  124.6 2.2 %scan_kernel.1 = (f32[3,48,1024]{2,1,0:T(8,128)S(1)}, f32[3,8,48]{2,1,0:T(8,128)S(1)}) custom-call(s32[4]{0:T(128)S(1)} %pad_add_fusion.1.place, bf16[144,512]{1,0:T(8,128)(2,1)S(1)} %get-tuple-element.51.refs_0_, bf16[144,512]{1,0:T(8,128)(2,1)S(1)} %collective-permute-done.19.refs_1_, bf16[144,512]{1,0:T(8,128)(2,1)S(1)} %collective-permute-done.20.refs_2_, ...), custom_call_target="tpu_custom_call" | custom-call | tf_op jit(solution)/shard_map/scan_kernel/pallas_call | solution.py:314
  127.8 2.8 %collective-permute-done.22 = f32[3,8,48]{2,1,0:T(8,128)S(1)} collective-permute-done((f32[3,8,48]{2,1,0:T(8,128)S(1)}, f32[3,8,48]{2,1,0:T(8,128)S(1)}, u32[]{:S(2)}, u32[]{:S(2)}) %collective-permute-start.22) | collective-permute-done | bytes 4640 | tf_op jit(solution)/shard_map/ppermute | solution.py:452
  130.6 2.5 %collective-permute-start.23 = (f32[3,8,48]{2,1,0:T(8,128)S(1)}, f32[3,8,48]{2,1,0:T(8,128)S(1)}, u32[]{:S(2)}, u32[]{:S(2)}) collective-permute-start(f32[3,8,48]{2,1,0:T(8,128)S(1)} %add.9), channel_id=1, source_target_pairs={{0,2},{1,3},{2,0},{3,1},{4,6},{5,7},{6,4},{7,5},{8,10},{9,11},{10,... | collective-permute-start | bytes 13832 | tf_op jit(solution)/shard_map/ppermute | solution.py:452
  133.0 2.7 %collective-permute-done.23 = f32[3,8,48]{2,1,0:T(8,128)S(1)} collective-permute-done((f32[3,8,48]{2,1,0:T(8,128)S(1)}, f32[3,8,48]{2,1,0:T(8,128)S(1)}, u32[]{:S(2)}, u32[]{:S(2)}) %collective-permute-start.23) | collective-permute-done | bytes 4640 | tf_op jit(solution)/shard_map/ppermute | solution.py:452
  135.8 1.4 collective-permute-start.24
  137.1 3.8 %collective-permute-done.24 = f32[3,8,48]{2,1,0:T(8,128)S(1)} collective-permute-done((f32[3,8,48]{2,1,0:T(8,128)S(1)}, f32[3,8,48]{2,1,0:T(8,128)S(1)}, u32[]{:S(2)}, u32[]{:S(2)}) %collective-permute-start.24) | collective-permute-done | bytes 4640 | tf_op jit(solution)/shard_map/ppermute | solution.py:452
  141.0 1.4 norm_kernel.1
  (84 shorter events, 24.4 us)
Async XLA Ops:
  0.0 12.7 %collective-permute-start = (bf16[144,4096]{1,0:T(8,128)(2,1)}, bf16[144,4096]{1,0:T(8,128)(2,1)S(1)}, u32[]{:S(2)}, u32[]{:S(2)}) collective-permute-start(bf16[144,4096]{1,0:T(8,128)(2,1)} %bitcast.33), channel_id=1, source_target_pairs={{0,8},{8,0},{64,72},{72,64},{1,9},{9,1},{65,73},{73,65},{2,10},{10... | collective-permute-start | bytes 3538952 | tf_op jit(solution)/shard_map/ppermute | solution.py:376
  1.0 11.7 %collective-permute-start.1 = (bf16[48,4096]{1,0:T(8,128)(2,1)S(1)}, bf16[48,4096]{1,0:T(8,128)(2,1)}, u32[]{:S(2)}, u32[]{:S(2)}) collective-permute-start(bf16[48,4096]{1,0:T(8,128)(2,1)S(1)} %slice_bitcast_fusion.1), channel_id=1, source_target_pairs={{0,64},{8,72},{64,0},{72,8},{1,65},{9,73},{65,1},{73,9},{2,66},{10... | collective-permute-start | bytes 1179656 | tf_op jit(solution)/shard_map/ppermute | solution.py:376
  12.7 27.1 %all-to-all-start = ((bf16[32,32,640]{2,1,0:T(8,128)(2,1)}), bf16[32,32,640]{2,1,0:T(8,128)(2,1)}, u32[]{:S(2)}, u32[]{:S(2)}) async-start(bf16[32,32,640]{2,1,0:T(8,128)(2,1)} %refit.1), calls=%async_computation | async-start | bytes 2621440 | tf_op jit(solution)/shard_map/all_to_all | solution.py:391
  20.3 44.5 %copy-start.16 = (bf16[48,3,2,1,128]{4,2,3,1,0:T(2,128)(2,1)S(1)}, bf16[48,3,2,1,128]{4,2,3,1,0:T(2,128)(2,1)}, u32[]{:S(2)}) copy-start(bf16[48,3,2,1,128]{4,2,3,1,0:T(2,128)(2,1)} %param.35) | copy-start | bytes 221188
  20.3 46.2 %copy-start.11 = (f32[8192]{0:T(1024)S(1)}, f32[8192]{0:T(1024)}, u32[]{:S(2)}) copy-start(f32[8192]{0:T(1024)} %param.39) | copy-start | bytes 98308
  20.3 46.2 %copy-start.12 = (s32[141]{0:T(256)S(1)}, s32[141]{0:T(256)}, u32[]{:S(2)}) copy-start(s32[141]{0:T(256)} %pad_add_fusion.ints) | copy-start | bytes 1696
  20.3 46.2 %copy-start.13 = (f32[128]{0:T(128)S(1)}, f32[128]{0:T(128)}, u32[]{:S(2)}) copy-start(f32[128]{0:T(128)} %param.36) | copy-start | bytes 1540
  20.3 46.2 %copy-start.14 = (f32[128]{0:T(128)S(1)}, f32[128]{0:T(128)}, u32[]{:S(2)}) copy-start(f32[128]{0:T(128)} %param.37) | copy-start | bytes 1540
  20.3 46.2 %copy-start.15 = (f32[128]{0:T(128)S(1)}, f32[128]{0:T(128)}, u32[]{:S(2)}) copy-start(f32[128]{0:T(128)} %param.38) | copy-start | bytes 1540
  39.8 19.3 %collective-permute-start.2 = (bf16[96,4096]{1,0:T(8,128)(2,1)}, bf16[96,4096]{1,0:T(8,128)(2,1)}, u32[]{:S(2)}, u32[]{:S(2)}) collective-permute-start(bf16[96,4096]{1,0:T(8,128)(2,1)} %bitcast.6), channel_id=1, source_target_pairs={{0,64},{8,72},{64,0},{72,8},{1,65},{9,73},{65,1},{73,9},{2,66},{10... | collective-permute-start | bytes 2359304 | tf_op jit(solution)/shard_map/ppermute | solution.py:376
  41.4 11.2 %collective-permute-start.5 = (bf16[1024,128]{1,0:T(8,128)(2,1)S(1)}, bf16[1024,128]{1,0:T(8,128)(2,1)S(1)}, u32[]{:S(2)}, u32[]{:S(2)}) collective-permute-start(bf16[1024,128]{1,0:T(8,128)(2,1)S(1)} %slice.24.refs_6_), channel_id=1, source_target_pairs={{0,32},{16,48},{32,0},{48,16},{1,33},{17,49},{33,1},{49,17},{2,34}... | collective-permute-start | bytes 786440 | tf_op jit(solution)/shard_map/ppermute | solution.py:413
  45.3 12.1 %collective-permute-start.4 = (bf16[1024,128]{1,0:T(8,128)(2,1)S(1)}, bf16[1024,128]{1,0:T(8,128)(2,1)S(1)}, u32[]{:S(2)}, u32[]{:S(2)}) collective-permute-start(bf16[1024,128]{1,0:T(8,128)(2,1)S(1)} %slice.24.refs_6_), channel_id=1, source_target_pairs={{0,48},{16,0},{32,16},{48,32},{1,49},{17,1},{33,17},{49,33},{2,50}... | collective-permute-start | bytes 786440 | tf_op jit(solution)/shard_map/ppermute | solution.py:373
  46.0 12.1 %collective-permute-start.3 = (bf16[1024,128]{1,0:T(8,128)(2,1)S(1)}, bf16[1024,128]{1,0:T(8,128)(2,1)S(1)}, u32[]{:S(2)}, u32[]{:S(2)}) collective-permute-start(bf16[1024,128]{1,0:T(8,128)(2,1)S(1)} %slice.24.refs_6_), channel_id=1, source_target_pairs={{0,16},{16,32},{32,48},{48,0},{1,17},{17,33},{33,49},{49,1},{2,18}... | collective-permute-start | bytes 786440 | tf_op jit(solution)/shard_map/ppermute | solution.py:372
  59.1 8.5 %collective-permute-start.7 = (bf16[96,4096]{1,0:T(8,128)(2,1)}, bf16[96,4096]{1,0:T(8,128)(2,1)}, u32[]{:S(2)}, u32[]{:S(2)}) collective-permute-start(bf16[96,4096]{1,0:T(8,128)(2,1)} %collective-permute-done.2.refs_3_), channel_id=1, source_target_pairs={{0,8},{8,0},{64,72},{72,64},{1,9},{9,1},{65,73},{73,65},{2,10},{10... | collective-permute-start | bytes 2359304 | tf_op jit(solution)/shard_map/ppermute | solution.py:376
  60.4 16.8 %collective-permute-start.15 = (bf16[512,512]{1,0:T(8,128)(2,1)S(1)}, bf16[512,512]{1,0:T(8,128)(2,1)}, u32[]{:S(2)}, u32[]{:S(2)}) collective-permute-start(bf16[512,512]{1,0:T(8,128)(2,1)S(1)} %get-tuple-element.47.refs_6_), channel_id=1, source_target_pairs={{0,16},{16,32},{32,48},{48,0},{1,17},{17,33},{33,49},{49,1},{2,18}... | collective-permute-start | bytes 1572872 | tf_op jit(solution)/shard_map/ppermute | solution.py:372
  62.3 14.8 %collective-permute-start.16 = (bf16[512,512]{1,0:T(8,128)(2,1)S(1)}, bf16[512,512]{1,0:T(8,128)(2,1)}, u32[]{:S(2)}, u32[]{:S(2)}) collective-permute-start(bf16[512,512]{1,0:T(8,128)(2,1)S(1)} %get-tuple-element.48.refs_7_), channel_id=1, source_target_pairs={{0,48},{16,0},{32,16},{48,32},{1,49},{17,1},{33,17},{49,33},{2,50}... | collective-permute-start | bytes 1572872 | tf_op jit(solution)/shard_map/ppermute | solution.py:373
  64.5 3.0 %collective-permute-start.6 = (bf16[48,4096]{1,0:T(8,128)(2,1)}, bf16[48,4096]{1,0:T(8,128)(2,1)}, u32[]{:S(2)}, u32[]{:S(2)}) collective-permute-start(bf16[48,4096]{1,0:T(8,128)(2,1)} %collective-permute-done.1.refs_2_), channel_id=1, source_target_pairs={{0,8},{8,0},{64,72},{72,64},{1,9},{9,1},{65,73},{73,65},{2,10},{10... | collective-permute-start | bytes 1179656 | tf_op jit(solution)/shard_map/ppermute | solution.py:376
  75.0 7.5 %collective-permute-start.8 = (bf16[224,128]{1,0:T(8,128)(2,1)S(1)}, bf16[224,128]{1,0:T(8,128)(2,1)S(1)}, u32[]{:S(2)}, u32[]{:S(2)}) collective-permute-start(bf16[224,128]{1,0:T(8,128)(2,1)S(1)} %get-tuple-element.40), channel_id=1, source_target_pairs={{0,8},{8,0},{64,72},{72,64},{1,9},{9,1},{65,73},{73,65},{2,10},{10... | collective-permute-start | bytes 172040 | tf_op jit(solution)/shard_map/ppermute | solution.py:376
  75.3 7.2 %collective-permute-start.9 = (bf16[224,128]{1,0:T(8,128)(2,1)S(1)}, bf16[224,128]{1,0:T(8,128)(2,1)S(1)}, u32[]{:S(2)}, u32[]{:S(2)}) collective-permute-start(bf16[224,128]{1,0:T(8,128)(2,1)S(1)} %get-tuple-element.41), channel_id=1, source_target_pairs={{0,64},{8,72},{64,0},{72,8},{1,65},{9,73},{65,1},{73,9},{2,66},{10... | collective-permute-start | bytes 172040 | tf_op jit(solution)/shard_map/ppermute | solution.py:376
  75.9 6.6 %collective-permute-start.10 = (bf16[224,128]{1,0:T(8,128)(2,1)S(1)}, bf16[224,128]{1,0:T(8,128)(2,1)S(1)}, u32[]{:S(2)}, u32[]{:S(2)}) collective-permute-start(bf16[224,128]{1,0:T(8,128)(2,1)S(1)} %get-tuple-element.42), channel_id=1, source_target_pairs={{0,72},{8,64},{64,8},{72,0},{1,73},{9,65},{65,9},{73,1},{2,74},{10... | collective-permute-start | bytes 172040 | tf_op jit(solution)/shard_map/ppermute | solution.py:376
  79.4 31.6 %collective-permute-start.18 = (bf16[1024,512]{1,0:T(8,128)(2,1)S(1)}, bf16[1024,512]{1,0:T(8,128)(2,1)S(1)}, u32[]{:S(2)}, u32[]{:S(2)}) collective-permute-start(bf16[1024,512]{1,0:T(8,128)(2,1)S(1)} %pad_maximum_fusion.1), channel_id=1, source_target_pairs={{0,48},{16,0},{32,16},{48,32},{1,49},{17,1},{33,17},{49,33},{2,50}... | collective-permute-start | bytes 3145736 | tf_op jit(solution)/shard_map/ppermute | solution.py:373
  82.5 28.5 %collective-permute-start.17 = (bf16[1024,512]{1,0:T(8,128)(2,1)S(1)}, bf16[1024,512]{1,0:T(8,128)(2,1)S(1)}, u32[]{:S(2)}, u32[]{:S(2)}) collective-permute-start(bf16[1024,512]{1,0:T(8,128)(2,1)S(1)} %pad_maximum_fusion), channel_id=1, source_target_pairs={{0,16},{16,32},{32,48},{48,0},{1,17},{17,33},{33,49},{49,1},{2,18}... | collective-permute-start | bytes 3145736 | tf_op jit(solution)/shard_map/ppermute | solution.py:372
  83.2 6.2 %collective-permute-start.13 = (bf16[3,48,256]{2,1,0:T(8,128)(2,1)S(1)}, bf16[3,48,256]{2,1,0:T(8,128)(2,1)S(1)}, u32[]{:S(2)}, u32[]{:S(2)}) collective-permute-start(bf16[3,48,256]{2,1,0:T(8,128)(2,1)S(1)} %get-tuple-element.43), channel_id=1, source_target_pairs={{0,1},{1,2},{2,3},{3,0},{4,5},{5,6},{6,7},{7,4},{8,9},{9,10},{10,1... | collective-permute-start | bytes 221192 | tf_op jit(solution)/shard_map/ppermute | solution.py:432
  85.4 5.9 %collective-permute-start.12 = (bf16[3,48,256]{2,1,0:T(8,128)(2,1)S(1)}, bf16[3,48,256]{2,1,0:T(8,128)(2,1)S(1)}, u32[]{:S(2)}, u32[]{:S(2)}) collective-permute-start(bf16[3,48,256]{2,1,0:T(8,128)(2,1)S(1)} %get-tuple-element.43), channel_id=1, source_target_pairs={{0,2},{1,3},{2,0},{3,1},{4,6},{5,7},{6,4},{7,5},{8,10},{9,11},{10,... | collective-permute-start | bytes 221192 | tf_op jit(solution)/shard_map/ppermute | solution.py:432
  86.8 4.4 %collective-permute-start.11 = (bf16[3,48,256]{2,1,0:T(8,128)(2,1)S(1)}, bf16[3,48,256]{2,1,0:T(8,128)(2,1)S(1)}, u32[]{:S(2)}, u32[]{:S(2)}) collective-permute-start(bf16[3,48,256]{2,1,0:T(8,128)(2,1)S(1)} %get-tuple-element.43), channel_id=1, source_target_pairs={{0,3},{1,0},{2,1},{3,2},{4,7},{5,4},{6,5},{7,6},{8,11},{9,8},{10,9... | collective-permute-start | bytes 221192 | tf_op jit(solution)/shard_map/ppermute | solution.py:432
  91.3 9.0 %collective-permute-start.14 = (bf16[4,3,48,256]{3,2,1,0:T(8,128)(2,1)S(1)}, bf16[4,3,48,256]{3,2,1,0:T(8,128)(2,1)S(1)}, u32[]{:S(2)}, u32[]{:S(2)}) collective-permute-start(bf16[4,3,48,256]{3,2,1,0:T(8,128)(2,1)S(1)} %pad_maximum_fusion.2), channel_id=1, source_target_pairs={{0,4},{1,5},{2,6},{3,7},{4,0},{5,1},{6,2},{7,3},{8,12},{9,13},{10,... | collective-permute-start | bytes 884744 | tf_op jit(solution)/shard_map/ppermute | solution.py:433
  115.6 2.0 %collective-permute-start.19 = (bf16[144,512]{1,0:T(8,128)(2,1)S(1)}, bf16[144,512]{1,0:T(8,128)(2,1)S(1)}, u32[]{:S(2)}, u32[]{:S(2)}) collective-permute-start(bf16[144,512]{1,0:T(8,128)(2,1)S(1)} %get-tuple-element.52), channel_id=1, source_target_pairs={{0,8},{8,0},{64,72},{72,64},{1,9},{9,1},{65,73},{73,65},{2,10},{10... | collective-permute-start | bytes 442376 | tf_op jit(solution)/shard_map/ppermute | solution.py:376
  115.7 6.7 %collective-permute-start.20 = (bf16[144,512]{1,0:T(8,128)(2,1)S(1)}, bf16[144,512]{1,0:T(8,128)(2,1)S(1)}, u32[]{:S(2)}, u32[]{:S(2)}) collective-permute-start(bf16[144,512]{1,0:T(8,128)(2,1)S(1)} %get-tuple-element.53), channel_id=1, source_target_pairs={{0,64},{8,72},{64,0},{72,8},{1,65},{9,73},{65,1},{73,9},{2,66},{10... | collective-permute-start | bytes 442376 | tf_op jit(solution)/shard_map/ppermute | solution.py:376
  116.2 8.4 %collective-permute-start.21 = (bf16[144,512]{1,0:T(8,128)(2,1)S(1)}, bf16[144,512]{1,0:T(8,128)(2,1)S(1)}, u32[]{:S(2)}, u32[]{:S(2)}) collective-permute-start(bf16[144,512]{1,0:T(8,128)(2,1)S(1)} %get-tuple-element.54), channel_id=1, source_target_pairs={{0,72},{8,64},{64,8},{72,0},{1,73},{9,65},{65,9},{73,1},{2,74},{10... | collective-permute-start | bytes 442376 | tf_op jit(solution)/shard_map/ppermute | solution.py:376
  126.8 3.7 %collective-permute-start.22 = (f32[3,8,48]{2,1,0:T(8,128)S(1)}, f32[3,8,48]{2,1,0:T(8,128)S(1)}, u32[]{:S(2)}, u32[]{:S(2)}) collective-permute-start(f32[3,8,48]{2,1,0:T(8,128)S(1)} %get-tuple-element.62), channel_id=1, source_target_pairs={{0,1},{1,0},{2,3},{3,2},{4,5},{5,4},{6,7},{7,6},{8,9},{9,8},{10,11... | collective-permute-start | bytes 13832 | tf_op jit(solution)/shard_map/ppermute | solution.py:452
  130.6 5.2 %collective-permute-start.23 = (f32[3,8,48]{2,1,0:T(8,128)S(1)}, f32[3,8,48]{2,1,0:T(8,128)S(1)}, u32[]{:S(2)}, u32[]{:S(2)}) collective-permute-start(f32[3,8,48]{2,1,0:T(8,128)S(1)} %add.9), channel_id=1, source_target_pairs={{0,2},{1,3},{2,0},{3,1},{4,6},{5,7},{6,4},{7,5},{8,10},{9,11},{10,... | collective-permute-start | bytes 13832 | tf_op jit(solution)/shard_map/ppermute | solution.py:452
  135.8 5.2 %collective-permute-start.24 = (f32[3,8,48]{2,1,0:T(8,128)S(1)}, f32[3,8,48]{2,1,0:T(8,128)S(1)}, u32[]{:S(2)}, u32[]{:S(2)}) collective-permute-start(f32[3,8,48]{2,1,0:T(8,128)S(1)} %add.10), channel_id=1, source_target_pairs={{0,4},{1,5},{2,6},{3,7},{4,0},{5,1},{6,2},{7,3},{8,12},{9,13},{10,... | collective-permute-start | bytes 13832 | tf_op jit(solution)/shard_map/ppermute | solution.py:452
  (11 other events, 33.4 us)

commit v3 on v2

--- a/solution.py
+++ b/solution.py
@@ -268,7 +268,9 @@
 
 
 def scan_kernel(place, *refs):
-    pieces, (stored, taps, read, pair, dt, spread, params, member, gated, squares, buffer) = refs[:4], refs[4:]
+    pieces, (stored, taps, *refs) = refs[:4], refs[4:]
+    read, read_more, pair, pair_more, dt, spread, params, member, gated, squares, buffer = refs
+    whole = lambda low, high, n: jnp.concatenate([low[n], high[n]], axis=0)
     both = gathered(place, pieces, buffer)
     inputs = [value[:, :SPAN] for value in both]
     values = [v.astype(jnp.float32) for v in convolve(inputs, stored, taps[...])]
@@ -287,28 +289,34 @@
         offset = n + t
         after = None
         for s in range(t, -1, -1):
-            term = pair[offset] * driven[s]
+            term = whole(pair, pair_more, offset) * driven[s]
             total = total + (term if after is None else after * term)
             after = keeps[s] if after is None else after * keeps[s]
             offset -= 1
-        value = (total + after * read[t]) * silu(both[t][:, SPAN:])
-        gated[t] = value
-        squares[t] = lax.dot_general(
+        value = (total + after * whole(read, read_more, t)) * silu(both[t][:, SPAN:])
+        gated[t] = value * params[3:4]
+        total = lax.dot_general(
             member[...], value * value, (((1,), (1,)), ((), ())), precision=HIGH, preferred_element_type=jnp.float32
         )
+        total = jnp.concatenate([total, jnp.zeros((GROUPS, 128 - ROWS), jnp.float32)], axis=1)
+        for to in range(8):
+            squares[to, 8 * t : 8 * t + 8, :] = total
         n += t + 1
 
 
-def norm_kernel(gated, squares, member, params, out):
+def norm_kernel(gated, squares, member, out):
     for t in range(STEPS):
-        scale = lax.rsqrt(squares[t] / SPAN + norm_eps)
+        total = squares[0, 8 * t : 8 * t + 8, 0:ROWS]
+        for owner in range(1, 8):
+            total = total + squares[owner, 8 * t : 8 * t + 8, 0:ROWS]
+        scale = lax.rsqrt(total / SPAN + norm_eps)
         lanes = lax.dot_general(
             scale, member[...], (((0,), (0,)), ((), ())), precision=HIGH, preferred_element_type=jnp.float32
         )
-        out[t] = (gated[t] * lanes * params[3:4]).astype(jnp.bfloat16)
-
-
-def call(kernel, shapes, *args, scalars=0, scratch=()):
+        out[t] = (gated[t] * lanes).astype(jnp.bfloat16)
+
+
+def call(kernel, shapes, *args, scalars=0, scratch=(), limit=12):
     vmem = pl.BlockSpec(memory_space=pltpu.VMEM)
     smem = pl.BlockSpec(memory_space=pltpu.SMEM)
     return pl.pallas_call(
@@ -317,19 +325,19 @@
         out_specs=[vmem] * len(shapes),
         out_shape=[jax.ShapeDtypeStruct(s, d) for s, d in shapes],
         scratch_shapes=scratch,
-        compiler_params=pltpu.CompilerParams(vmem_limit_bytes=32 * 2**20),
+        compiler_params=pltpu.CompilerParams(vmem_limit_bytes=limit * 2**20),
         name=kernel.__name__,
     )(*args)
 
 
-def read_state(state, every, c_all, mask):
+def read_state(state, every, c_all, mask, part):
     return pl.pallas_call(
         state_kernel,
-        grid=(ROWS // 8,),
+        grid=(ROWS // 16,),
         in_specs=[
-            pl.BlockSpec((8, OWN_HEADS, HEAD_DIM, STATE), lambda i: (i, 0, 0, 0)),
-            pl.BlockSpec((GROUPS, STEPS, 8, 2 * STATE), lambda i: (0, 0, i, 0)),
-            pl.BlockSpec((8, 24, STATE), lambda i: (i, 0, 0)),
+            pl.BlockSpec((8, OWN_HEADS, HEAD_DIM, STATE), lambda i: (i + 3 * part, 0, 0, 0)),
+            pl.BlockSpec((GROUPS, STEPS, 8, 2 * STATE), lambda i: (0, 0, i + 3 * part, 0)),
+            pl.BlockSpec((8, 24, STATE), lambda i: (i + 3 * part, 0, 0)),
             pl.BlockSpec((8, SPAN), lambda i: (0, 0)),
         ],
         out_specs=[
@@ -337,10 +345,10 @@
             pl.BlockSpec((6, 8, SPAN), lambda i: (0, i, 0)),
         ],
         out_shape=[
-            jax.ShapeDtypeStruct((3, ROWS, SPAN), jnp.float32),
-            jax.ShapeDtypeStruct((6, ROWS, SPAN), jnp.float32),
+            jax.ShapeDtypeStruct((3, ROWS // 2, SPAN), jnp.float32),
+            jax.ShapeDtypeStruct((6, ROWS // 2, SPAN), jnp.float32),
         ],
-        compiler_params=pltpu.CompilerParams(vmem_limit_bytes=20 * 2**20),
+        compiler_params=pltpu.CompilerParams(vmem_limit_bytes=50 * 2**20),
         name="read_state",
     )(state, every, c_all, mask)
 
@@ -418,7 +426,7 @@
 
     first = call(
         first_product_kernel, [((FLAT + 80, 128), jnp.bfloat16)] * 4, position, ints, *rows, *pieces,
-        scalars=2, scratch=[pltpu.VMEM((1024, 128), jnp.float32)],
+        scalars=2, scratch=[pltpu.VMEM((1024, 128), jnp.float32)], limit=20,
     )
     arrived = after((left_top, right_bottom), first)
     from_left = up(jnp.concatenate([bottom, arrived[0]]))
@@ -433,25 +441,26 @@
     every = jnp.concatenate([every, lax.ppermute(every, "tp", [(i, i ^ 4) for i in range(8)])])
     every = every.astype(jnp.float32)
     c_all = every[..., STATE:].transpose(2, 1, 0, 3).reshape(ROWS, STEPS * GROUPS, STATE)
-    read, pair = read_state(scan_state, every, c_all, mask)
-
-    second = exchanged(
-        call(
-            wide_product_kernel, [((FLAT, 512), jnp.bfloat16)] * 4, position, *rows,
-            after(top, read), bottom, left_top, right_bottom, from_left, from_right,
-            scalars=1,
-        )
-    )
+    read, pair = read_state(scan_state, every, c_all, mask, 0)
+
+    top, read = lax.optimization_barrier((top, read))
+    second = call(
+        wide_product_kernel, [((FLAT, 512), jnp.bfloat16)] * 4, position, *rows,
+        top, bottom, left_top, right_bottom, from_left, from_right,
+        scalars=1, limit=24,
+    )
+    c_all, *second = lax.optimization_barrier((c_all, *second))
+    read_more, pair_more = read_state(scan_state, every, c_all, mask, 1)
+    second = exchanged(second)
     gated, squares = call(
         scan_kernel,
-        [((STEPS, ROWS, SPAN), jnp.float32), ((STEPS, GROUPS, ROWS), jnp.float32)],
-        position, *second, stored_heads, head_taps, read, pair, dt, spread, params, member,
-        scalars=1, scratch=[pltpu.VMEM((FLAT, 2 * SPAN), jnp.bfloat16)],
-    )
-    for k in (1, 2, 4):
-        squares = squares + lax.ppermute(squares, "tp", [(i, i ^ k) for i in range(8)])
+        [((STEPS, ROWS, SPAN), jnp.float32), ((8, STEPS * GROUPS, 128), jnp.float32)],
+        position, *second, stored_heads, head_taps, read, read_more, pair, pair_more, dt, spread, params, member,
+        scalars=1, scratch=[pltpu.VMEM((FLAT, 2 * SPAN), jnp.bfloat16)], limit=20,
+    )
+    squares = lax.all_to_all(squares, "tp", split_axis=0, concat_axis=0, tiled=True)
     (mixer_out,) = call(
-        norm_kernel, [((STEPS, ROWS, SPAN), jnp.bfloat16)], gated, squares, member, params
+        norm_kernel, [((STEPS, ROWS, SPAN), jnp.bfloat16)], gated, squares, member
     )
     return mixer_out
 

time: 143 us -> 139 us (0.972)
  blocking collectives: 0 us -> 12.1 us
  waiting for transfers between devices: 55.2 us -> 46.1 us
  starting transfers between devices: 38.8 us -> 31.6 us
  local copies, waits for them, and re-layouts: 17.3 us -> 12.8 us
  Pallas kernels: 26.2 us -> 30.6 us
    all_to_all x0 -> x1, blocking collectives: none -> 12.1 us  [per_device(): lax.all_to_all(squares, 'tp', split_axis=0, concat_axis=0, tiled=True)]
    ppermute x3 -> x0, waiting for transfers between devices: 9.33 us -> none  [per_device(): lax.ppermute(squares, 'tp', [(i, i ^ k) for i in range(8)])]
    ppermute x3, waiting for transfers between devices: 0.29 us -> 6.65 us  [per_device(): lax.ppermute(value, 'z', [(i, (i + 1) % 4) for i in range(4)])]
    ppermute x11, waiting for transfers between devices: 8.27 us -> 3.37 us  [swap(): return lax.ppermute(value, ('x', 'c'), [(i, i ^ turn) for i in range(4)])]
    ppermute x3 -> x0, starting transfers between devices: 4.79 us -> none  [per_device(): lax.ppermute(squares, 'tp', [(i, i ^ k) for i in range(8)])]
    unnamed x39 -> x37, local copies, waits for them, and re-layouts: 11.9 us -> 7.39 us
    pallas_call x1 -> x2, Pallas kernels: 5.71 us -> 10.1 us  [read_state(): pl.pallas_call(state_kernel, grid=(ROWS // 16,), in_specs=[pl.BlockSpec((...]
    ppermute x1, waiting for transfers between devices: 4.49 us -> 1.08 us  [per_device(): lax.ppermute(own, 'z', [(i, (i + 2) % 4) for i in range(4)])]
  transfers between devices with their start and end apart: 26 -> 23, of which waited for: 14 -> 13; matrix products, arithmetic and copies ran while one was open for 7% -> 7% of each run, Pallas kernels for 13% -> 16%
where the time goes in v3:
time: 139 us; the launch traced here: 138 us
  waiting for transfers between devices  46.1 us (33%)
  starting transfers between devices  31.6 us (23%)
  Pallas kernels  30.6 us (22%)
  local copies, waits for them, and re-layouts  12.8 us (9%)
  blocking collectives  12.1 us (9%)
  other arithmetic  3.81 us (3%)
    all_to_all x1, waiting for transfers between devices, per_device(): lax.all_to_all(after(sent, *far, near), ('x', 'c', 'tp'), split_axis=0, c...  18.5 us
    pallas_call x6, Pallas kernels, call(): pl.pallas_call(kernel, in_specs=[smem] * scalars + [vmem] * (len(args) -...  13.4 us
    all_to_all x1, blocking collectives, per_device(): lax.all_to_all(squares, 'tp', split_axis=0, concat_axis=0, tiled=True)  12.1 us
    pallas_call x2, Pallas kernels, read_state(): pl.pallas_call(state_kernel, grid=(ROWS // 16,), in_specs=[pl.BlockSpec((...  10.1 us
    all_to_all x1, starting transfers between devices, per_device(): lax.all_to_all(after(sent, *far, near), ('x', 'c', 'tp'), split_axis=0, c...  7.52 us
    unnamed x37, local copies, waits for them, and re-layouts  7.39 us
    ppermute x1, waiting for transfers between devices, per_device(): lax.ppermute(every, 'tp', [(i, i ^ 4) for i in range(8)])  7.31 us
    pallas_call x1, Pallas kernels, refit(): pl.pallas_call(refit_kernel, in_specs=[pl.BlockSpec(memory_space=pltpu.SM...  7.09 us
  transfers between devices with their start and end apart: 23, of which 13 were waited for; matrix products, arithmetic and copies ran while one was open for 7% of the time, Pallas kernels for 16%

profile of v3, /device:TPU:0, one launch (start us, length us, event | category | flops | bytes accessed | tf_op | source)
XLA Modules:
  0.0 138.0 jit_solution(15329584141333282310)
XLA Ops:
  1.0 1.7 %collective-permute-start.1 = (bf16[48,4096]{1,0:T(8,128)(2,1)S(1)}, bf16[48,4096]{1,0:T(8,128)(2,1)}, u32[]{:S(2)}, u32[]{:S(2)}) collective-permute-start(bf16[48,4096]{1,0:T(8,128)(2,1)S(1)} %slice_bitcast_fusion.1), channel_id=1, source_target_pairs={{0,64},{8,72},{64,0},{72,8},{1,65},{9,73},{65,1},{73,9},{2,66},{10... | collective-permute-start | bytes 1179656 | tf_op jit(solution)/shard_map/ppermute | solution.py:384
  3.3 1.3 pad_add_fusion.ints
  4.7 7.1 %refit.1 = bf16[32,32,640]{2,1,0:T(8,128)(2,1)} custom-call(s32[141]{0:T(256)} %pad_add_fusion.ints, s32[1,128]{1,0:T(1,128)} %bitcast.48, f32[1,1]{1,0:T(1,128)} %bitcast.32.rate, f32[5,80]{1,0:T(8,128)} %conv_m.1, bf16[5,80]{1,0:T(8,128)(2,1)} %conv_g.1, f32[5,80]{1,0:T(8,128)} %conv_f.1, f32[5,80]{1,0:T(8,128)} %conv_s.1, f32[32,18560]{1,0:T(8,128)} %master.1, ...), custom_call_target="tpu_custom_call" | custom-call | tf_op jit(solution)/shard_map/refit/pallas_call | solution.py:106
  12.7 7.5 %all-to-all-start = ((bf16[32,32,640]{2,1,0:T(8,128)(2,1)}), bf16[32,32,640]{2,1,0:T(8,128)(2,1)}, u32[]{:S(2)}, u32[]{:S(2)}) async-start(bf16[32,32,640]{2,1,0:T(8,128)(2,1)} %refit.1), calls=%async_computation | async-start | bytes 2621440 | tf_op jit(solution)/shard_map/all_to_all | solution.py:399
  21.3 18.5 %all-to-all-done = bf16[32,32,640]{2,1,0:T(8,128)(2,1)} async-done(((bf16[32,32,640]{2,1,0:T(8,128)(2,1)}), bf16[32,32,640]{2,1,0:T(8,128)(2,1)}, u32[]{:S(2)}, u32[]{:S(2)}) %all-to-all-start) | async-done | bytes 1310752 | tf_op jit(solution)/shard_map/all_to_all | solution.py:399
  41.4 2.0 %collective-permute-start.3 = (bf16[1024,128]{1,0:T(8,128)(2,1)S(1)}, bf16[1024,128]{1,0:T(8,128)(2,1)S(1)}, u32[]{:S(2)}, u32[]{:S(2)}) collective-permute-start(bf16[1024,128]{1,0:T(8,128)(2,1)S(1)} %slice.24.refs_6_), channel_id=1, source_target_pairs={{0,16},{16,32},{32,48},{48,0},{1,17},{17,33},{33,49},{49,1},{2,18}... | collective-permute-start | bytes 786440 | tf_op jit(solution)/shard_map/ppermute | solution.py:380
  43.4 2.2 %collective-permute-start.4 = (bf16[1024,128]{1,0:T(8,128)(2,1)S(1)}, bf16[1024,128]{1,0:T(8,128)(2,1)S(1)}, u32[]{:S(2)}, u32[]{:S(2)}) collective-permute-start(bf16[1024,128]{1,0:T(8,128)(2,1)S(1)} %slice.24.refs_6_), channel_id=1, source_target_pairs={{0,48},{16,0},{32,16},{48,32},{1,49},{17,1},{33,17},{49,33},{2,50}... | collective-permute-start | bytes 786440 | tf_op jit(solution)/shard_map/ppermute | solution.py:381
  45.6 1.8 %collective-permute-start.5 = (bf16[1024,128]{1,0:T(8,128)(2,1)S(1)}, bf16[1024,128]{1,0:T(8,128)(2,1)S(1)}, u32[]{:S(2)}, u32[]{:S(2)}) collective-permute-start(bf16[1024,128]{1,0:T(8,128)(2,1)S(1)} %slice.24.refs_6_), channel_id=1, source_target_pairs={{0,32},{16,48},{32,0},{48,16},{1,33},{17,49},{33,1},{49,17},{2,34}... | collective-permute-start | bytes 786440 | tf_op jit(solution)/shard_map/ppermute | solution.py:421
  48.0 3.8 %collective-permute-done.3.refs_7_ = bf16[1024,128]{1,0:T(8,128)(2,1)S(1)} collective-permute-done((bf16[1024,128]{1,0:T(8,128)(2,1)S(1)}, bf16[1024,128]{1,0:T(8,128)(2,1)S(1)}, u32[]{:S(2)}, u32[]{:S(2)}) %collective-permute-start.3) | collective-permute-done | bytes 262176 | tf_op jit(solution)/shard_map/ppermute | solution.py:380
  52.5 3.7 %collective-permute-done.4.refs_8_ = bf16[1024,128]{1,0:T(8,128)(2,1)S(1)} collective-permute-done((bf16[1024,128]{1,0:T(8,128)(2,1)S(1)}, bf16[1024,128]{1,0:T(8,128)(2,1)S(1)}, u32[]{:S(2)}, u32[]{:S(2)}) %collective-permute-start.4) | collective-permute-done | bytes 262176 | tf_op jit(solution)/shard_map/ppermute | solution.py:381
  56.9 1.1 collective-permute-done.5.refs_9_
  59.1 1.3 fusion
  60.4 4.1 %collective-permute-start.16 = (bf16[512,512]{1,0:T(8,128)(2,1)S(1)}, bf16[512,512]{1,0:T(8,128)(2,1)}, u32[]{:S(2)}, u32[]{:S(2)}) collective-permute-start(bf16[512,512]{1,0:T(8,128)(2,1)S(1)} %get-tuple-element.56.refs_7_), channel_id=1, source_target_pairs={{0,48},{16,0},{32,16},{48,32},{1,49},{17,1},{33,17},{49,33},{2,50}... | collective-permute-start | bytes 1572872 | tf_op jit(solution)/shard_map/ppermute | solution.py:381
  71.3 3.7 %first_product_kernel.1 = (bf16[224,128]{1,0:T(8,128)(2,1)S(1)}, bf16[224,128]{1,0:T(8,128)(2,1)S(1)}, bf16[224,128]{1,0:T(8,128)(2,1)S(1)}, bf16[224,128]{1,0:T(8,128)(2,1)S(1)}) custom-call(s32[4]{0:T(128)S(1)} %pad_add_fusion.1.place, s32[141]{0:T(256)S(1)} %copy-done.11, bf16[144,4096]{1,0:T(8,128)(2,1)S(1)} %bitcast.34, ...), custom_call_target="tpu_custom_call" | custom-call | tf_op jit(solution)/shard_map/first_product_kernel/pallas_call | solution.py:322
  75.7 1.4 %collective-permute-start.9 = (bf16[224,128]{1,0:T(8,128)(2,1)S(1)}, bf16[224,128]{1,0:T(8,128)(2,1)S(1)}, u32[]{:S(2)}, u32[]{:S(2)}) collective-permute-start(bf16[224,128]{1,0:T(8,128)(2,1)S(1)} %get-tuple-element.48), channel_id=1, source_target_pairs={{0,64},{8,72},{64,0},{72,8},{1,65},{9,73},{65,1},{73,9},{2,66},{10... | collective-permute-start | bytes 172040 | tf_op jit(solution)/shard_map/ppermute | solution.py:384
  77.1 2.7 %collective-permute-done.15.refs_8_ = bf16[512,512]{1,0:T(8,128)(2,1)} collective-permute-done((bf16[512,512]{1,0:T(8,128)(2,1)S(1)}, bf16[512,512]{1,0:T(8,128)(2,1)}, u32[]{:S(2)}, u32[]{:S(2)}) %collective-permute-start.15) | collective-permute-done | bytes 524320 | tf_op jit(solution)/shard_map/ppermute | solution.py:380
  79.8 1.1 pad_maximum_fusion.1
  81.3 1.1 pad_maximum_fusion
  82.4 1.8 %collective-permute-start.17 = (bf16[1024,512]{1,0:T(8,128)(2,1)S(1)}, bf16[1024,512]{1,0:T(8,128)(2,1)S(1)}, u32[]{:S(2)}, u32[]{:S(2)}) collective-permute-start(bf16[1024,512]{1,0:T(8,128)(2,1)S(1)} %pad_maximum_fusion), channel_id=1, source_target_pairs={{0,16},{16,32},{32,48},{48,0},{1,17},{17,33},{33,49},{49,1},{2,18}... | collective-permute-start | bytes 3145736 | tf_op jit(solution)/shard_map/ppermute | solution.py:380
  84.9 2.2 %collective-permute-start.11 = (bf16[3,48,256]{2,1,0:T(8,128)(2,1)S(1)}, bf16[3,48,256]{2,1,0:T(8,128)(2,1)S(1)}, u32[]{:S(2)}, u32[]{:S(2)}) collective-permute-start(bf16[3,48,256]{2,1,0:T(8,128)(2,1)S(1)} %get-tuple-element.50), channel_id=1, source_target_pairs={{0,3},{1,0},{2,1},{3,2},{4,7},{5,4},{6,5},{7,6},{8,11},{9,8},{10,9... | collective-permute-start | bytes 221192 | tf_op jit(solution)/shard_map/ppermute | solution.py:440
  87.1 2.1 %collective-permute-start.12 = (bf16[3,48,256]{2,1,0:T(8,128)(2,1)S(1)}, bf16[3,48,256]{2,1,0:T(8,128)(2,1)S(1)}, u32[]{:S(2)}, u32[]{:S(2)}) collective-permute-start(bf16[3,48,256]{2,1,0:T(8,128)(2,1)S(1)} %get-tuple-element.50), channel_id=1, source_target_pairs={{0,2},{1,3},{2,0},{3,1},{4,6},{5,7},{6,4},{7,5},{8,10},{9,11},{10,... | collective-permute-start | bytes 221192 | tf_op jit(solution)/shard_map/ppermute | solution.py:440
  89.6 3.3 %collective-permute-done.12 = bf16[3,48,256]{2,1,0:T(8,128)(2,1)S(1)} collective-permute-done((bf16[3,48,256]{2,1,0:T(8,128)(2,1)S(1)}, bf16[3,48,256]{2,1,0:T(8,128)(2,1)S(1)}, u32[]{:S(2)}, u32[]{:S(2)}) %collective-permute-start.12) | collective-permute-done | bytes 73760 | tf_op jit(solution)/shard_map/ppermute | solution.py:440
  92.9 1.8 %collective-permute-done.13 = bf16[3,48,256]{2,1,0:T(8,128)(2,1)S(1)} collective-permute-done((bf16[3,48,256]{2,1,0:T(8,128)(2,1)S(1)}, bf16[3,48,256]{2,1,0:T(8,128)(2,1)S(1)}, u32[]{:S(2)}, u32[]{:S(2)}) %collective-permute-start.13) | collective-permute-done | bytes 73760 | tf_op jit(solution)/shard_map/ppermute | solution.py:440
  95.8 7.3 %collective-permute-done.14 = bf16[4,3,48,256]{3,2,1,0:T(8,128)(2,1)S(1)} collective-permute-done((bf16[4,3,48,256]{3,2,1,0:T(8,128)(2,1)S(1)}, bf16[4,3,48,256]{3,2,1,0:T(8,128)(2,1)S(1)}, u32[]{:S(2)}, u32[]{:S(2)}) %collective-permute-start.14) | collective-permute-done | bytes 294944 | tf_op jit(solution)/shard_map/ppermute | solution.py:441
  103.5 5.0 %read_state.2 = (f32[3,24,1024]{2,1,0:T(8,128)S(1)}, f32[6,24,1024]{2,1,0:T(8,128)S(1)}) custom-call(bf16[48,16,64,128]{3,2,1,0:T(8,128)(2,1)} %state.3, f32[8,3,48,256]{3,2,1,0:T(8,128)S(1)} %convert_element_type.3.every, f32[48,24,128]{2,1,0:T(8,128)S(1)} %bitcast.36, f32[8,1024]{1,0:T(8,128)S(1)} %get-tuple-element.53.mask), custom_call_target="tpu_custom_call" | custom-call | tf_op jit(solution)/shard_map/read_state/pallas_call | solution.py:334
  108.7 4.5 %wide_product_kernel.1 = (bf16[144,512]{1,0:T(8,128)(2,1)S(1)}, bf16[144,512]{1,0:T(8,128)(2,1)S(1)}, bf16[144,512]{1,0:T(8,128)(2,1)S(1)}, bf16[144,512]{1,0:T(8,128)(2,1)S(1)}) custom-call(s32[4]{0:T(128)S(1)} %pad_add_fusion.1.place, bf16[144,4096]{1,0:T(8,128)(2,1)S(1)} %bitcast.35, bf16[144,4096]{1,0:T(8,128)(2,1)S(1)} %collective-permute-done.refs_1_, ...), custom_call_target="tpu_custom_call" | custom-call | tf_op jit(solution)/shard_map/wide_product_kernel/pallas_call | solution.py:322
  114.0 1.2 collective-permute-start.21
  115.2 5.0 %read_state.3 = (f32[3,24,1024]{2,1,0:T(8,128)S(1)}, f32[6,24,1024]{2,1,0:T(8,128)S(1)}) custom-call(bf16[48,16,64,128]{3,2,1,0:T(8,128)(2,1)} %state.3, f32[8,3,48,256]{3,2,1,0:T(8,128)S(1)} %convert_element_type.3.every, f32[48,24,128]{2,1,0:T(8,128)S(1)} %bitcast.37, f32[8,1024]{1,0:T(8,128)S(1)} %get-tuple-element.53.mask), custom_call_target="tpu_custom_call" | custom-call | tf_op jit(solution)/shard_map/read_state/pallas_call | solution.py:334
  120.3 2.0 %collective-permute-done.21.refs_3_ = bf16[144,512]{1,0:T(8,128)(2,1)S(1)} collective-permute-done((bf16[144,512]{1,0:T(8,128)(2,1)S(1)}, bf16[144,512]{1,0:T(8,128)(2,1)S(1)}, u32[]{:S(2)}, u32[]{:S(2)}) %collective-permute-start.21) | collective-permute-done | bytes 147488 | tf_op jit(solution)/shard_map/ppermute | solution.py:384
  122.3 2.2 %scan_kernel.1 = (f32[3,48,1024]{2,1,0:T(8,128)S(1)}, f32[8,24,128]{2,1,0:T(8,128)S(1)}) custom-call(s32[4]{0:T(128)S(1)} %pad_add_fusion.1.place, bf16[144,512]{1,0:T(8,128)(2,1)S(1)} %get-tuple-element.63.refs_0_, bf16[144,512]{1,0:T(8,128)(2,1)S(1)} %collective-permute-done.19.refs_1_, bf16[144,512]{1,0:T(8,128)(2,1)S(1)} %collective-permute-done.20.refs_2_, ...), custom_call_target="tpu_custom_call" | custom-call | tf_op jit(solution)/shard_map/scan_kernel/pallas_call | solution.py:322
  124.5 12.1 %all_to_all.10.squares = f32[8,24,128]{2,1,0:T(8,128)S(1)} all-to-all(f32[8,24,128]{2,1,0:T(8,128)S(1)} %get-tuple-element.78), channel_id=1, replica_groups=mesh['x'=2,'z'=4,'c'=2,'tp'=8] {'tp'}, dimensions={0} | all-to-all | bytes 196608 | tf_op jit(solution)/shard_map/all_to_all | solution.py:461
  136.6 1.4 %norm_kernel.1 = bf16[3,48,1024]{2,1,0:T(8,128)(2,1)} custom-call(f32[3,48,1024]{2,1,0:T(8,128)S(1)} %get-tuple-element.77.gated, f32[8,24,128]{2,1,0:T(8,128)S(1)} %all_to_all.10.squares, f32[8,1024]{1,0:T(8,128)S(1)} %get-tuple-element.76.refs_13_.member), custom_call_target="tpu_custom_call" | custom-call | tf_op jit(solution)/shard_map/norm_kernel/pallas_call | solution.py:322
  (75 shorter events, 19.1 us)
Async XLA Ops:
  0.0 12.7 %collective-permute-start = (bf16[144,4096]{1,0:T(8,128)(2,1)}, bf16[144,4096]{1,0:T(8,128)(2,1)S(1)}, u32[]{:S(2)}, u32[]{:S(2)}) collective-permute-start(bf16[144,4096]{1,0:T(8,128)(2,1)} %bitcast.33), channel_id=1, source_target_pairs={{0,8},{8,0},{64,72},{72,64},{1,9},{9,1},{65,73},{73,65},{2,10},{10... | collective-permute-start | bytes 3538952 | tf_op jit(solution)/shard_map/ppermute | solution.py:384
  1.0 11.7 %collective-permute-start.1 = (bf16[48,4096]{1,0:T(8,128)(2,1)S(1)}, bf16[48,4096]{1,0:T(8,128)(2,1)}, u32[]{:S(2)}, u32[]{:S(2)}) collective-permute-start(bf16[48,4096]{1,0:T(8,128)(2,1)S(1)} %slice_bitcast_fusion.1), channel_id=1, source_target_pairs={{0,64},{8,72},{64,0},{72,8},{1,65},{9,73},{65,1},{73,9},{2,66},{10... | collective-permute-start | bytes 1179656 | tf_op jit(solution)/shard_map/ppermute | solution.py:384
  11.8 8.5 %copy-start = (bf16[3,48,4096]{2,1,0:T(8,128)(2,1)S(1)}, bf16[3,48,4096]{2,1,0:T(8,128)(2,1)}, u32[]{:S(2)}) copy-start(bf16[3,48,4096]{2,1,0:T(8,128)(2,1)} %param.32) | copy-start | bytes 3538948
  12.7 27.1 %all-to-all-start = ((bf16[32,32,640]{2,1,0:T(8,128)(2,1)}), bf16[32,32,640]{2,1,0:T(8,128)(2,1)}, u32[]{:S(2)}, u32[]{:S(2)}) async-start(bf16[32,32,640]{2,1,0:T(8,128)(2,1)} %refit.1), calls=%async_computation | async-start | bytes 2621440 | tf_op jit(solution)/shard_map/all_to_all | solution.py:399
  20.3 44.4 %copy-start.15 = (bf16[48,3,2,1,128]{4,2,3,1,0:T(2,128)(2,1)S(1)}, bf16[48,3,2,1,128]{4,2,3,1,0:T(2,128)(2,1)}, u32[]{:S(2)}) copy-start(bf16[48,3,2,1,128]{4,2,3,1,0:T(2,128)(2,1)} %param.35) | copy-start | bytes 221188
  20.3 46.1 %copy-start.10 = (f32[8192]{0:T(1024)S(1)}, f32[8192]{0:T(1024)}, u32[]{:S(2)}) copy-start(f32[8192]{0:T(1024)} %param.39) | copy-start | bytes 98308
  20.3 46.1 %copy-start.11 = (s32[141]{0:T(256)S(1)}, s32[141]{0:T(256)}, u32[]{:S(2)}) copy-start(s32[141]{0:T(256)} %pad_add_fusion.ints) | copy-start | bytes 1696
  20.3 46.1 %copy-start.12 = (f32[128]{0:T(128)S(1)}, f32[128]{0:T(128)}, u32[]{:S(2)}) copy-start(f32[128]{0:T(128)} %param.36) | copy-start | bytes 1540
  20.3 46.1 %copy-start.13 = (f32[128]{0:T(128)S(1)}, f32[128]{0:T(128)}, u32[]{:S(2)}) copy-start(f32[128]{0:T(128)} %param.37) | copy-start | bytes 1540
  20.3 46.1 %copy-start.14 = (f32[128]{0:T(128)S(1)}, f32[128]{0:T(128)}, u32[]{:S(2)}) copy-start(f32[128]{0:T(128)} %param.38) | copy-start | bytes 1540
  39.8 19.3 %collective-permute-start.2 = (bf16[96,4096]{1,0:T(8,128)(2,1)}, bf16[96,4096]{1,0:T(8,128)(2,1)}, u32[]{:S(2)}, u32[]{:S(2)}) collective-permute-start(bf16[96,4096]{1,0:T(8,128)(2,1)} %bitcast.6), channel_id=1, source_target_pairs={{0,64},{8,72},{64,0},{72,8},{1,65},{9,73},{65,1},{73,9},{2,66},{10... | collective-permute-start | bytes 2359304 | tf_op jit(solution)/shard_map/ppermute | solution.py:384
  41.4 10.4 %collective-permute-start.3 = (bf16[1024,128]{1,0:T(8,128)(2,1)S(1)}, bf16[1024,128]{1,0:T(8,128)(2,1)S(1)}, u32[]{:S(2)}, u32[]{:S(2)}) collective-permute-start(bf16[1024,128]{1,0:T(8,128)(2,1)S(1)} %slice.24.refs_6_), channel_id=1, source_target_pairs={{0,16},{16,32},{32,48},{48,0},{1,17},{17,33},{33,49},{49,1},{2,18}... | collective-permute-start | bytes 786440 | tf_op jit(solution)/shard_map/ppermute | solution.py:380
  43.4 12.8 %collective-permute-start.4 = (bf16[1024,128]{1,0:T(8,128)(2,1)S(1)}, bf16[1024,128]{1,0:T(8,128)(2,1)S(1)}, u32[]{:S(2)}, u32[]{:S(2)}) collective-permute-start(bf16[1024,128]{1,0:T(8,128)(2,1)S(1)} %slice.24.refs_6_), channel_id=1, source_target_pairs={{0,48},{16,0},{32,16},{48,32},{1,49},{17,1},{33,17},{49,33},{2,50}... | collective-permute-start | bytes 786440 | tf_op jit(solution)/shard_map/ppermute | solution.py:381
  45.6 12.4 %collective-permute-start.5 = (bf16[1024,128]{1,0:T(8,128)(2,1)S(1)}, bf16[1024,128]{1,0:T(8,128)(2,1)S(1)}, u32[]{:S(2)}, u32[]{:S(2)}) collective-permute-start(bf16[1024,128]{1,0:T(8,128)(2,1)S(1)} %slice.24.refs_6_), channel_id=1, source_target_pairs={{0,32},{16,48},{32,0},{48,16},{1,33},{17,49},{33,1},{49,17},{2,34}... | collective-permute-start | bytes 786440 | tf_op jit(solution)/shard_map/ppermute | solution.py:421
  59.1 8.4 %collective-permute-start.7 = (bf16[96,4096]{1,0:T(8,128)(2,1)}, bf16[96,4096]{1,0:T(8,128)(2,1)}, u32[]{:S(2)}, u32[]{:S(2)}) collective-permute-start(bf16[96,4096]{1,0:T(8,128)(2,1)} %collective-permute-done.2.refs_3_), channel_id=1, source_target_pairs={{0,8},{8,0},{64,72},{72,64},{1,9},{9,1},{65,73},{73,65},{2,10},{10... | collective-permute-start | bytes 2359304 | tf_op jit(solution)/shard_map/ppermute | solution.py:384
  60.4 16.7 %collective-permute-start.16 = (bf16[512,512]{1,0:T(8,128)(2,1)S(1)}, bf16[512,512]{1,0:T(8,128)(2,1)}, u32[]{:S(2)}, u32[]{:S(2)}) collective-permute-start(bf16[512,512]{1,0:T(8,128)(2,1)S(1)} %get-tuple-element.56.refs_7_), channel_id=1, source_target_pairs={{0,48},{16,0},{32,16},{48,32},{1,49},{17,1},{33,17},{49,33},{2,50}... | collective-permute-start | bytes 1572872 | tf_op jit(solution)/shard_map/ppermute | solution.py:381
  64.5 15.4 %collective-permute-start.15 = (bf16[512,512]{1,0:T(8,128)(2,1)S(1)}, bf16[512,512]{1,0:T(8,128)(2,1)}, u32[]{:S(2)}, u32[]{:S(2)}) collective-permute-start(bf16[512,512]{1,0:T(8,128)(2,1)S(1)} %get-tuple-element.55.refs_6_), channel_id=1, source_target_pairs={{0,16},{16,32},{32,48},{48,0},{1,17},{17,33},{33,49},{49,1},{2,18}... | collective-permute-start | bytes 1572872 | tf_op jit(solution)/shard_map/ppermute | solution.py:380
  64.5 3.0 %collective-permute-start.6 = (bf16[48,4096]{1,0:T(8,128)(2,1)}, bf16[48,4096]{1,0:T(8,128)(2,1)}, u32[]{:S(2)}, u32[]{:S(2)}) collective-permute-start(bf16[48,4096]{1,0:T(8,128)(2,1)} %collective-permute-done.1.refs_2_), channel_id=1, source_target_pairs={{0,8},{8,0},{64,72},{72,64},{1,9},{9,1},{65,73},{73,65},{2,10},{10... | collective-permute-start | bytes 1179656 | tf_op jit(solution)/shard_map/ppermute | solution.py:384
  67.5 1.0 copy-start.2
  74.9 9.3 %collective-permute-start.10 = (bf16[224,128]{1,0:T(8,128)(2,1)S(1)}, bf16[224,128]{1,0:T(8,128)(2,1)S(1)}, u32[]{:S(2)}, u32[]{:S(2)}) collective-permute-start(bf16[224,128]{1,0:T(8,128)(2,1)S(1)} %get-tuple-element.49), channel_id=1, source_target_pairs={{0,72},{8,64},{64,8},{72,0},{1,73},{9,65},{65,9},{73,1},{2,74},{10... | collective-permute-start | bytes 172040 | tf_op jit(solution)/shard_map/ppermute | solution.py:384
  75.4 8.8 %collective-permute-start.8 = (bf16[224,128]{1,0:T(8,128)(2,1)S(1)}, bf16[224,128]{1,0:T(8,128)(2,1)S(1)}, u32[]{:S(2)}, u32[]{:S(2)}) collective-permute-start(bf16[224,128]{1,0:T(8,128)(2,1)S(1)} %get-tuple-element.47), channel_id=1, source_target_pairs={{0,8},{8,0},{64,72},{72,64},{1,9},{9,1},{65,73},{73,65},{2,10},{10... | collective-permute-start | bytes 172040 | tf_op jit(solution)/shard_map/ppermute | solution.py:384
  75.7 8.6 %collective-permute-start.9 = (bf16[224,128]{1,0:T(8,128)(2,1)S(1)}, bf16[224,128]{1,0:T(8,128)(2,1)S(1)}, u32[]{:S(2)}, u32[]{:S(2)}) collective-permute-start(bf16[224,128]{1,0:T(8,128)(2,1)S(1)} %get-tuple-element.48), channel_id=1, source_target_pairs={{0,64},{8,72},{64,0},{72,8},{1,65},{9,73},{65,1},{73,9},{2,66},{10... | collective-permute-start | bytes 172040 | tf_op jit(solution)/shard_map/ppermute | solution.py:384
  80.9 27.6 %collective-permute-start.18 = (bf16[1024,512]{1,0:T(8,128)(2,1)S(1)}, bf16[1024,512]{1,0:T(8,128)(2,1)S(1)}, u32[]{:S(2)}, u32[]{:S(2)}) collective-permute-start(bf16[1024,512]{1,0:T(8,128)(2,1)S(1)} %pad_maximum_fusion.1), channel_id=1, source_target_pairs={{0,48},{16,0},{32,16},{48,32},{1,49},{17,1},{33,17},{49,33},{2,50}... | collective-permute-start | bytes 3145736 | tf_op jit(solution)/shard_map/ppermute | solution.py:381
  82.4 26.3 %collective-permute-start.17 = (bf16[1024,512]{1,0:T(8,128)(2,1)S(1)}, bf16[1024,512]{1,0:T(8,128)(2,1)S(1)}, u32[]{:S(2)}, u32[]{:S(2)}) collective-permute-start(bf16[1024,512]{1,0:T(8,128)(2,1)S(1)} %pad_maximum_fusion), channel_id=1, source_target_pairs={{0,16},{16,32},{32,48},{48,0},{1,17},{17,33},{33,49},{49,1},{2,18}... | collective-permute-start | bytes 3145736 | tf_op jit(solution)/shard_map/ppermute | solution.py:380
  84.9 4.7 %collective-permute-start.11 = (bf16[3,48,256]{2,1,0:T(8,128)(2,1)S(1)}, bf16[3,48,256]{2,1,0:T(8,128)(2,1)S(1)}, u32[]{:S(2)}, u32[]{:S(2)}) collective-permute-start(bf16[3,48,256]{2,1,0:T(8,128)(2,1)S(1)} %get-tuple-element.50), channel_id=1, source_target_pairs={{0,3},{1,0},{2,1},{3,2},{4,7},{5,4},{6,5},{7,6},{8,11},{9,8},{10,9... | collective-permute-start | bytes 221192 | tf_op jit(solution)/shard_map/ppermute | solution.py:440
  87.1 5.9 %collective-permute-start.12 = (bf16[3,48,256]{2,1,0:T(8,128)(2,1)S(1)}, bf16[3,48,256]{2,1,0:T(8,128)(2,1)S(1)}, u32[]{:S(2)}, u32[]{:S(2)}) collective-permute-start(bf16[3,48,256]{2,1,0:T(8,128)(2,1)S(1)} %get-tuple-element.50), channel_id=1, source_target_pairs={{0,2},{1,3},{2,0},{3,1},{4,6},{5,7},{6,4},{7,5},{8,10},{9,11},{10,... | collective-permute-start | bytes 221192 | tf_op jit(solution)/shard_map/ppermute | solution.py:440
  89.2 5.6 %collective-permute-start.13 = (bf16[3,48,256]{2,1,0:T(8,128)(2,1)S(1)}, bf16[3,48,256]{2,1,0:T(8,128)(2,1)S(1)}, u32[]{:S(2)}, u32[]{:S(2)}) collective-permute-start(bf16[3,48,256]{2,1,0:T(8,128)(2,1)S(1)} %get-tuple-element.50), channel_id=1, source_target_pairs={{0,1},{1,2},{2,3},{3,0},{4,5},{5,6},{6,7},{7,4},{8,9},{9,10},{10,1... | collective-permute-start | bytes 221192 | tf_op jit(solution)/shard_map/ppermute | solution.py:440
  94.8 8.3 %collective-permute-start.14 = (bf16[4,3,48,256]{3,2,1,0:T(8,128)(2,1)S(1)}, bf16[4,3,48,256]{3,2,1,0:T(8,128)(2,1)S(1)}, u32[]{:S(2)}, u32[]{:S(2)}) collective-permute-start(bf16[4,3,48,256]{3,2,1,0:T(8,128)(2,1)S(1)} %pad_maximum_fusion.2), channel_id=1, source_target_pairs={{0,4},{1,5},{2,6},{3,7},{4,0},{5,1},{6,2},{7,3},{8,12},{9,13},{10,... | collective-permute-start | bytes 884744 | tf_op jit(solution)/shard_map/ppermute | solution.py:441
  113.2 9.1 %copy-start.3 = (bf16[48,3,1024]{2,0,1:T(8,128)(2,1)S(1)}, bf16[48,3,1024]{2,0,1:T(8,128)(2,1)}, u32[]{:S(2)}) copy-start(bf16[48,3,1024]{2,0,1:T(8,128)(2,1)} %param.34) | copy-start | bytes 884740
  113.2 7.0 %collective-permute-start.19 = (bf16[144,512]{1,0:T(8,128)(2,1)S(1)}, bf16[144,512]{1,0:T(8,128)(2,1)S(1)}, u32[]{:S(2)}, u32[]{:S(2)}) collective-permute-start(bf16[144,512]{1,0:T(8,128)(2,1)S(1)} %get-tuple-element.64), channel_id=1, source_target_pairs={{0,8},{8,0},{64,72},{72,64},{1,9},{9,1},{65,73},{73,65},{2,10},{10... | collective-permute-start | bytes 442376 | tf_op jit(solution)/shard_map/ppermute | solution.py:384
  113.3 6.9 %collective-permute-start.20 = (bf16[144,512]{1,0:T(8,128)(2,1)S(1)}, bf16[144,512]{1,0:T(8,128)(2,1)S(1)}, u32[]{:S(2)}, u32[]{:S(2)}) collective-permute-start(bf16[144,512]{1,0:T(8,128)(2,1)S(1)} %get-tuple-element.65), channel_id=1, source_target_pairs={{0,64},{8,72},{64,0},{72,8},{1,65},{9,73},{65,1},{73,9},{2,66},{10... | collective-permute-start | bytes 442376 | tf_op jit(solution)/shard_map/ppermute | solution.py:384
  114.0 8.3 %collective-permute-start.21 = (bf16[144,512]{1,0:T(8,128)(2,1)S(1)}, bf16[144,512]{1,0:T(8,128)(2,1)S(1)}, u32[]{:S(2)}, u32[]{:S(2)}) collective-permute-start(bf16[144,512]{1,0:T(8,128)(2,1)S(1)} %get-tuple-element.66), channel_id=1, source_target_pairs={{0,72},{8,64},{64,8},{72,0},{1,73},{9,65},{65,9},{73,1},{2,74},{10... | collective-permute-start | bytes 442376 | tf_op jit(solution)/shard_map/ppermute | solution.py:384
  (7 other events, 5.7 us)

commit v4 on v3

--- a/solution.py
+++ b/solution.py
@@ -161,12 +161,13 @@
 
 
 def wide_product_kernel(place, *refs):
-    top, bottom, left_top, right_bottom, from_left, from_right = refs[6:12]
+    count = len(refs) - 10
+    top, bottom, left_top, right_bottom, from_left, from_right = refs[count : count + 6]
     halves = lambda ref: (ref.at[0:512, :], ref.at[512:1024, :])
     left_bottom, far_top = halves(from_left)
     right_top, far_bottom = halves(from_right)
     weights = ((top, bottom), (left_top, left_bottom), (right_top, right_bottom), (far_top, far_bottom))
-    multiply(place, refs[:6], weights, refs[12:16])
+    multiply(place, refs[:count], weights, refs[count + 6 :])
 
 
 def first_product_kernel(place, ints, *refs):
@@ -330,14 +331,14 @@
     )(*args)
 
 
-def read_state(state, every, c_all, mask, part):
+def read_state(state, every, c_all, mask, first, count):
     return pl.pallas_call(
         state_kernel,
-        grid=(ROWS // 16,),
+        grid=(count,),
         in_specs=[
-            pl.BlockSpec((8, OWN_HEADS, HEAD_DIM, STATE), lambda i: (i + 3 * part, 0, 0, 0)),
-            pl.BlockSpec((GROUPS, STEPS, 8, 2 * STATE), lambda i: (0, 0, i + 3 * part, 0)),
-            pl.BlockSpec((8, 24, STATE), lambda i: (i + 3 * part, 0, 0)),
+            pl.BlockSpec((8, OWN_HEADS, HEAD_DIM, STATE), lambda i: (i + first, 0, 0, 0)),
+            pl.BlockSpec((GROUPS, STEPS, 8, 2 * STATE), lambda i: (0, 0, i + first, 0)),
+            pl.BlockSpec((8, 24, STATE), lambda i: (i + first, 0, 0)),
             pl.BlockSpec((8, SPAN), lambda i: (0, 0)),
         ],
         out_specs=[
@@ -345,8 +346,8 @@
             pl.BlockSpec((6, 8, SPAN), lambda i: (0, i, 0)),
         ],
         out_shape=[
-            jax.ShapeDtypeStruct((3, ROWS // 2, SPAN), jnp.float32),
-            jax.ShapeDtypeStruct((6, ROWS // 2, SPAN), jnp.float32),
+            jax.ShapeDtypeStruct((3, 8 * count, SPAN), jnp.float32),
+            jax.ShapeDtypeStruct((6, 8 * count, SPAN), jnp.float32),
         ],
         compiler_params=pltpu.CompilerParams(vmem_limit_bytes=50 * 2**20),
         name="read_state",
@@ -418,10 +419,12 @@
     stored_groups = jnp.swapaxes(conv_groups.reshape(ROWS, TAPS - 1, 2 * STATE), 0, 1)
 
     own = owned[:, :128]
-    pieces = [own, up(own), down(own), lax.ppermute(own, "z", [(i, (i + 2) % 4) for i in range(4)])]
+    halves = [owned[512 * i : 512 * i + 512, 128:] for i in range(2)]
+    own_late, *halves = lax.optimization_barrier((own, *halves))
+    pieces = [own, up(own_late), down(own), lax.ppermute(own, "z", [(i, (i + 2) % 4) for i in range(4)])]
     far_pair = after(far, *pieces[1:])
     rows = [hidden_input.reshape(FLAT, -1), near, *far, *[swap(value, 1) for value in far_pair]]
-    top, bottom = [after(owned[512 * i : 512 * i + 512, 128:], *pieces[1:]) for i in range(2)]
+    top, bottom = [after(half, *pieces[1:]) for half in halves]
     left_top, right_bottom = up(top), down(bottom)
 
     first = call(
@@ -441,7 +444,7 @@
     every = jnp.concatenate([every, lax.ppermute(every, "tp", [(i, i ^ 4) for i in range(8)])])
     every = every.astype(jnp.float32)
     c_all = every[..., STATE:].transpose(2, 1, 0, 3).reshape(ROWS, STEPS * GROUPS, STATE)
-    read, pair = read_state(scan_state, every, c_all, mask, 0)
+    read, pair = read_state(scan_state, every, c_all, mask, 0, 4)
 
     top, read = lax.optimization_barrier((top, read))
     second = call(
@@ -450,7 +453,7 @@
         scalars=1, limit=24,
     )
     c_all, *second = lax.optimization_barrier((c_all, *second))
-    read_more, pair_more = read_state(scan_state, every, c_all, mask, 1)
+    read_more, pair_more = read_state(scan_state, every, c_all, mask, 4, 2)
     second = exchanged(second)
     gated, squares = call(
         scan_kernel,

time: 139 us -> 137 us (0.986)
  waiting for transfers between devices: 46.1 us -> 43.3 us
  starting transfers between devices: 31.6 us -> 33.8 us
    ppermute x1, waiting for transfers between devices: 1.08 us -> 5.47 us  [per_device(): lax.ppermute(own, 'z', [(i, (i + 2) % 4) for i in range(4)])]
    ppermute x3, waiting for transfers between devices: 3.67 us -> 0.01 us  [per_device(): lax.ppermute(value, 'z', [(i, (i + 3) % 4) for i in range(4)])]
    ppermute x3, waiting for transfers between devices: 5.55 us -> 2.7 us  [per_device(): lax.ppermute(b_and_c, 'tp', ahead(k))]
    ppermute x1, starting transfers between devices: 1.78 us -> 3.58 us  [per_device(): lax.ppermute(own, 'z', [(i, (i + 2) % 4) for i in range(4)])]
  transfers between devices with their start and end apart: 23 -> 23, of which waited for: 13 -> 12; matrix products, arithmetic and copies ran while one was open for 7% -> 7% of each run, Pallas kernels for 16% -> 16%
where the time goes in v4:
time: 137 us; the launch traced here: 136 us
  waiting for transfers between devices  43.3 us (32%)
  starting transfers between devices  33.8 us (25%)
  Pallas kernels  30.1 us (22%)
  local copies, waits for them, and re-layouts  12.2 us (9%)
  blocking collectives  12.1 us (9%)
  other arithmetic  3.82 us (3%)
    all_to_all x1, waiting for transfers between devices, per_device(): lax.all_to_all(after(sent, *far, near), ('x', 'c', 'tp'), split_axis=0, c...  18.5 us
    pallas_call x6, Pallas kernels, call(): pl.pallas_call(kernel, in_specs=[smem] * scalars + [vmem] * (len(args) -...  13.4 us
    all_to_all x1, blocking collectives, per_device(): lax.all_to_all(squares, 'tp', split_axis=0, concat_axis=0, tiled=True)  12.1 us
    pallas_call x2, Pallas kernels, read_state(): pl.pallas_call(state_kernel, grid=(count,), in_specs=[pl.BlockSpec((8, OW...  9.6 us
    all_to_all x1, starting transfers between devices, per_device(): lax.all_to_all(after(sent, *far, near), ('x', 'c', 'tp'), split_axis=0, c...  7.52 us
    pallas_call x1, Pallas kernels, refit(): pl.pallas_call(refit_kernel, in_specs=[pl.BlockSpec(memory_space=pltpu.SM...  7.08 us
    ppermute x3, starting transfers between devices, per_device(): lax.ppermute(value, 'z', [(i, (i + 3) % 4) for i in range(4)])  6.74 us
    unnamed x37, local copies, waits for them, and re-layouts  6.69 us
  transfers between devices with their start and end apart: 23, of which 12 were waited for; matrix products, arithmetic and copies ran while one was open for 7% of the time, Pallas kernels for 16%

profile of v4, /device:TPU:0, one launch (start us, length us, event | category | flops | bytes accessed | tf_op | source)
XLA Modules:
  0.0 136.2 jit_solution(1905268482604806729)
XLA Ops:
  1.0 1.7 %collective-permute-start.1 = (bf16[48,4096]{1,0:T(8,128)(2,1)S(1)}, bf16[48,4096]{1,0:T(8,128)(2,1)}, u32[]{:S(2)}, u32[]{:S(2)}) collective-permute-start(bf16[48,4096]{1,0:T(8,128)(2,1)S(1)} %slice_bitcast_fusion.1), channel_id=1, source_target_pairs={{0,64},{8,72},{64,0},{72,8},{1,65},{9,73},{65,1},{73,9},{2,66},{10... | collective-permute-start | bytes 1179656 | tf_op jit(solution)/shard_map/ppermute | solution.py:385
  3.3 1.3 pad_add_fusion.ints
  4.7 7.1 %refit.1 = bf16[32,32,640]{2,1,0:T(8,128)(2,1)} custom-call(s32[141]{0:T(256)} %pad_add_fusion.ints, s32[1,128]{1,0:T(1,128)} %bitcast.48, f32[1,1]{1,0:T(1,128)} %bitcast.32.rate, f32[5,80]{1,0:T(8,128)} %conv_m.1, bf16[5,80]{1,0:T(8,128)(2,1)} %conv_g.1, f32[5,80]{1,0:T(8,128)} %conv_f.1, f32[5,80]{1,0:T(8,128)} %conv_s.1, f32[32,18560]{1,0:T(8,128)} %master.1, ...), custom_call_target="tpu_custom_call" | custom-call | tf_op jit(solution)/shard_map/refit/pallas_call | solution.py:106
  12.7 7.5 %all-to-all-start = ((bf16[32,32,640]{2,1,0:T(8,128)(2,1)}), bf16[32,32,640]{2,1,0:T(8,128)(2,1)}, u32[]{:S(2)}, u32[]{:S(2)}) async-start(bf16[32,32,640]{2,1,0:T(8,128)(2,1)} %refit.1), calls=%async_computation | async-start | bytes 2621440 | tf_op jit(solution)/shard_map/all_to_all | solution.py:400
  21.3 18.5 %all-to-all-done = bf16[32,32,640]{2,1,0:T(8,128)(2,1)} async-done(((bf16[32,32,640]{2,1,0:T(8,128)(2,1)}), bf16[32,32,640]{2,1,0:T(8,128)(2,1)}, u32[]{:S(2)}, u32[]{:S(2)}) %all-to-all-start) | async-done | bytes 1310752 | tf_op jit(solution)/shard_map/all_to_all | solution.py:400
  41.4 1.4 %fusion = (bf16[512,512]{1,0:T(8,128)(2,1)S(1)}, bf16[512,512]{1,0:T(8,128)(2,1)S(1)}) fusion(bf16[1024,640]{1,0:T(8,128)(2,1)} %bitcast.9), kind=kLoop, calls=%fused_computation.13 | loop fusion | bytes 2097152 | tf_op jit(solution)/shard_map/slice | solution.py:422
  42.8 2.0 %collective-permute-start.3 = (bf16[1024,128]{1,0:T(8,128)(2,1)S(1)}, bf16[1024,128]{1,0:T(8,128)(2,1)S(1)}, u32[]{:S(2)}, u32[]{:S(2)}) collective-permute-start(bf16[1024,128]{1,0:T(8,128)(2,1)S(1)} %slice.24.refs_6_), channel_id=1, source_target_pairs={{0,16},{16,32},{32,48},{48,0},{1,17},{17,33},{33,49},{49,1},{2,18}... | collective-permute-start | bytes 786440 | tf_op jit(solution)/shard_map/ppermute | solution.py:381
  44.7 3.6 %collective-permute-start.5 = (bf16[1024,128]{1,0:T(8,128)(2,1)S(1)}, bf16[1024,128]{1,0:T(8,128)(2,1)S(1)}, u32[]{:S(2)}, u32[]{:S(2)}) collective-permute-start(bf16[1024,128]{1,0:T(8,128)(2,1)S(1)} %slice.24.refs_6_), channel_id=1, source_target_pairs={{0,32},{16,48},{32,0},{48,16},{1,33},{17,49},{33,1},{49,17},{2,34}... | collective-permute-start | bytes 786440 | tf_op jit(solution)/shard_map/ppermute | solution.py:424
  49.3 3.9 %collective-permute-done.3.refs_7_ = bf16[1024,128]{1,0:T(8,128)(2,1)S(1)} collective-permute-done((bf16[1024,128]{1,0:T(8,128)(2,1)S(1)}, bf16[1024,128]{1,0:T(8,128)(2,1)S(1)}, u32[]{:S(2)}, u32[]{:S(2)}) %collective-permute-start.3) | collective-permute-done | bytes 262176 | tf_op jit(solution)/shard_map/ppermute | solution.py:381
  53.9 5.5 %collective-permute-done.5.refs_9_ = bf16[1024,128]{1,0:T(8,128)(2,1)S(1)} collective-permute-done((bf16[1024,128]{1,0:T(8,128)(2,1)S(1)}, bf16[1024,128]{1,0:T(8,128)(2,1)S(1)}, u32[]{:S(2)}, u32[]{:S(2)}) %collective-permute-start.5) | collective-permute-done | bytes 262176 | tf_op jit(solution)/shard_map/ppermute | solution.py:424
  61.4 2.7 %collective-permute-start.16 = (bf16[512,512]{1,0:T(8,128)(2,1)S(1)}, bf16[512,512]{1,0:T(8,128)(2,1)}, u32[]{:S(2)}, u32[]{:S(2)}) collective-permute-start(bf16[512,512]{1,0:T(8,128)(2,1)S(1)} %get-tuple-element.62.refs_7_), channel_id=1, source_target_pairs={{0,48},{16,0},{32,16},{48,32},{1,49},{17,1},{33,17},{49,33},{2,50}... | collective-permute-start | bytes 1572872 | tf_op jit(solution)/shard_map/ppermute | solution.py:382
  70.7 3.7 %first_product_kernel.1 = (bf16[224,128]{1,0:T(8,128)(2,1)S(1)}, bf16[224,128]{1,0:T(8,128)(2,1)S(1)}, bf16[224,128]{1,0:T(8,128)(2,1)S(1)}, bf16[224,128]{1,0:T(8,128)(2,1)S(1)}) custom-call(s32[4]{0:T(128)S(1)} %pad_add_fusion.1.place, s32[141]{0:T(256)S(1)} %copy-done.11, bf16[144,4096]{1,0:T(8,128)(2,1)S(1)} %bitcast.34, ...), custom_call_target="tpu_custom_call" | custom-call | tf_op jit(solution)/shard_map/first_product_kernel/pallas_call | solution.py:323
  74.9 1.4 %collective-permute-start.9 = (bf16[224,128]{1,0:T(8,128)(2,1)S(1)}, bf16[224,128]{1,0:T(8,128)(2,1)S(1)}, u32[]{:S(2)}, u32[]{:S(2)}) collective-permute-start(bf16[224,128]{1,0:T(8,128)(2,1)S(1)} %get-tuple-element.52), channel_id=1, source_target_pairs={{0,64},{8,72},{64,0},{72,8},{1,65},{9,73},{65,1},{73,9},{2,66},{10... | collective-permute-start | bytes 172040 | tf_op jit(solution)/shard_map/ppermute | solution.py:385
  77.6 1.1 pad_maximum_fusion.1
  78.7 3.0 %collective-permute-start.18 = (bf16[1024,512]{1,0:T(8,128)(2,1)S(1)}, bf16[1024,512]{1,0:T(8,128)(2,1)S(1)}, u32[]{:S(2)}, u32[]{:S(2)}) collective-permute-start(bf16[1024,512]{1,0:T(8,128)(2,1)S(1)} %pad_maximum_fusion.1), channel_id=1, source_target_pairs={{0,48},{16,0},{32,16},{48,32},{1,49},{17,1},{33,17},{49,33},{2,50}... | collective-permute-start | bytes 3145736 | tf_op jit(solution)/shard_map/ppermute | solution.py:382
  82.4 1.9 %collective-permute-start.13 = (bf16[3,48,256]{2,1,0:T(8,128)(2,1)S(1)}, bf16[3,48,256]{2,1,0:T(8,128)(2,1)S(1)}, u32[]{:S(2)}, u32[]{:S(2)}) collective-permute-start(bf16[3,48,256]{2,1,0:T(8,128)(2,1)S(1)} %get-tuple-element.54), channel_id=1, source_target_pairs={{0,1},{1,2},{2,3},{3,0},{4,5},{5,6},{6,7},{7,4},{8,9},{9,10},{10,1... | collective-permute-start | bytes 221192 | tf_op jit(solution)/shard_map/ppermute | solution.py:443
  84.3 1.7 %collective-permute-start.12 = (bf16[3,48,256]{2,1,0:T(8,128)(2,1)S(1)}, bf16[3,48,256]{2,1,0:T(8,128)(2,1)S(1)}, u32[]{:S(2)}, u32[]{:S(2)}) collective-permute-start(bf16[3,48,256]{2,1,0:T(8,128)(2,1)S(1)} %get-tuple-element.54), channel_id=1, source_target_pairs={{0,2},{1,3},{2,0},{3,1},{4,6},{5,7},{6,4},{7,5},{8,10},{9,11},{10,... | collective-permute-start | bytes 221192 | tf_op jit(solution)/shard_map/ppermute | solution.py:443
  86.0 1.6 %collective-permute-start.11 = (bf16[3,48,256]{2,1,0:T(8,128)(2,1)S(1)}, bf16[3,48,256]{2,1,0:T(8,128)(2,1)S(1)}, u32[]{:S(2)}, u32[]{:S(2)}) collective-permute-start(bf16[3,48,256]{2,1,0:T(8,128)(2,1)S(1)} %get-tuple-element.54), channel_id=1, source_target_pairs={{0,3},{1,0},{2,1},{3,2},{4,7},{5,4},{6,5},{7,6},{8,11},{9,8},{10,9... | collective-permute-start | bytes 221192 | tf_op jit(solution)/shard_map/ppermute | solution.py:443
  87.6 1.2 collective-permute-done.13
  88.9 1.3 collective-permute-done.12
  90.4 2.0 %collective-permute-start.14 = (bf16[4,3,48,256]{3,2,1,0:T(8,128)(2,1)S(1)}, bf16[4,3,48,256]{3,2,1,0:T(8,128)(2,1)S(1)}, u32[]{:S(2)}, u32[]{:S(2)}) collective-permute-start(bf16[4,3,48,256]{3,2,1,0:T(8,128)(2,1)S(1)} %pad_maximum_fusion.2), channel_id=1, source_target_pairs={{0,4},{1,5},{2,6},{3,7},{4,0},{5,1},{6,2},{7,3},{8,12},{9,13},{10,... | collective-permute-start | bytes 884744 | tf_op jit(solution)/shard_map/ppermute | solution.py:444
  92.4 6.6 %collective-permute-done.14 = bf16[4,3,48,256]{3,2,1,0:T(8,128)(2,1)S(1)} collective-permute-done((bf16[4,3,48,256]{3,2,1,0:T(8,128)(2,1)S(1)}, bf16[4,3,48,256]{3,2,1,0:T(8,128)(2,1)S(1)}, u32[]{:S(2)}, u32[]{:S(2)}) %collective-permute-start.14) | collective-permute-done | bytes 294944 | tf_op jit(solution)/shard_map/ppermute | solution.py:444
  99.4 6.1 %read_state.2 = (f32[3,32,1024]{2,1,0:T(8,128)S(1)}, f32[6,32,1024]{2,1,0:T(8,128)S(1)}) custom-call(bf16[48,16,64,128]{3,2,1,0:T(8,128)(2,1)} %state.3, f32[8,3,48,256]{3,2,1,0:T(8,128)S(1)} %convert_element_type.3.every, f32[48,24,128]{2,1,0:T(8,128)S(1)} %bitcast.36, f32[8,1024]{1,0:T(8,128)S(1)} %get-tuple-element.58.mask), custom_call_target="tpu_custom_call" | custom-call | tf_op jit(solution)/shard_map/read_state/pallas_call | solution.py:335
  105.6 1.5 %collective-permute-done.17.refs_10_ = bf16[1024,512]{1,0:T(8,128)(2,1)S(1)} collective-permute-done((bf16[1024,512]{1,0:T(8,128)(2,1)S(1)}, bf16[1024,512]{1,0:T(8,128)(2,1)S(1)}, u32[]{:S(2)}, u32[]{:S(2)}) %collective-permute-start.17) | collective-permute-done | bytes 1048608 | tf_op jit(solution)/shard_map/ppermute | solution.py:381
  107.0 4.5 %wide_product_kernel.1 = (bf16[144,512]{1,0:T(8,128)(2,1)S(1)}, bf16[144,512]{1,0:T(8,128)(2,1)S(1)}, bf16[144,512]{1,0:T(8,128)(2,1)S(1)}, bf16[144,512]{1,0:T(8,128)(2,1)S(1)}) custom-call(s32[4]{0:T(128)S(1)} %pad_add_fusion.1.place, bf16[144,4096]{1,0:T(8,128)(2,1)S(1)} %bitcast.35, bf16[144,4096]{1,0:T(8,128)(2,1)S(1)} %collective-permute-done.refs_1_, ...), custom_call_target="tpu_custom_call" | custom-call | tf_op jit(solution)/shard_map/wide_product_kernel/pallas_call | solution.py:323
  111.7 1.5 %collective-permute-start.20 = (bf16[144,512]{1,0:T(8,128)(2,1)S(1)}, bf16[144,512]{1,0:T(8,128)(2,1)S(1)}, u32[]{:S(2)}, u32[]{:S(2)}) collective-permute-start(bf16[144,512]{1,0:T(8,128)(2,1)S(1)} %get-tuple-element.71), channel_id=1, source_target_pairs={{0,64},{8,72},{64,0},{72,8},{1,65},{9,73},{65,1},{73,9},{2,66},{10... | collective-permute-start | bytes 442376 | tf_op jit(solution)/shard_map/ppermute | solution.py:385
  113.5 3.5 %read_state.3 = (f32[3,16,1024]{2,1,0:T(8,128)S(1)}, f32[6,16,1024]{2,1,0:T(8,128)S(1)}) custom-call(bf16[48,16,64,128]{3,2,1,0:T(8,128)(2,1)} %state.3, f32[8,3,48,256]{3,2,1,0:T(8,128)S(1)} %convert_element_type.3.every, f32[48,24,128]{2,1,0:T(8,128)S(1)} %bitcast.37, f32[8,1024]{1,0:T(8,128)S(1)} %get-tuple-element.58.mask), custom_call_target="tpu_custom_call" | custom-call | tf_op jit(solution)/shard_map/read_state/pallas_call | solution.py:335
  117.0 1.4 %collective-permute-done.20.refs_2_ = bf16[144,512]{1,0:T(8,128)(2,1)S(1)} collective-permute-done((bf16[144,512]{1,0:T(8,128)(2,1)S(1)}, bf16[144,512]{1,0:T(8,128)(2,1)S(1)}, u32[]{:S(2)}, u32[]{:S(2)}) %collective-permute-start.20) | collective-permute-done | bytes 147488 | tf_op jit(solution)/shard_map/ppermute | solution.py:385
  118.4 2.2 %collective-permute-done.21.refs_3_ = bf16[144,512]{1,0:T(8,128)(2,1)S(1)} collective-permute-done((bf16[144,512]{1,0:T(8,128)(2,1)S(1)}, bf16[144,512]{1,0:T(8,128)(2,1)S(1)}, u32[]{:S(2)}, u32[]{:S(2)}) %collective-permute-start.21) | collective-permute-done | bytes 147488 | tf_op jit(solution)/shard_map/ppermute | solution.py:385
  120.6 2.2 %scan_kernel.1 = (f32[3,48,1024]{2,1,0:T(8,128)S(1)}, f32[8,24,128]{2,1,0:T(8,128)S(1)}) custom-call(s32[4]{0:T(128)S(1)} %pad_add_fusion.1.place, bf16[144,512]{1,0:T(8,128)(2,1)S(1)} %get-tuple-element.69.refs_0_, bf16[144,512]{1,0:T(8,128)(2,1)S(1)} %collective-permute-done.19.refs_1_, bf16[144,512]{1,0:T(8,128)(2,1)S(1)} %collective-permute-done.20.refs_2_, ...), custom_call_target="tpu_custom_call" | custom-call | tf_op jit(solution)/shard_map/scan_kernel/pallas_call | solution.py:323
  122.8 12.1 %all_to_all.10.squares = f32[8,24,128]{2,1,0:T(8,128)S(1)} all-to-all(f32[8,24,128]{2,1,0:T(8,128)S(1)} %get-tuple-element.84), channel_id=1, replica_groups=mesh['x'=2,'z'=4,'c'=2,'tp'=8] {'tp'}, dimensions={0} | all-to-all | bytes 196608 | tf_op jit(solution)/shard_map/all_to_all | solution.py:464
  134.9 1.4 %norm_kernel.1 = bf16[3,48,1024]{2,1,0:T(8,128)(2,1)} custom-call(f32[3,48,1024]{2,1,0:T(8,128)S(1)} %get-tuple-element.83.gated, f32[8,24,128]{2,1,0:T(8,128)S(1)} %all_to_all.10.squares, f32[8,1024]{1,0:T(8,128)S(1)} %get-tuple-element.82.refs_13_.member), custom_call_target="tpu_custom_call" | custom-call | tf_op jit(solution)/shard_map/norm_kernel/pallas_call | solution.py:323
  (75 shorter events, 18.4 us)
Async XLA Ops:
  0.0 12.7 %collective-permute-start = (bf16[144,4096]{1,0:T(8,128)(2,1)}, bf16[144,4096]{1,0:T(8,128)(2,1)S(1)}, u32[]{:S(2)}, u32[]{:S(2)}) collective-permute-start(bf16[144,4096]{1,0:T(8,128)(2,1)} %bitcast.33), channel_id=1, source_target_pairs={{0,8},{8,0},{64,72},{72,64},{1,9},{9,1},{65,73},{73,65},{2,10},{10... | collective-permute-start | bytes 3538952 | tf_op jit(solution)/shard_map/ppermute | solution.py:385
  1.0 11.7 %collective-permute-start.1 = (bf16[48,4096]{1,0:T(8,128)(2,1)S(1)}, bf16[48,4096]{1,0:T(8,128)(2,1)}, u32[]{:S(2)}, u32[]{:S(2)}) collective-permute-start(bf16[48,4096]{1,0:T(8,128)(2,1)S(1)} %slice_bitcast_fusion.1), channel_id=1, source_target_pairs={{0,64},{8,72},{64,0},{72,8},{1,65},{9,73},{65,1},{73,9},{2,66},{10... | collective-permute-start | bytes 1179656 | tf_op jit(solution)/shard_map/ppermute | solution.py:385
  11.8 8.5 %copy-start = (bf16[3,48,4096]{2,1,0:T(8,128)(2,1)S(1)}, bf16[3,48,4096]{2,1,0:T(8,128)(2,1)}, u32[]{:S(2)}) copy-start(bf16[3,48,4096]{2,1,0:T(8,128)(2,1)} %param.32) | copy-start | bytes 3538948
  12.7 27.1 %all-to-all-start = ((bf16[32,32,640]{2,1,0:T(8,128)(2,1)}), bf16[32,32,640]{2,1,0:T(8,128)(2,1)}, u32[]{:S(2)}, u32[]{:S(2)}) async-start(bf16[32,32,640]{2,1,0:T(8,128)(2,1)} %refit.1), calls=%async_computation | async-start | bytes 2621440 | tf_op jit(solution)/shard_map/all_to_all | solution.py:400
  20.3 43.8 %copy-start.15 = (bf16[48,3,2,1,128]{4,2,3,1,0:T(2,128)(2,1)S(1)}, bf16[48,3,2,1,128]{4,2,3,1,0:T(2,128)(2,1)}, u32[]{:S(2)}) copy-start(bf16[48,3,2,1,128]{4,2,3,1,0:T(2,128)(2,1)} %param.35) | copy-start | bytes 221188
  20.3 45.5 %copy-start.10 = (f32[8192]{0:T(1024)S(1)}, f32[8192]{0:T(1024)}, u32[]{:S(2)}) copy-start(f32[8192]{0:T(1024)} %param.39) | copy-start | bytes 98308
  20.3 45.5 %copy-start.11 = (s32[141]{0:T(256)S(1)}, s32[141]{0:T(256)}, u32[]{:S(2)}) copy-start(s32[141]{0:T(256)} %pad_add_fusion.ints) | copy-start | bytes 1696
  20.3 45.5 %copy-start.12 = (f32[128]{0:T(128)S(1)}, f32[128]{0:T(128)}, u32[]{:S(2)}) copy-start(f32[128]{0:T(128)} %param.36) | copy-start | bytes 1540
  20.3 45.5 %copy-start.13 = (f32[128]{0:T(128)S(1)}, f32[128]{0:T(128)}, u32[]{:S(2)}) copy-start(f32[128]{0:T(128)} %param.37) | copy-start | bytes 1540
  20.3 45.5 %copy-start.14 = (f32[128]{0:T(128)S(1)}, f32[128]{0:T(128)}, u32[]{:S(2)}) copy-start(f32[128]{0:T(128)} %param.38) | copy-start | bytes 1540
  39.8 21.0 %collective-permute-start.2 = (bf16[96,4096]{1,0:T(8,128)(2,1)}, bf16[96,4096]{1,0:T(8,128)(2,1)}, u32[]{:S(2)}, u32[]{:S(2)}) collective-permute-start(bf16[96,4096]{1,0:T(8,128)(2,1)} %bitcast.6), channel_id=1, source_target_pairs={{0,64},{8,72},{64,0},{72,8},{1,65},{9,73},{65,1},{73,9},{2,66},{10... | collective-permute-start | bytes 2359304 | tf_op jit(solution)/shard_map/ppermute | solution.py:385
  41.4 19.4 %copy-start.1 = (bf16[1024,128]{1,0:T(8,128)(2,1)}, bf16[1024,128]{1,0:T(8,128)(2,1)S(1)}, u32[]{:S(2)}) copy-start(bf16[1024,128]{1,0:T(8,128)(2,1)S(1)} %slice.24.refs_6_) | copy-start | bytes 786436
  42.8 10.4 %collective-permute-start.3 = (bf16[1024,128]{1,0:T(8,128)(2,1)S(1)}, bf16[1024,128]{1,0:T(8,128)(2,1)S(1)}, u32[]{:S(2)}, u32[]{:S(2)}) collective-permute-start(bf16[1024,128]{1,0:T(8,128)(2,1)S(1)} %slice.24.refs_6_), channel_id=1, source_target_pairs={{0,16},{16,32},{32,48},{48,0},{1,17},{17,33},{33,49},{49,1},{2,18}... | collective-permute-start | bytes 786440 | tf_op jit(solution)/shard_map/ppermute | solution.py:381
  44.7 14.6 %collective-permute-start.5 = (bf16[1024,128]{1,0:T(8,128)(2,1)S(1)}, bf16[1024,128]{1,0:T(8,128)(2,1)S(1)}, u32[]{:S(2)}, u32[]{:S(2)}) collective-permute-start(bf16[1024,128]{1,0:T(8,128)(2,1)S(1)} %slice.24.refs_6_), channel_id=1, source_target_pairs={{0,32},{16,48},{32,0},{48,16},{1,33},{17,49},{33,1},{49,17},{2,34}... | collective-permute-start | bytes 786440 | tf_op jit(solution)/shard_map/ppermute | solution.py:424
  48.3 11.7 %collective-permute-start.4 = (bf16[1024,128]{1,0:T(8,128)(2,1)S(1)}, bf16[1024,128]{1,0:T(8,128)(2,1)S(1)}, u32[]{:S(2)}, u32[]{:S(2)}) collective-permute-start(bf16[1024,128]{1,0:T(8,128)(2,1)S(1)} %slice.24.refs_6_), channel_id=1, source_target_pairs={{0,48},{16,0},{32,16},{48,32},{1,49},{17,1},{33,17},{49,33},{2,50}... | collective-permute-start | bytes 786440 | tf_op jit(solution)/shard_map/ppermute | solution.py:382
  60.8 6.1 %collective-permute-start.7 = (bf16[96,4096]{1,0:T(8,128)(2,1)}, bf16[96,4096]{1,0:T(8,128)(2,1)}, u32[]{:S(2)}, u32[]{:S(2)}) collective-permute-start(bf16[96,4096]{1,0:T(8,128)(2,1)} %collective-permute-done.2.refs_3_), channel_id=1, source_target_pairs={{0,8},{8,0},{64,72},{72,64},{1,9},{9,1},{65,73},{73,65},{2,10},{10... | collective-permute-start | bytes 2359304 | tf_op jit(solution)/shard_map/ppermute | solution.py:385
  60.8 15.7 %collective-permute-start.15 = (bf16[512,512]{1,0:T(8,128)(2,1)S(1)}, bf16[512,512]{1,0:T(8,128)(2,1)}, u32[]{:S(2)}, u32[]{:S(2)}) collective-permute-start(bf16[512,512]{1,0:T(8,128)(2,1)S(1)} %get-tuple-element.60.refs_6_), channel_id=1, source_target_pairs={{0,16},{16,32},{32,48},{48,0},{1,17},{17,33},{33,49},{49,1},{2,18}... | collective-permute-start | bytes 1572872 | tf_op jit(solution)/shard_map/ppermute | solution.py:381
  61.4 15.1 %collective-permute-start.16 = (bf16[512,512]{1,0:T(8,128)(2,1)S(1)}, bf16[512,512]{1,0:T(8,128)(2,1)}, u32[]{:S(2)}, u32[]{:S(2)}) collective-permute-start(bf16[512,512]{1,0:T(8,128)(2,1)S(1)} %get-tuple-element.62.refs_7_), channel_id=1, source_target_pairs={{0,48},{16,0},{32,16},{48,32},{1,49},{17,1},{33,17},{49,33},{2,50}... | collective-permute-start | bytes 1572872 | tf_op jit(solution)/shard_map/ppermute | solution.py:382
  64.1 2.8 %collective-permute-start.6 = (bf16[48,4096]{1,0:T(8,128)(2,1)}, bf16[48,4096]{1,0:T(8,128)(2,1)}, u32[]{:S(2)}, u32[]{:S(2)}) collective-permute-start(bf16[48,4096]{1,0:T(8,128)(2,1)} %collective-permute-done.1.refs_2_), channel_id=1, source_target_pairs={{0,8},{8,0},{64,72},{72,64},{1,9},{9,1},{65,73},{73,65},{2,10},{10... | collective-permute-start | bytes 1179656 | tf_op jit(solution)/shard_map/ppermute | solution.py:385
  74.3 7.4 %collective-permute-start.8 = (bf16[224,128]{1,0:T(8,128)(2,1)S(1)}, bf16[224,128]{1,0:T(8,128)(2,1)S(1)}, u32[]{:S(2)}, u32[]{:S(2)}) collective-permute-start(bf16[224,128]{1,0:T(8,128)(2,1)S(1)} %get-tuple-element.51), channel_id=1, source_target_pairs={{0,8},{8,0},{64,72},{72,64},{1,9},{9,1},{65,73},{73,65},{2,10},{10... | collective-permute-start | bytes 172040 | tf_op jit(solution)/shard_map/ppermute | solution.py:385
  74.9 6.8 %collective-permute-start.9 = (bf16[224,128]{1,0:T(8,128)(2,1)S(1)}, bf16[224,128]{1,0:T(8,128)(2,1)S(1)}, u32[]{:S(2)}, u32[]{:S(2)}) collective-permute-start(bf16[224,128]{1,0:T(8,128)(2,1)S(1)} %get-tuple-element.52), channel_id=1, source_target_pairs={{0,64},{8,72},{64,0},{72,8},{1,65},{9,73},{65,1},{73,9},{2,66},{10... | collective-permute-start | bytes 172040 | tf_op jit(solution)/shard_map/ppermute | solution.py:385
  76.3 5.4 %collective-permute-start.10 = (bf16[224,128]{1,0:T(8,128)(2,1)S(1)}, bf16[224,128]{1,0:T(8,128)(2,1)S(1)}, u32[]{:S(2)}, u32[]{:S(2)}) collective-permute-start(bf16[224,128]{1,0:T(8,128)(2,1)S(1)} %get-tuple-element.53), channel_id=1, source_target_pairs={{0,72},{8,64},{64,8},{72,0},{1,73},{9,65},{65,9},{73,1},{2,74},{10... | collective-permute-start | bytes 172040 | tf_op jit(solution)/shard_map/ppermute | solution.py:385
  78.7 26.9 %collective-permute-start.18 = (bf16[1024,512]{1,0:T(8,128)(2,1)S(1)}, bf16[1024,512]{1,0:T(8,128)(2,1)S(1)}, u32[]{:S(2)}, u32[]{:S(2)}) collective-permute-start(bf16[1024,512]{1,0:T(8,128)(2,1)S(1)} %pad_maximum_fusion.1), channel_id=1, source_target_pairs={{0,48},{16,0},{32,16},{48,32},{1,49},{17,1},{33,17},{49,33},{2,50}... | collective-permute-start | bytes 3145736 | tf_op jit(solution)/shard_map/ppermute | solution.py:382
  81.7 25.3 %collective-permute-start.17 = (bf16[1024,512]{1,0:T(8,128)(2,1)S(1)}, bf16[1024,512]{1,0:T(8,128)(2,1)S(1)}, u32[]{:S(2)}, u32[]{:S(2)}) collective-permute-start(bf16[1024,512]{1,0:T(8,128)(2,1)S(1)} %pad_maximum_fusion), channel_id=1, source_target_pairs={{0,16},{16,32},{32,48},{48,0},{1,17},{17,33},{33,49},{49,1},{2,18}... | collective-permute-start | bytes 3145736 | tf_op jit(solution)/shard_map/ppermute | solution.py:381
  82.4 6.5 %collective-permute-start.13 = (bf16[3,48,256]{2,1,0:T(8,128)(2,1)S(1)}, bf16[3,48,256]{2,1,0:T(8,128)(2,1)S(1)}, u32[]{:S(2)}, u32[]{:S(2)}) collective-permute-start(bf16[3,48,256]{2,1,0:T(8,128)(2,1)S(1)} %get-tuple-element.54), channel_id=1, source_target_pairs={{0,1},{1,2},{2,3},{3,0},{4,5},{5,6},{6,7},{7,4},{8,9},{9,10},{10,1... | collective-permute-start | bytes 221192 | tf_op jit(solution)/shard_map/ppermute | solution.py:443
  84.3 5.9 %collective-permute-start.12 = (bf16[3,48,256]{2,1,0:T(8,128)(2,1)S(1)}, bf16[3,48,256]{2,1,0:T(8,128)(2,1)S(1)}, u32[]{:S(2)}, u32[]{:S(2)}) collective-permute-start(bf16[3,48,256]{2,1,0:T(8,128)(2,1)S(1)} %get-tuple-element.54), channel_id=1, source_target_pairs={{0,2},{1,3},{2,0},{3,1},{4,6},{5,7},{6,4},{7,5},{8,10},{9,11},{10,... | collective-permute-start | bytes 221192 | tf_op jit(solution)/shard_map/ppermute | solution.py:443
  86.0 4.4 %collective-permute-start.11 = (bf16[3,48,256]{2,1,0:T(8,128)(2,1)S(1)}, bf16[3,48,256]{2,1,0:T(8,128)(2,1)S(1)}, u32[]{:S(2)}, u32[]{:S(2)}) collective-permute-start(bf16[3,48,256]{2,1,0:T(8,128)(2,1)S(1)} %get-tuple-element.54), channel_id=1, source_target_pairs={{0,3},{1,0},{2,1},{3,2},{4,7},{5,4},{6,5},{7,6},{8,11},{9,8},{10,9... | collective-permute-start | bytes 221192 | tf_op jit(solution)/shard_map/ppermute | solution.py:443
  90.4 8.6 %collective-permute-start.14 = (bf16[4,3,48,256]{3,2,1,0:T(8,128)(2,1)S(1)}, bf16[4,3,48,256]{3,2,1,0:T(8,128)(2,1)S(1)}, u32[]{:S(2)}, u32[]{:S(2)}) collective-permute-start(bf16[4,3,48,256]{3,2,1,0:T(8,128)(2,1)S(1)} %pad_maximum_fusion.2), channel_id=1, source_target_pairs={{0,4},{1,5},{2,6},{3,7},{4,0},{5,1},{6,2},{7,3},{8,12},{9,13},{10,... | collective-permute-start | bytes 884744 | tf_op jit(solution)/shard_map/ppermute | solution.py:444
  111.5 9.1 %copy-start.3 = (bf16[48,3,1024]{2,0,1:T(8,128)(2,1)S(1)}, bf16[48,3,1024]{2,0,1:T(8,128)(2,1)}, u32[]{:S(2)}) copy-start(bf16[48,3,1024]{2,0,1:T(8,128)(2,1)} %param.34) | copy-start | bytes 884740
  111.6 5.4 %collective-permute-start.19 = (bf16[144,512]{1,0:T(8,128)(2,1)S(1)}, bf16[144,512]{1,0:T(8,128)(2,1)S(1)}, u32[]{:S(2)}, u32[]{:S(2)}) collective-permute-start(bf16[144,512]{1,0:T(8,128)(2,1)S(1)} %get-tuple-element.70), channel_id=1, source_target_pairs={{0,8},{8,0},{64,72},{72,64},{1,9},{9,1},{65,73},{73,65},{2,10},{10... | collective-permute-start | bytes 442376 | tf_op jit(solution)/shard_map/ppermute | solution.py:385
  111.7 6.7 %collective-permute-start.20 = (bf16[144,512]{1,0:T(8,128)(2,1)S(1)}, bf16[144,512]{1,0:T(8,128)(2,1)S(1)}, u32[]{:S(2)}, u32[]{:S(2)}) collective-permute-start(bf16[144,512]{1,0:T(8,128)(2,1)S(1)} %get-tuple-element.71), channel_id=1, source_target_pairs={{0,64},{8,72},{64,0},{72,8},{1,65},{9,73},{65,1},{73,9},{2,66},{10... | collective-permute-start | bytes 442376 | tf_op jit(solution)/shard_map/ppermute | solution.py:385
  113.1 7.4 %collective-permute-start.21 = (bf16[144,512]{1,0:T(8,128)(2,1)S(1)}, bf16[144,512]{1,0:T(8,128)(2,1)S(1)}, u32[]{:S(2)}, u32[]{:S(2)}) collective-permute-start(bf16[144,512]{1,0:T(8,128)(2,1)S(1)} %get-tuple-element.72), channel_id=1, source_target_pairs={{0,72},{8,64},{64,8},{72,0},{1,73},{9,65},{65,9},{73,1},{2,74},{10... | collective-permute-start | bytes 442376 | tf_op jit(solution)/shard_map/ppermute | solution.py:385
  (7 other events, 5.9 us)

commit v5 on v4

--- a/solution.py
+++ b/solution.py
@@ -20,7 +20,7 @@
 OWN_HEADS = 16
 SPAN = OWN_HEADS * HEAD_DIM
 JOINED = 18560
-PIECE = 3712
+PIECE = 640
 PIECES = JOINED // PIECE
 SHARD = 80
 INNER = HEADS * HEAD_DIM

time: 137 us -> 137 us (level)
  transfers between devices with their start and end apart: 23 -> 23, of which waited for: 12 -> 12; matrix products, arithmetic and copies ran while one was open for 7% -> 7% of each run, Pallas kernels for 16% -> 17%
where the time goes in v5:
time: 137 us; the launch traced here: 136 us
  waiting for transfers between devices  42.8 us (31%)
  starting transfers between devices  33.8 us (25%)
  Pallas kernels  30.8 us (22%)
  local copies, waits for them, and re-layouts  12.2 us (9%)
  blocking collectives  12.1 us (9%)
  other arithmetic  3.82 us (3%)
    all_to_all x1, waiting for transfers between devices, per_device(): lax.all_to_all(after(sent, *far, near), ('x', 'c', 'tp'), split_axis=0, c...  18.5 us
    pallas_call x6, Pallas kernels, call(): pl.pallas_call(kernel, in_specs=[smem] * scalars + [vmem] * (len(args) -...  13.4 us
    all_to_all x1, blocking collectives, per_device(): lax.all_to_all(squares, 'tp', split_axis=0, concat_axis=0, tiled=True)  12.1 us
    pallas_call x2, Pallas kernels, read_state(): pl.pallas_call(state_kernel, grid=(count,), in_specs=[pl.BlockSpec((8, OW...  9.6 us
    pallas_call x1, Pallas kernels, refit(): pl.pallas_call(refit_kernel, in_specs=[pl.BlockSpec(memory_space=pltpu.SM...  7.79 us
    all_to_all x1, starting transfers between devices, per_device(): lax.all_to_all(after(sent, *far, near), ('x', 'c', 'tp'), split_axis=0, c...  7.52 us
    ppermute x3, starting transfers between devices, per_device(): lax.ppermute(value, 'z', [(i, (i + 3) % 4) for i in range(4)])  6.92 us
    unnamed x37, local copies, waits for them, and re-layouts  6.69 us
  transfers between devices with their start and end apart: 23, of which 12 were waited for; matrix products, arithmetic and copies ran while one was open for 7% of the time, Pallas kernels for 17%

profile of v5, /device:TPU:0, one launch (start us, length us, event | category | flops | bytes accessed | tf_op | source)
XLA Modules:
  0.0 136.4 jit_solution(17438547815225649242)
XLA Ops:
  1.0 1.7 %collective-permute-start.1 = (bf16[48,4096]{1,0:T(8,128)(2,1)S(1)}, bf16[48,4096]{1,0:T(8,128)(2,1)}, u32[]{:S(2)}, u32[]{:S(2)}) collective-permute-start(bf16[48,4096]{1,0:T(8,128)(2,1)S(1)} %slice_bitcast_fusion.1), channel_id=1, source_target_pairs={{0,64},{8,72},{64,0},{72,8},{1,65},{9,73},{65,1},{73,9},{2,66},{10... | collective-permute-start | bytes 1179656 | tf_op jit(solution)/shard_map/ppermute | solution.py:385
  3.3 1.3 pad_add_fusion.ints
  4.7 7.8 %refit.1 = bf16[32,32,640]{2,1,0:T(8,128)(2,1)} custom-call(s32[141]{0:T(256)} %pad_add_fusion.ints, s32[1,128]{1,0:T(1,128)} %bitcast.48, f32[1,1]{1,0:T(1,128)} %bitcast.32.rate, f32[5,80]{1,0:T(8,128)} %conv_m.1, bf16[5,80]{1,0:T(8,128)(2,1)} %conv_g.1, f32[5,80]{1,0:T(8,128)} %conv_f.1, f32[5,80]{1,0:T(8,128)} %conv_s.1, f32[32,18560]{1,0:T(8,128)} %master.1, ...), custom_call_target="tpu_custom_call" | custom-call | tf_op jit(solution)/shard_map/refit/pallas_call | solution.py:106
  12.7 7.5 %all-to-all-start = ((bf16[32,32,640]{2,1,0:T(8,128)(2,1)}), bf16[32,32,640]{2,1,0:T(8,128)(2,1)}, u32[]{:S(2)}, u32[]{:S(2)}) async-start(bf16[32,32,640]{2,1,0:T(8,128)(2,1)} %refit.1), calls=%async_computation | async-start | bytes 2621440 | tf_op jit(solution)/shard_map/all_to_all | solution.py:400
  21.3 18.5 %all-to-all-done = bf16[32,32,640]{2,1,0:T(8,128)(2,1)} async-done(((bf16[32,32,640]{2,1,0:T(8,128)(2,1)}), bf16[32,32,640]{2,1,0:T(8,128)(2,1)}, u32[]{:S(2)}, u32[]{:S(2)}) %all-to-all-start) | async-done | bytes 1310752 | tf_op jit(solution)/shard_map/all_to_all | solution.py:400
  41.4 1.4 %fusion = (bf16[512,512]{1,0:T(8,128)(2,1)S(1)}, bf16[512,512]{1,0:T(8,128)(2,1)S(1)}) fusion(bf16[1024,640]{1,0:T(8,128)(2,1)} %bitcast.9), kind=kLoop, calls=%fused_computation.13 | loop fusion | bytes 2097152 | tf_op jit(solution)/shard_map/slice | solution.py:422
  42.8 2.0 %collective-permute-start.3 = (bf16[1024,128]{1,0:T(8,128)(2,1)S(1)}, bf16[1024,128]{1,0:T(8,128)(2,1)S(1)}, u32[]{:S(2)}, u32[]{:S(2)}) collective-permute-start(bf16[1024,128]{1,0:T(8,128)(2,1)S(1)} %slice.24.refs_6_), channel_id=1, source_target_pairs={{0,16},{16,32},{32,48},{48,0},{1,17},{17,33},{33,49},{49,1},{2,18}... | collective-permute-start | bytes 786440 | tf_op jit(solution)/shard_map/ppermute | solution.py:381
  44.7 3.6 %collective-permute-start.5 = (bf16[1024,128]{1,0:T(8,128)(2,1)S(1)}, bf16[1024,128]{1,0:T(8,128)(2,1)S(1)}, u32[]{:S(2)}, u32[]{:S(2)}) collective-permute-start(bf16[1024,128]{1,0:T(8,128)(2,1)S(1)} %slice.24.refs_6_), channel_id=1, source_target_pairs={{0,32},{16,48},{32,0},{48,16},{1,33},{17,49},{33,1},{49,17},{2,34}... | collective-permute-start | bytes 786440 | tf_op jit(solution)/shard_map/ppermute | solution.py:424
  49.3 3.9 %collective-permute-done.3.refs_7_ = bf16[1024,128]{1,0:T(8,128)(2,1)S(1)} collective-permute-done((bf16[1024,128]{1,0:T(8,128)(2,1)S(1)}, bf16[1024,128]{1,0:T(8,128)(2,1)S(1)}, u32[]{:S(2)}, u32[]{:S(2)}) %collective-permute-start.3) | collective-permute-done | bytes 262176 | tf_op jit(solution)/shard_map/ppermute | solution.py:381
  53.9 5.5 %collective-permute-done.5.refs_9_ = bf16[1024,128]{1,0:T(8,128)(2,1)S(1)} collective-permute-done((bf16[1024,128]{1,0:T(8,128)(2,1)S(1)}, bf16[1024,128]{1,0:T(8,128)(2,1)S(1)}, u32[]{:S(2)}, u32[]{:S(2)}) %collective-permute-start.5) | collective-permute-done | bytes 262176 | tf_op jit(solution)/shard_map/ppermute | solution.py:424
  61.4 2.7 %collective-permute-start.16 = (bf16[512,512]{1,0:T(8,128)(2,1)S(1)}, bf16[512,512]{1,0:T(8,128)(2,1)}, u32[]{:S(2)}, u32[]{:S(2)}) collective-permute-start(bf16[512,512]{1,0:T(8,128)(2,1)S(1)} %get-tuple-element.62.refs_7_), channel_id=1, source_target_pairs={{0,48},{16,0},{32,16},{48,32},{1,49},{17,1},{33,17},{49,33},{2,50}... | collective-permute-start | bytes 1572872 | tf_op jit(solution)/shard_map/ppermute | solution.py:382
  70.7 3.7 %first_product_kernel.1 = (bf16[224,128]{1,0:T(8,128)(2,1)S(1)}, bf16[224,128]{1,0:T(8,128)(2,1)S(1)}, bf16[224,128]{1,0:T(8,128)(2,1)S(1)}, bf16[224,128]{1,0:T(8,128)(2,1)S(1)}) custom-call(s32[4]{0:T(128)S(1)} %pad_add_fusion.1.place, s32[141]{0:T(256)S(1)} %copy-done.11, bf16[144,4096]{1,0:T(8,128)(2,1)S(1)} %bitcast.34, ...), custom_call_target="tpu_custom_call" | custom-call | tf_op jit(solution)/shard_map/first_product_kernel/pallas_call | solution.py:323
  74.9 1.4 %collective-permute-start.9 = (bf16[224,128]{1,0:T(8,128)(2,1)S(1)}, bf16[224,128]{1,0:T(8,128)(2,1)S(1)}, u32[]{:S(2)}, u32[]{:S(2)}) collective-permute-start(bf16[224,128]{1,0:T(8,128)(2,1)S(1)} %get-tuple-element.52), channel_id=1, source_target_pairs={{0,64},{8,72},{64,0},{72,8},{1,65},{9,73},{65,1},{73,9},{2,66},{10... | collective-permute-start | bytes 172040 | tf_op jit(solution)/shard_map/ppermute | solution.py:385
  76.5 1.1 pad_maximum_fusion
  77.6 1.1 pad_maximum_fusion.1
  78.7 3.2 %collective-permute-start.18 = (bf16[1024,512]{1,0:T(8,128)(2,1)S(1)}, bf16[1024,512]{1,0:T(8,128)(2,1)S(1)}, u32[]{:S(2)}, u32[]{:S(2)}) collective-permute-start(bf16[1024,512]{1,0:T(8,128)(2,1)S(1)} %pad_maximum_fusion.1), channel_id=1, source_target_pairs={{0,48},{16,0},{32,16},{48,32},{1,49},{17,1},{33,17},{49,33},{2,50}... | collective-permute-start | bytes 3145736 | tf_op jit(solution)/shard_map/ppermute | solution.py:382
  82.6 1.7 %collective-permute-start.13 = (bf16[3,48,256]{2,1,0:T(8,128)(2,1)S(1)}, bf16[3,48,256]{2,1,0:T(8,128)(2,1)S(1)}, u32[]{:S(2)}, u32[]{:S(2)}) collective-permute-start(bf16[3,48,256]{2,1,0:T(8,128)(2,1)S(1)} %get-tuple-element.54), channel_id=1, source_target_pairs={{0,1},{1,2},{2,3},{3,0},{4,5},{5,6},{6,7},{7,4},{8,9},{9,10},{10,1... | collective-permute-start | bytes 221192 | tf_op jit(solution)/shard_map/ppermute | solution.py:443
  84.3 1.7 %collective-permute-start.12 = (bf16[3,48,256]{2,1,0:T(8,128)(2,1)S(1)}, bf16[3,48,256]{2,1,0:T(8,128)(2,1)S(1)}, u32[]{:S(2)}, u32[]{:S(2)}) collective-permute-start(bf16[3,48,256]{2,1,0:T(8,128)(2,1)S(1)} %get-tuple-element.54), channel_id=1, source_target_pairs={{0,2},{1,3},{2,0},{3,1},{4,6},{5,7},{6,4},{7,5},{8,10},{9,11},{10,... | collective-permute-start | bytes 221192 | tf_op jit(solution)/shard_map/ppermute | solution.py:443
  86.0 1.6 %collective-permute-start.11 = (bf16[3,48,256]{2,1,0:T(8,128)(2,1)S(1)}, bf16[3,48,256]{2,1,0:T(8,128)(2,1)S(1)}, u32[]{:S(2)}, u32[]{:S(2)}) collective-permute-start(bf16[3,48,256]{2,1,0:T(8,128)(2,1)S(1)} %get-tuple-element.54), channel_id=1, source_target_pairs={{0,3},{1,0},{2,1},{3,2},{4,7},{5,4},{6,5},{7,6},{8,11},{9,8},{10,9... | collective-permute-start | bytes 221192 | tf_op jit(solution)/shard_map/ppermute | solution.py:443
  88.7 1.4 %collective-permute-done.12 = bf16[3,48,256]{2,1,0:T(8,128)(2,1)S(1)} collective-permute-done((bf16[3,48,256]{2,1,0:T(8,128)(2,1)S(1)}, bf16[3,48,256]{2,1,0:T(8,128)(2,1)S(1)}, u32[]{:S(2)}, u32[]{:S(2)}) %collective-permute-start.12) | collective-permute-done | bytes 73760 | tf_op jit(solution)/shard_map/ppermute | solution.py:443
  90.4 2.0 %collective-permute-start.14 = (bf16[4,3,48,256]{3,2,1,0:T(8,128)(2,1)S(1)}, bf16[4,3,48,256]{3,2,1,0:T(8,128)(2,1)S(1)}, u32[]{:S(2)}, u32[]{:S(2)}) collective-permute-start(bf16[4,3,48,256]{3,2,1,0:T(8,128)(2,1)S(1)} %pad_maximum_fusion.2), channel_id=1, source_target_pairs={{0,4},{1,5},{2,6},{3,7},{4,0},{5,1},{6,2},{7,3},{8,12},{9,13},{10,... | collective-permute-start | bytes 884744 | tf_op jit(solution)/shard_map/ppermute | solution.py:444
  92.4 6.5 %collective-permute-done.14 = bf16[4,3,48,256]{3,2,1,0:T(8,128)(2,1)S(1)} collective-permute-done((bf16[4,3,48,256]{3,2,1,0:T(8,128)(2,1)S(1)}, bf16[4,3,48,256]{3,2,1,0:T(8,128)(2,1)S(1)}, u32[]{:S(2)}, u32[]{:S(2)}) %collective-permute-start.14) | collective-permute-done | bytes 294944 | tf_op jit(solution)/shard_map/ppermute | solution.py:444
  99.2 6.1 %read_state.2 = (f32[3,32,1024]{2,1,0:T(8,128)S(1)}, f32[6,32,1024]{2,1,0:T(8,128)S(1)}) custom-call(bf16[48,16,64,128]{3,2,1,0:T(8,128)(2,1)} %state.3, f32[8,3,48,256]{3,2,1,0:T(8,128)S(1)} %convert_element_type.3.every, f32[48,24,128]{2,1,0:T(8,128)S(1)} %bitcast.36, f32[8,1024]{1,0:T(8,128)S(1)} %get-tuple-element.58.mask), custom_call_target="tpu_custom_call" | custom-call | tf_op jit(solution)/shard_map/read_state/pallas_call | solution.py:335
  105.4 1.8 %collective-permute-done.17.refs_10_ = bf16[1024,512]{1,0:T(8,128)(2,1)S(1)} collective-permute-done((bf16[1024,512]{1,0:T(8,128)(2,1)S(1)}, bf16[1024,512]{1,0:T(8,128)(2,1)S(1)}, u32[]{:S(2)}, u32[]{:S(2)}) %collective-permute-start.17) | collective-permute-done | bytes 1048608 | tf_op jit(solution)/shard_map/ppermute | solution.py:381
  107.2 4.5 %wide_product_kernel.1 = (bf16[144,512]{1,0:T(8,128)(2,1)S(1)}, bf16[144,512]{1,0:T(8,128)(2,1)S(1)}, bf16[144,512]{1,0:T(8,128)(2,1)S(1)}, bf16[144,512]{1,0:T(8,128)(2,1)S(1)}) custom-call(s32[4]{0:T(128)S(1)} %pad_add_fusion.1.place, bf16[144,4096]{1,0:T(8,128)(2,1)S(1)} %bitcast.35, bf16[144,4096]{1,0:T(8,128)(2,1)S(1)} %collective-permute-done.refs_1_, ...), custom_call_target="tpu_custom_call" | custom-call | tf_op jit(solution)/shard_map/wide_product_kernel/pallas_call | solution.py:323
  111.8 1.5 %collective-permute-start.20 = (bf16[144,512]{1,0:T(8,128)(2,1)S(1)}, bf16[144,512]{1,0:T(8,128)(2,1)S(1)}, u32[]{:S(2)}, u32[]{:S(2)}) collective-permute-start(bf16[144,512]{1,0:T(8,128)(2,1)S(1)} %get-tuple-element.71), channel_id=1, source_target_pairs={{0,64},{8,72},{64,0},{72,8},{1,65},{9,73},{65,1},{73,9},{2,66},{10... | collective-permute-start | bytes 442376 | tf_op jit(solution)/shard_map/ppermute | solution.py:385
  113.7 3.5 %read_state.3 = (f32[3,16,1024]{2,1,0:T(8,128)S(1)}, f32[6,16,1024]{2,1,0:T(8,128)S(1)}) custom-call(bf16[48,16,64,128]{3,2,1,0:T(8,128)(2,1)} %state.3, f32[8,3,48,256]{3,2,1,0:T(8,128)S(1)} %convert_element_type.3.every, f32[48,24,128]{2,1,0:T(8,128)S(1)} %bitcast.37, f32[8,1024]{1,0:T(8,128)S(1)} %get-tuple-element.58.mask), custom_call_target="tpu_custom_call" | custom-call | tf_op jit(solution)/shard_map/read_state/pallas_call | solution.py:335
  117.2 1.4 %collective-permute-done.20.refs_2_ = bf16[144,512]{1,0:T(8,128)(2,1)S(1)} collective-permute-done((bf16[144,512]{1,0:T(8,128)(2,1)S(1)}, bf16[144,512]{1,0:T(8,128)(2,1)S(1)}, u32[]{:S(2)}, u32[]{:S(2)}) %collective-permute-start.20) | collective-permute-done | bytes 147488 | tf_op jit(solution)/shard_map/ppermute | solution.py:385
  118.6 2.2 %collective-permute-done.21.refs_3_ = bf16[144,512]{1,0:T(8,128)(2,1)S(1)} collective-permute-done((bf16[144,512]{1,0:T(8,128)(2,1)S(1)}, bf16[144,512]{1,0:T(8,128)(2,1)S(1)}, u32[]{:S(2)}, u32[]{:S(2)}) %collective-permute-start.21) | collective-permute-done | bytes 147488 | tf_op jit(solution)/shard_map/ppermute | solution.py:385
  120.8 2.2 %scan_kernel.1 = (f32[3,48,1024]{2,1,0:T(8,128)S(1)}, f32[8,24,128]{2,1,0:T(8,128)S(1)}) custom-call(s32[4]{0:T(128)S(1)} %pad_add_fusion.1.place, bf16[144,512]{1,0:T(8,128)(2,1)S(1)} %get-tuple-element.69.refs_0_, bf16[144,512]{1,0:T(8,128)(2,1)S(1)} %collective-permute-done.19.refs_1_, bf16[144,512]{1,0:T(8,128)(2,1)S(1)} %collective-permute-done.20.refs_2_, ...), custom_call_target="tpu_custom_call" | custom-call | tf_op jit(solution)/shard_map/scan_kernel/pallas_call | solution.py:323
  123.0 12.1 %all_to_all.10.squares = f32[8,24,128]{2,1,0:T(8,128)S(1)} all-to-all(f32[8,24,128]{2,1,0:T(8,128)S(1)} %get-tuple-element.84), channel_id=1, replica_groups=mesh['x'=2,'z'=4,'c'=2,'tp'=8] {'tp'}, dimensions={0} | all-to-all | bytes 196608 | tf_op jit(solution)/shard_map/all_to_all | solution.py:464
  135.0 1.4 %norm_kernel.1 = bf16[3,48,1024]{2,1,0:T(8,128)(2,1)} custom-call(f32[3,48,1024]{2,1,0:T(8,128)S(1)} %get-tuple-element.83.gated, f32[8,24,128]{2,1,0:T(8,128)S(1)} %all_to_all.10.squares, f32[8,1024]{1,0:T(8,128)S(1)} %get-tuple-element.82.refs_13_.member), custom_call_target="tpu_custom_call" | custom-call | tf_op jit(solution)/shard_map/norm_kernel/pallas_call | solution.py:323
  (75 shorter events, 17.7 us)
Async XLA Ops:
  0.0 12.7 %collective-permute-start = (bf16[144,4096]{1,0:T(8,128)(2,1)}, bf16[144,4096]{1,0:T(8,128)(2,1)S(1)}, u32[]{:S(2)}, u32[]{:S(2)}) collective-permute-start(bf16[144,4096]{1,0:T(8,128)(2,1)} %bitcast.33), channel_id=1, source_target_pairs={{0,8},{8,0},{64,72},{72,64},{1,9},{9,1},{65,73},{73,65},{2,10},{10... | collective-permute-start | bytes 3538952 | tf_op jit(solution)/shard_map/ppermute | solution.py:385
  1.0 11.7 %collective-permute-start.1 = (bf16[48,4096]{1,0:T(8,128)(2,1)S(1)}, bf16[48,4096]{1,0:T(8,128)(2,1)}, u32[]{:S(2)}, u32[]{:S(2)}) collective-permute-start(bf16[48,4096]{1,0:T(8,128)(2,1)S(1)} %slice_bitcast_fusion.1), channel_id=1, source_target_pairs={{0,64},{8,72},{64,0},{72,8},{1,65},{9,73},{65,1},{73,9},{2,66},{10... | collective-permute-start | bytes 1179656 | tf_op jit(solution)/shard_map/ppermute | solution.py:385
  12.5 7.8 %copy-start = (bf16[3,48,4096]{2,1,0:T(8,128)(2,1)S(1)}, bf16[3,48,4096]{2,1,0:T(8,128)(2,1)}, u32[]{:S(2)}) copy-start(bf16[3,48,4096]{2,1,0:T(8,128)(2,1)} %param.32) | copy-start | bytes 3538948
  12.7 27.1 %all-to-all-start = ((bf16[32,32,640]{2,1,0:T(8,128)(2,1)}), bf16[32,32,640]{2,1,0:T(8,128)(2,1)}, u32[]{:S(2)}, u32[]{:S(2)}) async-start(bf16[32,32,640]{2,1,0:T(8,128)(2,1)} %refit.1), calls=%async_computation | async-start | bytes 2621440 | tf_op jit(solution)/shard_map/all_to_all | solution.py:400
  20.3 43.8 %copy-start.15 = (bf16[48,3,2,1,128]{4,2,3,1,0:T(2,128)(2,1)S(1)}, bf16[48,3,2,1,128]{4,2,3,1,0:T(2,128)(2,1)}, u32[]{:S(2)}) copy-start(bf16[48,3,2,1,128]{4,2,3,1,0:T(2,128)(2,1)} %param.35) | copy-start | bytes 221188
  20.3 45.5 %copy-start.10 = (f32[8192]{0:T(1024)S(1)}, f32[8192]{0:T(1024)}, u32[]{:S(2)}) copy-start(f32[8192]{0:T(1024)} %param.39) | copy-start | bytes 98308
  20.3 45.5 %copy-start.11 = (s32[141]{0:T(256)S(1)}, s32[141]{0:T(256)}, u32[]{:S(2)}) copy-start(s32[141]{0:T(256)} %pad_add_fusion.ints) | copy-start | bytes 1696
  20.3 45.5 %copy-start.12 = (f32[128]{0:T(128)S(1)}, f32[128]{0:T(128)}, u32[]{:S(2)}) copy-start(f32[128]{0:T(128)} %param.36) | copy-start | bytes 1540
  20.3 45.5 %copy-start.13 = (f32[128]{0:T(128)S(1)}, f32[128]{0:T(128)}, u32[]{:S(2)}) copy-start(f32[128]{0:T(128)} %param.37) | copy-start | bytes 1540
  20.3 45.5 %copy-start.14 = (f32[128]{0:T(128)S(1)}, f32[128]{0:T(128)}, u32[]{:S(2)}) copy-start(f32[128]{0:T(128)} %param.38) | copy-start | bytes 1540
  39.8 21.0 %collective-permute-start.2 = (bf16[96,4096]{1,0:T(8,128)(2,1)}, bf16[96,4096]{1,0:T(8,128)(2,1)}, u32[]{:S(2)}, u32[]{:S(2)}) collective-permute-start(bf16[96,4096]{1,0:T(8,128)(2,1)} %bitcast.6), channel_id=1, source_target_pairs={{0,64},{8,72},{64,0},{72,8},{1,65},{9,73},{65,1},{73,9},{2,66},{10... | collective-permute-start | bytes 2359304 | tf_op jit(solution)/shard_map/ppermute | solution.py:385
  41.4 19.4 %copy-start.1 = (bf16[1024,128]{1,0:T(8,128)(2,1)}, bf16[1024,128]{1,0:T(8,128)(2,1)S(1)}, u32[]{:S(2)}) copy-start(bf16[1024,128]{1,0:T(8,128)(2,1)S(1)} %slice.24.refs_6_) | copy-start | bytes 786436
  42.8 10.4 %collective-permute-start.3 = (bf16[1024,128]{1,0:T(8,128)(2,1)S(1)}, bf16[1024,128]{1,0:T(8,128)(2,1)S(1)}, u32[]{:S(2)}, u32[]{:S(2)}) collective-permute-start(bf16[1024,128]{1,0:T(8,128)(2,1)S(1)} %slice.24.refs_6_), channel_id=1, source_target_pairs={{0,16},{16,32},{32,48},{48,0},{1,17},{17,33},{33,49},{49,1},{2,18}... | collective-permute-start | bytes 786440 | tf_op jit(solution)/shard_map/ppermute | solution.py:381
  44.7 14.6 %collective-permute-start.5 = (bf16[1024,128]{1,0:T(8,128)(2,1)S(1)}, bf16[1024,128]{1,0:T(8,128)(2,1)S(1)}, u32[]{:S(2)}, u32[]{:S(2)}) collective-permute-start(bf16[1024,128]{1,0:T(8,128)(2,1)S(1)} %slice.24.refs_6_), channel_id=1, source_target_pairs={{0,32},{16,48},{32,0},{48,16},{1,33},{17,49},{33,1},{49,17},{2,34}... | collective-permute-start | bytes 786440 | tf_op jit(solution)/shard_map/ppermute | solution.py:424
  48.3 11.7 %collective-permute-start.4 = (bf16[1024,128]{1,0:T(8,128)(2,1)S(1)}, bf16[1024,128]{1,0:T(8,128)(2,1)S(1)}, u32[]{:S(2)}, u32[]{:S(2)}) collective-permute-start(bf16[1024,128]{1,0:T(8,128)(2,1)S(1)} %slice.24.refs_6_), channel_id=1, source_target_pairs={{0,48},{16,0},{32,16},{48,32},{1,49},{17,1},{33,17},{49,33},{2,50}... | collective-permute-start | bytes 786440 | tf_op jit(solution)/shard_map/ppermute | solution.py:382
  60.8 6.1 %collective-permute-start.7 = (bf16[96,4096]{1,0:T(8,128)(2,1)}, bf16[96,4096]{1,0:T(8,128)(2,1)}, u32[]{:S(2)}, u32[]{:S(2)}) collective-permute-start(bf16[96,4096]{1,0:T(8,128)(2,1)} %collective-permute-done.2.refs_3_), channel_id=1, source_target_pairs={{0,8},{8,0},{64,72},{72,64},{1,9},{9,1},{65,73},{73,65},{2,10},{10... | collective-permute-start | bytes 2359304 | tf_op jit(solution)/shard_map/ppermute | solution.py:385
  60.8 15.7 %collective-permute-start.15 = (bf16[512,512]{1,0:T(8,128)(2,1)S(1)}, bf16[512,512]{1,0:T(8,128)(2,1)}, u32[]{:S(2)}, u32[]{:S(2)}) collective-permute-start(bf16[512,512]{1,0:T(8,128)(2,1)S(1)} %get-tuple-element.60.refs_6_), channel_id=1, source_target_pairs={{0,16},{16,32},{32,48},{48,0},{1,17},{17,33},{33,49},{49,1},{2,18}... | collective-permute-start | bytes 1572872 | tf_op jit(solution)/shard_map/ppermute | solution.py:381
  61.4 15.1 %collective-permute-start.16 = (bf16[512,512]{1,0:T(8,128)(2,1)S(1)}, bf16[512,512]{1,0:T(8,128)(2,1)}, u32[]{:S(2)}, u32[]{:S(2)}) collective-permute-start(bf16[512,512]{1,0:T(8,128)(2,1)S(1)} %get-tuple-element.62.refs_7_), channel_id=1, source_target_pairs={{0,48},{16,0},{32,16},{48,32},{1,49},{17,1},{33,17},{49,33},{2,50}... | collective-permute-start | bytes 1572872 | tf_op jit(solution)/shard_map/ppermute | solution.py:382
  64.1 2.8 %collective-permute-start.6 = (bf16[48,4096]{1,0:T(8,128)(2,1)}, bf16[48,4096]{1,0:T(8,128)(2,1)}, u32[]{:S(2)}, u32[]{:S(2)}) collective-permute-start(bf16[48,4096]{1,0:T(8,128)(2,1)} %collective-permute-done.1.refs_2_), channel_id=1, source_target_pairs={{0,8},{8,0},{64,72},{72,64},{1,9},{9,1},{65,73},{73,65},{2,10},{10... | collective-permute-start | bytes 1179656 | tf_op jit(solution)/shard_map/ppermute | solution.py:385
  74.3 7.6 %collective-permute-start.8 = (bf16[224,128]{1,0:T(8,128)(2,1)S(1)}, bf16[224,128]{1,0:T(8,128)(2,1)S(1)}, u32[]{:S(2)}, u32[]{:S(2)}) collective-permute-start(bf16[224,128]{1,0:T(8,128)(2,1)S(1)} %get-tuple-element.51), channel_id=1, source_target_pairs={{0,8},{8,0},{64,72},{72,64},{1,9},{9,1},{65,73},{73,65},{2,10},{10... | collective-permute-start | bytes 172040 | tf_op jit(solution)/shard_map/ppermute | solution.py:385
  74.9 7.0 %collective-permute-start.9 = (bf16[224,128]{1,0:T(8,128)(2,1)S(1)}, bf16[224,128]{1,0:T(8,128)(2,1)S(1)}, u32[]{:S(2)}, u32[]{:S(2)}) collective-permute-start(bf16[224,128]{1,0:T(8,128)(2,1)S(1)} %get-tuple-element.52), channel_id=1, source_target_pairs={{0,64},{8,72},{64,0},{72,8},{1,65},{9,73},{65,1},{73,9},{2,66},{10... | collective-permute-start | bytes 172040 | tf_op jit(solution)/shard_map/ppermute | solution.py:385
  76.3 5.6 %collective-permute-start.10 = (bf16[224,128]{1,0:T(8,128)(2,1)S(1)}, bf16[224,128]{1,0:T(8,128)(2,1)S(1)}, u32[]{:S(2)}, u32[]{:S(2)}) collective-permute-start(bf16[224,128]{1,0:T(8,128)(2,1)S(1)} %get-tuple-element.53), channel_id=1, source_target_pairs={{0,72},{8,64},{64,8},{72,0},{1,73},{9,65},{65,9},{73,1},{2,74},{10... | collective-permute-start | bytes 172040 | tf_op jit(solution)/shard_map/ppermute | solution.py:385
  78.7 26.7 %collective-permute-start.18 = (bf16[1024,512]{1,0:T(8,128)(2,1)S(1)}, bf16[1024,512]{1,0:T(8,128)(2,1)S(1)}, u32[]{:S(2)}, u32[]{:S(2)}) collective-permute-start(bf16[1024,512]{1,0:T(8,128)(2,1)S(1)} %pad_maximum_fusion.1), channel_id=1, source_target_pairs={{0,48},{16,0},{32,16},{48,32},{1,49},{17,1},{33,17},{49,33},{2,50}... | collective-permute-start | bytes 3145736 | tf_op jit(solution)/shard_map/ppermute | solution.py:382
  81.9 25.3 %collective-permute-start.17 = (bf16[1024,512]{1,0:T(8,128)(2,1)S(1)}, bf16[1024,512]{1,0:T(8,128)(2,1)S(1)}, u32[]{:S(2)}, u32[]{:S(2)}) collective-permute-start(bf16[1024,512]{1,0:T(8,128)(2,1)S(1)} %pad_maximum_fusion), channel_id=1, source_target_pairs={{0,16},{16,32},{32,48},{48,0},{1,17},{17,33},{33,49},{49,1},{2,18}... | collective-permute-start | bytes 3145736 | tf_op jit(solution)/shard_map/ppermute | solution.py:381
  82.6 6.1 %collective-permute-start.13 = (bf16[3,48,256]{2,1,0:T(8,128)(2,1)S(1)}, bf16[3,48,256]{2,1,0:T(8,128)(2,1)S(1)}, u32[]{:S(2)}, u32[]{:S(2)}) collective-permute-start(bf16[3,48,256]{2,1,0:T(8,128)(2,1)S(1)} %get-tuple-element.54), channel_id=1, source_target_pairs={{0,1},{1,2},{2,3},{3,0},{4,5},{5,6},{6,7},{7,4},{8,9},{9,10},{10,1... | collective-permute-start | bytes 221192 | tf_op jit(solution)/shard_map/ppermute | solution.py:443
  84.3 5.9 %collective-permute-start.12 = (bf16[3,48,256]{2,1,0:T(8,128)(2,1)S(1)}, bf16[3,48,256]{2,1,0:T(8,128)(2,1)S(1)}, u32[]{:S(2)}, u32[]{:S(2)}) collective-permute-start(bf16[3,48,256]{2,1,0:T(8,128)(2,1)S(1)} %get-tuple-element.54), channel_id=1, source_target_pairs={{0,2},{1,3},{2,0},{3,1},{4,6},{5,7},{6,4},{7,5},{8,10},{9,11},{10,... | collective-permute-start | bytes 221192 | tf_op jit(solution)/shard_map/ppermute | solution.py:443
  86.0 4.4 %collective-permute-start.11 = (bf16[3,48,256]{2,1,0:T(8,128)(2,1)S(1)}, bf16[3,48,256]{2,1,0:T(8,128)(2,1)S(1)}, u32[]{:S(2)}, u32[]{:S(2)}) collective-permute-start(bf16[3,48,256]{2,1,0:T(8,128)(2,1)S(1)} %get-tuple-element.54), channel_id=1, source_target_pairs={{0,3},{1,0},{2,1},{3,2},{4,7},{5,4},{6,5},{7,6},{8,11},{9,8},{10,9... | collective-permute-start | bytes 221192 | tf_op jit(solution)/shard_map/ppermute | solution.py:443
  90.4 8.4 %collective-permute-start.14 = (bf16[4,3,48,256]{3,2,1,0:T(8,128)(2,1)S(1)}, bf16[4,3,48,256]{3,2,1,0:T(8,128)(2,1)S(1)}, u32[]{:S(2)}, u32[]{:S(2)}) collective-permute-start(bf16[4,3,48,256]{3,2,1,0:T(8,128)(2,1)S(1)} %pad_maximum_fusion.2), channel_id=1, source_target_pairs={{0,4},{1,5},{2,6},{3,7},{4,0},{5,1},{6,2},{7,3},{8,12},{9,13},{10,... | collective-permute-start | bytes 884744 | tf_op jit(solution)/shard_map/ppermute | solution.py:444
  111.7 9.1 %copy-start.3 = (bf16[48,3,1024]{2,0,1:T(8,128)(2,1)S(1)}, bf16[48,3,1024]{2,0,1:T(8,128)(2,1)}, u32[]{:S(2)}) copy-start(bf16[48,3,1024]{2,0,1:T(8,128)(2,1)} %param.34) | copy-start | bytes 884740
  111.7 5.4 %collective-permute-start.19 = (bf16[144,512]{1,0:T(8,128)(2,1)S(1)}, bf16[144,512]{1,0:T(8,128)(2,1)S(1)}, u32[]{:S(2)}, u32[]{:S(2)}) collective-permute-start(bf16[144,512]{1,0:T(8,128)(2,1)S(1)} %get-tuple-element.70), channel_id=1, source_target_pairs={{0,8},{8,0},{64,72},{72,64},{1,9},{9,1},{65,73},{73,65},{2,10},{10... | collective-permute-start | bytes 442376 | tf_op jit(solution)/shard_map/ppermute | solution.py:385
  111.8 6.7 %collective-permute-start.20 = (bf16[144,512]{1,0:T(8,128)(2,1)S(1)}, bf16[144,512]{1,0:T(8,128)(2,1)S(1)}, u32[]{:S(2)}, u32[]{:S(2)}) collective-permute-start(bf16[144,512]{1,0:T(8,128)(2,1)S(1)} %get-tuple-element.71), channel_id=1, source_target_pairs={{0,64},{8,72},{64,0},{72,8},{1,65},{9,73},{65,1},{73,9},{2,66},{10... | collective-permute-start | bytes 442376 | tf_op jit(solution)/shard_map/ppermute | solution.py:385
  113.3 7.5 %collective-permute-start.21 = (bf16[144,512]{1,0:T(8,128)(2,1)S(1)}, bf16[144,512]{1,0:T(8,128)(2,1)S(1)}, u32[]{:S(2)}, u32[]{:S(2)}) collective-permute-start(bf16[144,512]{1,0:T(8,128)(2,1)S(1)} %get-tuple-element.72), channel_id=1, source_target_pairs={{0,72},{8,64},{64,8},{72,0},{1,73},{9,65},{65,9},{73,1},{2,74},{10... | collective-permute-start | bytes 442376 | tf_op jit(solution)/shard_map/ppermute | solution.py:385
  (7 other events, 5.9 us)
